TPU v7x, 512 devices: a whole 4x4x16 slice. The times are simulated.
512 devices in a mesh: row: 32 (over y, x, core), col: 16 (over z).
Axes of the slice: x: 4, y: 4, z: 16, core: 2. Of those that a mesh axis runs over, the one named last changes fastest.
Arguments:
- tokens: bfloat16 [4096, 6144], P('row', 'col'), may hold values from -6 to 6
- weight_blocks: bfloat16 [16, 128, 4096], P('col', 'row'), may hold values from -0.375 to 0.375
- block_rows: int32 [16, 128], P('col', 'row'), may hold values from 0 to 95, as said below
- block_columns: int32 [16, 128], P('col', 'row'), may hold values from 0 to 47
- panel_counts: int32 [16], P('col'), may hold values from 16 to 128, as said below
- hidden_grad: bfloat16 [4096, 49152], P('row', 'col'), may hold values from -1.1953125 to 1.1953125
Outputs:
- hidden: bfloat16 [4096, 49152], P('row', 'col')
- input_grad: bfloat16 [4096, 6144], P('row', 'col')
- weight_grad: bfloat16 [16, 128, 4096], P('col', 'row')
Inputs may be any that keep to these rules, and one draw needn't show every extreme that they name: `block_rows`: in each panel the live slots name distinct pairs of block row and block column; ids in the other slots lie in the same ranges and mean nothing. `panel_counts`: some panel has all 128 slots live.
All inputs are finite; a program needn't handle non-finite values.
Results may differ from a plain program's by a relative error of at most 0.02.
Values may be sent and summed in bfloat16 or wider, within the bound.
No kernel may reach another device: no remote copies, remote signals or barrier semaphores. Data moves between devices by JAX's collectives and lax.ppermute only.
A program may use at most 64 MiB of HBM per device.

v0:
```python
import math

import jax
import jax.numpy as jnp
from jax import lax
from jax.sharding import PartitionSpec as P

root_two_pi = 0.7978845608028654
cubic_term = 0.044715


def gelu_value(pre_act):
    inner = root_two_pi * (pre_act + cubic_term * pre_act * pre_act * pre_act)
    return 0.5 * pre_act * (1.0 + jnp.tanh(inner))


def gelu_slope(pre_act):
    inner = root_two_pi * (pre_act + cubic_term * pre_act * pre_act * pre_act)
    tangent = jnp.tanh(inner)
    return 0.5 * (1.0 + tangent) + 0.5 * pre_act * (1.0 - tangent * tangent) * root_two_pi * (
        1.0 + 3.0 * cubic_term * pre_act * pre_act
    )


def grouped_inputs(blocks, rows_here, cols_here, live_here):
    length = rows_here.shape[0]
    stride = max([width for width in range(1, 65) if length % width == 0])
    group_count = length // stride
    block_side = math.isqrt(blocks.shape[-1])
    shaped = blocks.reshape(group_count, stride, block_side, block_side)
    return (
        shaped,
        rows_here.reshape(group_count, stride),
        cols_here.reshape(group_count, stride),
        live_here.reshape(group_count, stride),
    )


def forward_blocks(running_start, token_blocks, blocks, rows_here, cols_here, live_here):
    tok_rows = token_blocks.shape[0]
    block_side = token_blocks.shape[2]

    def forward_advance(running, inputs):
        part_blocks, part_rows, part_cols, part_live = inputs
        masked = jnp.where(part_live[:, None, None], part_blocks, jnp.zeros_like(part_blocks))
        picked = jnp.take(token_blocks, part_rows, axis=1)
        products = jnp.einsum("tsa,sab->stb", picked, masked, preferred_element_type=jnp.float32)
        return (
            running.at[part_cols].add(products.reshape(part_rows.shape[0], tok_rows * block_side)),
            None,
        )

    result, unused = lax.scan(
        forward_advance, running_start, grouped_inputs(blocks, rows_here, cols_here, live_here)
    )
    return result


def backward_blocks(running_start, grad_blocks, blocks, rows_here, cols_here, live_here):
    tok_rows = grad_blocks.shape[0]
    block_side = grad_blocks.shape[2]

    def backward_advance(running, inputs):
        part_blocks, part_rows, part_cols, part_live = inputs
        masked = jnp.where(part_live[:, None, None], part_blocks, jnp.zeros_like(part_blocks))
        picked = jnp.take(grad_blocks, part_cols, axis=1)
        products = jnp.einsum("tsb,sab->sta", picked, masked, preferred_element_type=jnp.float32)
        return (
            running.at[part_rows].add(products.reshape(part_rows.shape[0], tok_rows * block_side)),
            None,
        )

    result, unused = lax.scan(
        backward_advance, running_start, grouped_inputs(blocks, rows_here, cols_here, live_here)
    )
    return result


def on_device(tokens, weight_blocks, block_rows, block_columns, panel_counts, hidden_grad):
    whole = lax.all_gather(tokens, "col", axis=1, tiled=True)
    tok_rows = whole.shape[0]
    block_side = math.isqrt(weight_blocks.shape[2])
    row_blocks = whole.shape[1] // block_side
    col_blocks = hidden_grad.shape[1] // block_side
    per_device = weight_blocks.shape[1]
    capacity = per_device * lax.axis_size("row")
    count_live = panel_counts[0]
    token_blocks = whole.reshape(tok_rows, row_blocks, block_side)
    empty_pre = jnp.zeros((col_blocks, tok_rows * block_side), jnp.float32)
    empty_ids = jnp.zeros((capacity,), jnp.int32)
    shard_piece = (
        lax.all_gather(weight_blocks, "row", axis=1, tiled=True),
        lax.all_gather(block_rows, "row", axis=1, tiled=True),
        lax.all_gather(block_columns, "row", axis=1, tiled=True),
    )
    begin_at = jnp.int32(0)
    pre_sum = empty_pre
    fold_rows_all = empty_ids
    fold_cols_all = empty_ids
    rows_here = shard_piece[1][0]
    cols_here = shard_piece[2][0]
    live_here = jnp.arange(rows_here.shape[0], dtype=jnp.int32) < count_live
    pre_sum = forward_blocks(
        pre_sum, token_blocks, shard_piece[0][0], rows_here, cols_here, live_here
    )
    fold_rows_all = lax.dynamic_update_slice_in_dim(fold_rows_all, rows_here, begin_at, 0)
    fold_cols_all = lax.dynamic_update_slice_in_dim(fold_cols_all, cols_here, begin_at, 0)
    pre_sum, rows_all, cols_all = (pre_sum, fold_rows_all, fold_cols_all)
    pre_act = pre_sum.reshape(col_blocks, tok_rows, block_side).transpose(1, 0, 2)
    hidden = gelu_value(pre_act).astype(jnp.bfloat16).reshape(tok_rows, col_blocks * block_side)
    upstream = hidden_grad.reshape(tok_rows, col_blocks, block_side)
    grad_blocks = (upstream.astype(jnp.float32) * gelu_slope(pre_act)).astype(jnp.bfloat16)
    empty_back = jnp.zeros((row_blocks, tok_rows * block_side), jnp.float32)
    shard_piece = (
        lax.all_gather(weight_blocks, "row", axis=1, tiled=True),
        lax.all_gather(block_rows, "row", axis=1, tiled=True),
        lax.all_gather(block_columns, "row", axis=1, tiled=True),
    )
    rows_here = shard_piece[1][0]
    cols_here = shard_piece[2][0]
    live_here = jnp.arange(rows_here.shape[0], dtype=jnp.int32) < count_live
    input_part = backward_blocks(
        empty_back, grad_blocks, shard_piece[0][0], rows_here, cols_here, live_here
    )
    own_sums = lax.psum_scatter(
        input_part.astype(jnp.bfloat16), "col", scatter_dimension=0, tiled=True
    ).astype(jnp.float32)
    input_grad = (
        own_sums.reshape(-1, tok_rows, block_side)
        .transpose(1, 0, 2)
        .reshape(tok_rows, -1)
        .astype(jnp.bfloat16)
    )
    live_part = jnp.arange(per_device * lax.axis_size("row"), dtype=jnp.int32) < count_live
    picked_in = jnp.take(token_blocks, rows_all, axis=1)
    picked_grad = jnp.take(grad_blocks, cols_all, axis=1)
    products = jnp.einsum(
        "tsa,tsb->sab", picked_in, picked_grad, preferred_element_type=jnp.float32
    )
    products = jnp.where(live_part[:, None, None], products, jnp.zeros_like(products))
    weight_sum = lax.psum_scatter(
        products.reshape(per_device * lax.axis_size("row"), block_side * block_side).astype(
            jnp.bfloat16
        ),
        "row",
        scatter_dimension=0,
        tiled=True,
    )
    weight_grad = weight_sum.reshape(1, per_device, block_side * block_side)
    return (hidden, input_grad, weight_grad)


def solution(mesh):
    placed = (
        P("row", "col"),
        P("col", "row", None),
        P("col", "row"),
        P("col", "row"),
        P("col"),
        P("row", "col"),
    )
    return jax.shard_map(
        on_device,
        mesh=mesh,
        in_specs=placed,
        out_specs=(P("row", "col"), P("row", "col"), P("col", "row", None)),
        check_vma=False,
    )
```

profile of v0, /device:TPU:6, one launch (start us, length us, event | category | flops | bytes accessed | tf_op | source)
XLA Modules:
  0.0 446.8 jit_solution(2087213582369064578)
XLA Ops:
  15.8 14.9 %all-reduce.5 = (s32[128]{0:T(128)S(1)}, s32[128]{0:T(128)S(1)}) all-reduce(s32[128]{0:T(128)S(1)} %bitcast_dynamic-update-slice_fusion.1, s32[128]{0:T(128)S(1)} %bitcast_dynamic-update-slice_fusion), channel_id=1, replica_groups=mesh['row'=32,'col'=16] {'row'}, use_global_device_ids=true, to_apply=%add | all-reduce | flops 256 | bytes 2048 | tf_op jit(solution)/shard_map/squeeze | solution.py:101
  36.0 38.9 %all-gather.5.cloned.1.call-done = bf16[1,128,4096]{2,0,1:T(2,128)(2,1)} async-done(((bf16[1,4,4096]{2,0,1:T(2,128)(2,1)}), bf16[1,128,4096]{2,0,1:T(2,128)(2,1)}) %all-gather.5.cloned.1.call-update) | async-done | bytes 1048592 | tf_op jit(solution)/shard_map/all_gather | solution.py:92
  74.8 7.7 %reduce = bf16[128,4096]{1,0:T(8,128)(2,1)S(1)} reduce(bf16[1,128,4096]{2,0,1:T(2,128)(2,1)} %all-gather.5.cloned.1.call-done, bf16[]{:T(256)} %constant.132), dimensions={0}, to_apply=%all_gather.18.reduce_sub_computation | reduce | bytes 2097154 | tf_op jit(solution)/shard_map/all_gather | solution.py:92
  82.6 3.5 reshape_squeeze.14
  86.0 63.5 %all-gather.3.cloned.1.call-done = bf16[128,6144]{0,1:T(8,128)(2,1)} async-done(((bf16[128,384]{0,1:T(8,128)(2,1)}), bf16[128,6144]{0,1:T(8,128)(2,1)}) %all-gather.3.cloned.1.call-update) | async-done | bytes 1572880 | tf_op jit(solution)/shard_map/all_gather | solution.py:80
  149.7 40.8 %while.20 = (s32[]{:T(128)}, f32[48,8192]{1,0:T(8,128)S(1)}, s32[2,64]{1,0:T(2,128)S(1)}, s32[2,64]{1,0:T(2,128)S(1)}, bf16[128,96,64]{0,2,1:T(8,128)(2,1)}, /*i...) while((s32[]{:T(128)}, f32[48,8192]{1,0:T(8,128)S(1)}, s32[2,64]{1,0:T(2,128)S(1)}, ...), condition=%wide.region_2.3_spmd, body=%wide.region_0.2_spmd.sunk | while | flops 68421376 | bytes 18356652 | solution.py:53
  156.5 4.1 fusion.54
  160.6 4.8 %reshape.324 = f32[64,8192]{1,0:T(8,128)} reshape(f32[64,128,64]{2,1,0:T(8,128)} %fusion.54) | data formatting | bytes 4194304 | tf_op jit(solution)/shard_map/while/body/eval_jaxpr/reshape | solution.py:49
  165.4 4.6 %scatter_fusion = f32[48,8192]{1,0:T(8,128)S(1)} fusion(f32[48,8192]{1,0:T(8,128)S(1)} %get-tuple-element.269, s32[64]{0:T(128)S(1)} %get-tuple-element.249, f32[64,8192]{1,0:T(8,128)} %reshape.324), kind=kCustom, calls=%fused_computation.4.clone.1 | custom fusion | flops 524288 | bytes 6291712 | tf_op jit(solution)/shard_map/while/body/eval_jaxpr/scatter-add | solution.py:49
  176.9 4.1 fusion.54
  181.0 4.8 %reshape.324 = f32[64,8192]{1,0:T(8,128)} reshape(f32[64,128,64]{2,1,0:T(8,128)} %fusion.54) | data formatting | bytes 4194304 | tf_op jit(solution)/shard_map/while/body/eval_jaxpr/reshape | solution.py:49
  185.8 4.6 %scatter_fusion = f32[48,8192]{1,0:T(8,128)S(1)} fusion(f32[48,8192]{1,0:T(8,128)S(1)} %get-tuple-element.269, s32[64]{0:T(128)S(1)} %get-tuple-element.249, f32[64,8192]{1,0:T(8,128)} %reshape.324), kind=kCustom, calls=%fused_computation.4.clone.1 | custom fusion | flops 524288 | bytes 6291712 | tf_op jit(solution)/shard_map/while/body/eval_jaxpr/scatter-add | solution.py:49
  197.8 34.9 %while.21 = (s32[]{:T(128)}, f32[96,8192]{1,0:T(8,128)S(1)}, s32[2,64]{1,0:T(2,128)S(1)}, s32[2,64]{1,0:T(2,128)S(1)}, bf16[128,48,64]{0,2,1:T(8,128)(2,1)}, /*i...) while((s32[]{:T(128)}, f32[96,8192]{1,0:T(8,128)S(1)}, s32[2,64]{1,0:T(2,128)S(1)}, ...), condition=%wide.region_5.6_spmd, body=%wide.region_3.5_spmd.sunk | while | flops 68421376 | bytes 16783788 | solution.py:73
  200.9 4.4 fusion.57
  205.4 4.8 %reshape.329 = f32[64,8192]{1,0:T(8,128)} reshape(f32[64,128,64]{2,1,0:T(8,128)} %fusion.57) | data formatting | bytes 4194304 | tf_op jit(solution)/shard_map/while/body/eval_jaxpr/reshape | solution.py:69
  210.2 5.2 %scatter_fusion.1 = f32[96,8192]{1,0:T(8,128)S(1)} fusion(f32[96,8192]{1,0:T(8,128)S(1)} %get-tuple-element.293, s32[64]{0:T(128)S(1)} %get-tuple-element.258, f32[64,8192]{1,0:T(8,128)} %reshape.329), kind=kCustom, calls=%fused_computation.5.clone.1 | custom fusion | flops 524288 | bytes 6291712 | tf_op jit(solution)/shard_map/while/body/eval_jaxpr/scatter-add | solution.py:69
  218.2 4.4 fusion.57
  222.7 4.8 %reshape.329 = f32[64,8192]{1,0:T(8,128)} reshape(f32[64,128,64]{2,1,0:T(8,128)} %fusion.57) | data formatting | bytes 4194304 | tf_op jit(solution)/shard_map/while/body/eval_jaxpr/reshape | solution.py:69
  227.5 5.2 %scatter_fusion.1 = f32[96,8192]{1,0:T(8,128)S(1)} fusion(f32[96,8192]{1,0:T(8,128)S(1)} %get-tuple-element.293, s32[64]{0:T(128)S(1)} %get-tuple-element.258, f32[64,8192]{1,0:T(8,128)} %reshape.329), kind=kCustom, calls=%fused_computation.5.clone.1 | custom fusion | flops 524288 | bytes 6291712 | tf_op jit(solution)/shard_map/while/body/eval_jaxpr/scatter-add | solution.py:69
  234.0 41.6 %fusion = bf16[8,8192]{1,0:T(8,128)(2,1)S(1)} fusion(bf16[96,8192]{1,0:T(8,128)(2,1)} %convert_element_type.36), kind=kCustom, calls=%all-reduce-scatter | all-reduce-scatter fusion | flops 1048577 | bytes 1705984
  279.1 5.1 %collective-permute-start.1 = (bf16[8,8192]{1,0:T(8,128)(2,1)S(1)}, bf16[8,8192]{1,0:T(8,128)(2,1)S(1)}, u32[]{:S(2)}, u32[]{:S(2)}) collective-permute-start(bf16[8,8192]{1,0:T(8,128)(2,1)S(1)} %fusion), channel_id=1, source_target_pairs={{0,2},{1,3},{2,4},{3,5},{4,6},{5,7},{6,8},{7,9},{8,10},{9,11},{10,... | collective-permute-start | bytes 393224
  291.6 4.8 %fusion.27 = bf16[128,64,64]{2,1,0:T(8,128)(2,1)} fusion(bf16[128,128,64]{1,2,0:T(8,128)(2,1)} %gather_fusion.3, bf16[128,128,64]{1,2,0:T(8,128)(2,1)} %gather_fusion.2, pred[128]{0:T(512)(128)(4,1)S(1)} %copy-done.4, pred[128]{0:T(512)(128)(4,1)S(1)} %copy-done.5), kind=kOutput, calls=%fused_computation.53 | convolution fusion | flops 136314880 | bytes 5243136 | tf_op jit(solution)/shard_map/tsa,tsb->sab/dot_general | solution.py:137
  299.8 6.4 %collective-permute-start.3 = (bf16[6,8192]{1,0:T(8,128)(2,1)S(1)}, bf16[6,8192]{1,0:T(8,128)(2,1)S(1)}, u32[]{:S(2)}, u32[]{:S(2)}) collective-permute-start(bf16[6,8192]{1,0:T(8,128)(2,1)S(1)} %slice.8), channel_id=1, source_target_pairs={{0,4},{1,5},{2,6},{3,7},{4,8},{5,9},{6,10},{7,11},{8,12},{9,13},{1... | collective-permute-start | bytes 294920
  311.4 126.2 %all-reduce.8.cloned.1.call-done = bf16[128,4096]{0,1:T(8,128)(2,1)} async-done(((bf16[128,4096]{0,1:T(8,128)(2,1)}), bf16[128,4096]{0,1:T(8,128)(2,1)}) %all-reduce.8.cloned.1.call-update) | async-done | bytes 1048592
  (85 shorter events, 61.3 us)
Async XLA Ops:
  7.2 67.7 %all-gather.5.cloned.1.call-start = ((), (), s32[]{:S(2)}) async-start(), calls=%async_computation.1 | async-start | bytes 2162688 | tf_op jit(solution)/shard_map/all_gather | solution.py:92
  8.7 140.9 %all-gather.3.cloned.1.call-start = ((), (), s32[]{:S(2)}) async-start(), calls=%async_computation | async-start | bytes 1671168 | tf_op jit(solution)/shard_map/all_gather | solution.py:80
  10.4 427.3 %all-reduce.8.cloned.1.call-start = ((), (), s32[]{:S(2)}) async-start(), calls=%async_computation.2 | async-start | bytes 2097152
  234.0 52.8 %copy-start = (bf16[128,48,64]{0,2,1:T(8,128)(2,1)S(1)}, bf16[128,48,64]{0,2,1:T(8,128)(2,1)}, u32[]{:S(2)}) copy-start(bf16[128,48,64]{0,2,1:T(8,128)(2,1)} %get-tuple-element.311) | copy-start | bytes 2359300
  275.7 33.0 %collective-permute-start.2 = (bf16[8,8192]{1,0:T(8,128)(2,1)S(1)}, bf16[8,8192]{1,0:T(8,128)(2,1)S(1)}, u32[]{:S(2)}, u32[]{:S(2)}) collective-permute-start(bf16[8,8192]{1,0:T(8,128)(2,1)S(1)} %fusion), channel_id=1, source_target_pairs={{0,3},{1,4},{2,5},{3,6},{4,7},{5,8},{6,9},{7,10},{8,11},{9,12},{10... | collective-permute-start | bytes 393224
  279.1 29.6 %collective-permute-start.1 = (bf16[8,8192]{1,0:T(8,128)(2,1)S(1)}, bf16[8,8192]{1,0:T(8,128)(2,1)S(1)}, u32[]{:S(2)}, u32[]{:S(2)}) collective-permute-start(bf16[8,8192]{1,0:T(8,128)(2,1)S(1)} %fusion), channel_id=1, source_target_pairs={{0,2},{1,3},{2,4},{3,5},{4,6},{5,7},{6,8},{7,9},{8,10},{9,11},{10,... | collective-permute-start | bytes 393224
  284.2 24.5 %collective-permute-start = (bf16[8,8192]{1,0:T(8,128)(2,1)S(1)}, bf16[8,8192]{1,0:T(8,128)(2,1)S(1)}, u32[]{:S(2)}, u32[]{:S(2)}) collective-permute-start(bf16[8,8192]{1,0:T(8,128)(2,1)S(1)} %fusion), channel_id=1, source_target_pairs={{0,1},{1,2},{2,3},{3,4},{4,5},{5,6},{6,7},{7,8},{8,9},{9,10},{10,1... | collective-permute-start | bytes 393224
  286.8 2.4 copy-start.1
  289.2 2.4 copy-start.4
  289.2 2.4 copy-start.5
  296.4 9.8 %copy-start.3 = (pred[128]{0:T(512)(128)(4,1)S(1)}, pred[128]{0:T(512)(128)(4,1)}, u32[]{:S(2)}) copy-start(pred[128]{0:T(512)(128)(4,1)} %iota_compare_fusion) | copy-start | bytes 388
  296.4 11.1 %copy-start.2 = (bf16[128,48,64]{0,2,1:T(8,128)(2,1)S(1)}, bf16[128,48,64]{0,2,1:T(8,128)(2,1)}, u32[]{:S(2)}) copy-start(bf16[128,48,64]{0,2,1:T(8,128)(2,1)} %get-tuple-element.161) | copy-start | bytes 2359300
  299.8 8.9 %collective-permute-start.3 = (bf16[6,8192]{1,0:T(8,128)(2,1)S(1)}, bf16[6,8192]{1,0:T(8,128)(2,1)S(1)}, u32[]{:S(2)}, u32[]{:S(2)}) collective-permute-start(bf16[6,8192]{1,0:T(8,128)(2,1)S(1)} %slice.8), channel_id=1, source_target_pairs={{0,4},{1,5},{2,6},{3,7},{4,8},{5,9},{6,10},{7,11},{8,12},{9,13},{1... | collective-permute-start | bytes 294920
Sparse Core Ops, SparseCore 0:
  11.7 63.0 all-gather.4
  77.5 72.0 all-gather.2
  308.8 128.8 all-reduce.7
where the time goes:
time: 448 us; the launch traced here: 447 us
  waiting for transfers between devices  229 us (51%)
  local copies, waits for them, and re-layouts  70.5 us (16%)
  blocking collectives  56.6 us (13%)
  other arithmetic  34.7 us (8%)
  matrix products  21.9 us (5%)
  starting transfers between devices  17.6 us (4%)
  between operations  16.4 us (4%)
    unnamed x8, waiting for transfers between devices  126 us
    all_gather x1, waiting for transfers between devices, on_device(): whole = lax.all_gather(tokens, 'col', axis=1, tiled=True)  63.5 us
    unnamed x1, blocking collectives  41.6 us
    all_gather x1, waiting for transfers between devices, on_device(): lax.all_gather(weight_blocks, 'row', axis=1, tiled=True)  38.9 us
    unnamed x5, starting transfers between devices  17.5 us
    squeeze x1, blocking collectives, on_device(): cols_here = shard_piece[2][0]  14.9 us
    unnamed x27, local copies, waits for them, and re-layouts  13.3 us
    scatter-add x2, other arithmetic, backward_advance(): running.at[part_rows]  10.4 us
  transfers between devices with their start and end apart: 7, of which 3 were waited for; matrix products, arithmetic and copies ran while one was open for 9% of the time, Pallas kernels for 0%

commit v1 on v0

v1 whole, which is shorter than its diff:
```python
import jax
import jax.numpy as jnp
from jax import lax
from jax.experimental import pallas as pl
from jax.experimental.pallas import tpu as pltpu
from jax.sharding import PartitionSpec as P

root_two_pi = 0.7978845608028654
cubic_term = 0.044715
BF = jnp.bfloat16
F32 = jnp.float32
BLK = 64
NT = (((1,), (1,)), ((), ()))
TN = (((0,), (0,)), ((), ()))
SEEDS = (0, 5, -5)
ABOVE1 = (1, 6, -4)
BELOW1 = (-1, 4, -6)
ABOVE2 = (2, 7, -3)
BELOW2 = (-2, 3, -7)


def dot(a, b, dims=(((1,), (0,)), ((), ()))):
    return lax.dot_general(a, b, dims, preferred_element_type=F32)


def eye():
    i = lax.broadcasted_iota(jnp.int32, (128, 128), 0)
    j = lax.broadcasted_iota(jnp.int32, (128, 128), 1)
    return (i == j).astype(BF)


def forward_kernel(
    ids, weights, s0, a1, b1, a2, b2, e8, upstream, hidden, grad, whole, pre
):
    for piece, offsets in ((s0, SEEDS), (a1, ABOVE1), (b1, BELOW1), (a2, ABOVE2), (b2, BELOW2), (e8, (8,))):
        for k, offset in enumerate(offsets):
            at = offset % 16 * 6
            whole[at : at + 6] = piece[k].reshape(6, BLK, 128)
    pre[...] = jnp.zeros_like(pre)

    def some_slots(g, carry):
        for q in range(4):
            d = g * 4 + q
            for j in range(4):
                half = (j % 2) * BLK
                block = weights[d, (j // 2) * BLK : (j // 2 + 1) * BLK, half : half + BLK]
                row, column = ids[d, j], ids[d, 4 + j]
                pre[column] += dot(block, whole[row], TN)
        return carry

    lax.fori_loop(0, 8, some_slots, 0)

    unit = eye()

    def some_columns(g, carry):
        at = pl.multiple_of(g * 128, 128)
        v = pre[pl.ds(g * 2, 2)].reshape(128, 128)
        tangent = jnp.tanh(root_two_pi * (v + cubic_term * v * v * v))
        value = 0.5 * v * (1.0 + tangent)
        slope = 0.5 * (1.0 + tangent) + 0.5 * v * (1.0 - tangent * tangent) * root_two_pi * (
            1.0 + 3.0 * cubic_term * v * v
        )
        turned = dot(unit, upstream[:, pl.ds(at, 128)], NT)
        grad[pl.ds(g * 2, 2)] = (turned * slope).astype(BF).reshape(2, BLK, 128)
        hidden[:, pl.ds(at, 128)] = dot(unit, value.astype(BF), NT).astype(BF)
        return carry

    lax.fori_loop(0, 24, some_columns, 0)


def input_kernel(ids, weights, grad, v0, a1, b1, a2, b2, e8, total):
    total[...] = jnp.zeros_like(total)

    def some_slots(g, carry):
        for q in range(4):
            d = g * 4 + q
            for j in range(4):
                half = (j % 2) * BLK
                block = weights[d, (j // 2) * BLK : (j // 2 + 1) * BLK, half : half + BLK]
                row, column = ids[d, j], ids[d, 4 + j]
                total[row] += dot(block, grad[column])
        return carry

    lax.fori_loop(0, 8, some_slots, 0)
    for piece, offsets in ((v0, SEEDS), (a1, ABOVE1), (b1, BELOW1), (a2, ABOVE2), (b2, BELOW2), (e8, (8,))):
        for k, offset in enumerate(offsets):
            at = offset % 16 * 6
            piece[k] = total[at : at + 6].reshape(384, 128).astype(BF)


def weight_kernel(ids, whole, grad, out):
    def some_slots(g, carry):
        for q in range(4):
            d = g * 4 + q
            for j in range(4):
                half = (j % 2) * BLK
                row, column = ids[d, j], ids[d, 4 + j]
                block = dot(whole[row], grad[column], NT).astype(BF)
                out[d, (j // 2) * BLK : (j // 2 + 1) * BLK, half : half + BLK] = block
        return carry

    lax.fori_loop(0, 8, some_slots, 0)


SM = pl.BlockSpec(memory_space=pltpu.SMEM)
VM = pl.BlockSpec(memory_space=pltpu.VMEM)
MIB = 1 << 20


def shape(*dims):
    return jax.ShapeDtypeStruct(dims, BF)


def call(kernel, outs, n_in, scratch, flops, limit):
    return pl.pallas_call(
        kernel,
        out_shape=outs,
        in_specs=[SM] + [VM] * (n_in - 1),
        out_specs=jax.tree.map(lambda _: VM, outs),
        scratch_shapes=scratch,
        compiler_params=pltpu.CompilerParams(vmem_limit_bytes=limit * MIB),
        cost_estimate=pl.CostEstimate(flops=flops, bytes_accessed=6 * MIB, transcendentals=0),
    )


def on_device(tokens, weight_blocks, block_rows, block_columns, panel_counts, hidden_grad):
    n_col, n_row = lax.axis_size("col"), lax.axis_size("row")
    me_col, me_row = lax.axis_index("col"), lax.axis_index("row")

    def shift(a, by):
        return lax.ppermute(a, "col", [(i, (i + by) % n_col) for i in range(n_col)])

    mine = tokens.T
    far = jnp.stack([mine, shift(mine, -5), shift(mine, 5)])

    slot = me_row * 4 + jnp.arange(4, dtype=jnp.int32)
    live = slot < panel_counts[0]
    blocks = jnp.where(live[:, None, None], weight_blocks[0].reshape(4, BLK, BLK), 0)
    blocks = blocks.reshape(2, 2, BLK, BLK).transpose(0, 2, 1, 3).reshape(128, 128)
    named = jnp.concatenate([block_rows[0], block_columns[0]]).astype(BF)
    named = jnp.pad(named[None, :], ((0, 15), (0, 120)))
    parcel = jnp.broadcast_to(jnp.concatenate([blocks, named])[None], (n_row, 144, 128))
    parcels = lax.all_to_all(parcel, "row", 0, 0, tiled=True)
    ids = parcels[:, 128, :8].astype(jnp.int32)
    rows = (ids[:, :4] + (96 - 6 * me_col)) % 96
    ids = jnp.concatenate([rows, ids[:, 4:]], axis=1)

    above1, below1 = shift(far, -1), shift(far, 1)
    above2, below2 = shift(above1, -1), shift(below1, 1)
    eight = shift(above1[1:2], -2)

    hidden, grad, whole = call(
        forward_kernel,
        (shape(128, 3072), shape(48, BLK, 128), shape(96, BLK, 128)),
        9,
        [pltpu.VMEM((48, BLK, 128), F32)],
        400_000_000,
        24,
    )(ids, parcels, far, above1, below1, above2, below2, eight, hidden_grad)

    three = shape(3, 384, 128)
    v0, a1, b1, a2, b2, e8 = call(
        input_kernel,
        (three, three, three, three, three, shape(1, 384, 128)),
        3,
        [pltpu.VMEM((96, BLK, 128), F32)],
        300_000_000,
        24,
    )(ids, parcels, grad)

    def plus(a, *more):
        total = a.astype(F32)
        for m in more:
            total = total + m.astype(F32)
        return total.astype(BF)

    from8 = shift(e8, 2)
    up, down = shift(a2, 1), shift(b2, -1)
    a1 = plus(a1, up, jnp.pad(from8, ((1, 1), (0, 0), (0, 0))))
    b1 = plus(b1, down)

    terms = call(weight_kernel, shape(n_row, 128, 128), 3, [], 300_000_000, 16)(ids, whole, grad)
    back = lax.all_to_all(terms, "row", 0, 0, tiled=True)

    v0 = plus(v0, shift(a1, 1), shift(b1, -1))
    own = plus(v0[0], shift(v0[1], 5), shift(v0[2], -5))
    input_grad = own.T

    sums = jnp.sum(back.astype(F32), axis=0).astype(BF)
    sums = sums.reshape(2, BLK, 2, BLK).transpose(0, 2, 1, 3).reshape(4, BLK * BLK)
    weight_grad = jnp.where(live[:, None], sums, 0)[None]
    return hidden, input_grad, weight_grad


def solution(mesh):
    placed = (
        P("row", "col"),
        P("col", "row", None),
        P("col", "row"),
        P("col", "row"),
        P("col"),
        P("row", "col"),
    )
    return jax.shard_map(
        on_device,
        mesh=mesh,
        in_specs=placed,
        out_specs=(P("row", "col"), P("row", "col"), P("col", "row", None)),
        check_vma=False,
    )
```

time: 448 us -> 148 us (0.33)
  waiting for transfers between devices: 229 us -> 44 us
  local copies, waits for them, and re-layouts: 70.5 us -> 4.01 us
  starting transfers between devices: 17.6 us -> 76.5 us
  blocking collectives: 56.6 us -> 0 us
  other arithmetic: 34.7 us -> 2.89 us
  matrix products: 21.9 us -> 0 us
  Pallas kernels: 0 us -> 17.3 us
  between operations: 16.4 us -> 1.58 us
    unnamed x8 -> x0, waiting for transfers between devices: 126 us -> none
    all_gather x2 -> x0, waiting for transfers between devices: 102 us -> none  [the longest x1 63.5 us: on_device(): whole = lax.all_gather(tokens, 'col', axis=1, tiled=True)]
    ppermute x0 -> x14, starting transfers between devices: none -> 59.5 us  [shift(): return lax.ppermute(a, 'col', [(i, (i + by) % n_col) for i in range(n_col)])]
    ppermute x0 -> x14, waiting for transfers between devices: none -> 43.9 us  [shift(): return lax.ppermute(a, 'col', [(i, (i + by) % n_col) for i in range(n_col)])]
    unnamed x1 -> x0, blocking collectives: 41.6 us -> none
    reshape x7 -> x3, local copies, waits for them, and re-layouts: 25.6 us -> 0.3 us  [the longest x2 0.2 us: on_device(): sums.reshape(2, BLK, 2, BLK).transpose(0, 2, 1, 3).reshape(4, BLK * BLK)]
    dot_general x5 -> x0, matrix products: 21.9 us -> none  [the longest x2 8.86 us: backward_advance(): jnp.einsum('tsb,sab->sta', picked, masked, preferred_element_type=jnp.flo...]
    scatter-add x4 -> x0, other arithmetic: 19.6 us -> none  [the longest x2 10.4 us: backward_advance(): running.at[part_rows]]
  transfers between devices with their start and end apart: 7 -> 16, of which waited for: 3 -> 8; matrix products, arithmetic and copies ran while one was open for 9% -> 1% of each run, Pallas kernels for 0% -> 3%
where the time goes in v1:
time: 148 us; the launch traced here: 146 us
  starting transfers between devices  76.5 us (52%)
  waiting for transfers between devices  44 us (30%)
  Pallas kernels  17.3 us (12%)
  local copies, waits for them, and re-layouts  4.01 us (3%)
  other arithmetic  2.89 us (2%)
  between operations  1.58 us (1%)
    ppermute x14, starting transfers between devices, shift(): return lax.ppermute(a, 'col', [(i, (i + by) % n_col) for i in range(n_col)])  59.5 us
    ppermute x14, waiting for transfers between devices, shift(): return lax.ppermute(a, 'col', [(i, (i + by) % n_col) for i in range(n_col)])  43.9 us
    all_to_all x1, starting transfers between devices, on_device(): parcels = lax.all_to_all(parcel, 'row', 0, 0, tiled=True)  9.61 us
    pallas_call x1, Pallas kernels, on_device(): call(forward_kernel, (shape(128, 3072), shape(48, BLK, 128), shape(96, BL...  9.49 us
    all_to_all x1, starting transfers between devices, on_device(): back = lax.all_to_all(terms, 'row', 0, 0, tiled=True)  7.38 us
    pallas_call x1, Pallas kernels, on_device(): call(weight_kernel, shape(n_row, 128, 128), 3, [], 300000000, 16)  4.44 us
    pallas_call x1, Pallas kernels, on_device(): call(input_kernel, (three, three, three, three, three, shape(1, 384, 128)...  3.33 us
  transfers between devices with their start and end apart: 16, of which 8 were waited for; matrix products, arithmetic and copies ran while one was open for 1% of the time, Pallas kernels for 3%

profile of v1, /device:TPU:6, one launch (start us, length us, event | category | flops | bytes accessed | tf_op | source)
XLA Modules:
  0.0 146.1 jit_solution(9438808890973337333)
XLA Ops:
  5.0 9.6 %all-to-all-start = ((bf16[32,144,128]{2,1,0:T(8,128)(2,1)}), bf16[32,144,128]{2,1,0:T(8,128)(2,1)S(1)}, u32[]{:S(2)}, u32[]{:S(2)}) async-start(bf16[32,144,128]{2,1,0:T(8,128)(2,1)} %broadcast_in_dim.36), calls=%async_computation | async-start | bytes 2359296 | tf_op jit(solution)/shard_map/all_to_all | solution.py:143
  14.8 12.6 %collective-permute-start = (bf16[384,128]{1,0:T(8,128)(2,1)S(1)}, bf16[384,128]{1,0:T(8,128)(2,1)S(1)}, u32[]{:S(2)}, u32[]{:S(2)}) collective-permute-start(bf16[384,128]{1,0:T(8,128)(2,1)S(1)} %bitcast.29), channel_id=1, source_target_pairs={{0,11},{1,12},{2,13},{3,14},{4,15},{5,0},{6,1},{7,2},{8,3},{9,4},{... | collective-permute-start | bytes 294920 | tf_op jit(solution)/shard_map/ppermute | solution.py:131
  29.3 8.2 %collective-permute-done = bf16[384,128]{1,0:T(8,128)(2,1)S(1)} collective-permute-done((bf16[384,128]{1,0:T(8,128)(2,1)S(1)}, bf16[384,128]{1,0:T(8,128)(2,1)S(1)}, u32[]{:S(2)}, u32[]{:S(2)}) %collective-permute-start) | collective-permute-done | bytes 98336 | tf_op jit(solution)/shard_map/ppermute | solution.py:131
  37.6 10.0 %collective-permute-done.1 = bf16[384,128]{1,0:T(8,128)(2,1)S(1)} collective-permute-done((bf16[384,128]{1,0:T(8,128)(2,1)S(1)}, bf16[384,128]{1,0:T(8,128)(2,1)S(1)}, u32[]{:S(2)}, u32[]{:S(2)}) %collective-permute-start.1) | collective-permute-done | bytes 98336 | tf_op jit(solution)/shard_map/ppermute | solution.py:131
  47.6 2.4 %collective-permute-start.2 = (bf16[3,384,128]{2,1,0:T(8,128)(2,1)S(1)}, bf16[3,384,128]{2,1,0:T(8,128)(2,1)S(1)}, u32[]{:S(2)}, u32[]{:S(2)}) collective-permute-start(bf16[3,384,128]{2,1,0:T(8,128)(2,1)S(1)} %pad_maximum_fusion.s0), channel_id=1, source_target_pairs={{0,15},{1,0},{2,1},{3,2},{4,3},{5,4},{6,5},{7,6},{8,7},{9,8},{10,9... | collective-permute-start | bytes 884744 | tf_op jit(solution)/shard_map/ppermute | solution.py:131
  50.1 3.4 %collective-permute-start.3 = (bf16[3,384,128]{2,1,0:T(8,128)(2,1)S(1)}, bf16[3,384,128]{2,1,0:T(8,128)(2,1)S(1)}, u32[]{:S(2)}, u32[]{:S(2)}) collective-permute-start(bf16[3,384,128]{2,1,0:T(8,128)(2,1)S(1)} %pad_maximum_fusion.s0), channel_id=1, source_target_pairs={{0,1},{1,2},{2,3},{3,4},{4,5},{5,6},{6,7},{7,8},{8,9},{9,10},{10,1... | collective-permute-start | bytes 884744 | tf_op jit(solution)/shard_map/ppermute | solution.py:131
  53.5 2.8 %collective-permute-done.2.a1 = bf16[3,384,128]{2,1,0:T(8,128)(2,1)S(1)} collective-permute-done((bf16[3,384,128]{2,1,0:T(8,128)(2,1)S(1)}, bf16[3,384,128]{2,1,0:T(8,128)(2,1)S(1)}, u32[]{:S(2)}, u32[]{:S(2)}) %collective-permute-start.2) | collective-permute-done | bytes 294944 | tf_op jit(solution)/shard_map/ppermute | solution.py:131
  56.9 3.5 %collective-permute-start.6 = (bf16[1,384,128]{2,1,0:T(8,128)(2,1)}, bf16[1,384,128]{2,1,0:T(8,128)(2,1)S(1)}, u32[]{:S(2)}, u32[]{:S(2)}) collective-permute-start(bf16[1,384,128]{2,1,0:T(8,128)(2,1)} %slice.31), channel_id=1, source_target_pairs={{0,14},{1,15},{2,0},{3,1},{4,2},{5,3},{6,4},{7,5},{8,6},{9,7},{10,... | collective-permute-start | bytes 294920 | tf_op jit(solution)/shard_map/ppermute | solution.py:131
  60.5 2.2 %collective-permute-start.4 = (bf16[3,384,128]{2,1,0:T(8,128)(2,1)S(1)}, bf16[3,384,128]{2,1,0:T(8,128)(2,1)S(1)}, u32[]{:S(2)}, u32[]{:S(2)}) collective-permute-start(bf16[3,384,128]{2,1,0:T(8,128)(2,1)S(1)} %collective-permute-done.2.a1), channel_id=1, source_target_pairs={{0,15},{1,0},{2,1},{3,2},{4,3},{5,4},{6,5},{7,6},{8,7},{9,8},{10,9... | collective-permute-start | bytes 884744 | tf_op jit(solution)/shard_map/ppermute | solution.py:131
  62.7 3.6 %collective-permute-start.5 = (bf16[3,384,128]{2,1,0:T(8,128)(2,1)S(1)}, bf16[3,384,128]{2,1,0:T(8,128)(2,1)S(1)}, u32[]{:S(2)}, u32[]{:S(2)}) collective-permute-start(bf16[3,384,128]{2,1,0:T(8,128)(2,1)S(1)} %collective-permute-done.3.b1), channel_id=1, source_target_pairs={{0,1},{1,2},{2,3},{3,4},{4,5},{5,6},{6,7},{7,8},{8,9},{9,10},{10,1... | collective-permute-start | bytes 884744 | tf_op jit(solution)/shard_map/ppermute | solution.py:131
  66.5 6.1 %collective-permute-done.5.b2 = bf16[3,384,128]{2,1,0:T(8,128)(2,1)S(1)} collective-permute-done((bf16[3,384,128]{2,1,0:T(8,128)(2,1)S(1)}, bf16[3,384,128]{2,1,0:T(8,128)(2,1)S(1)}, u32[]{:S(2)}, u32[]{:S(2)}) %collective-permute-start.5) | collective-permute-done | bytes 294944 | tf_op jit(solution)/shard_map/ppermute | solution.py:131
  72.6 9.5 %shard_map.85 = (bf16[128,3072]{1,0:T(8,128)(2,1)}, bf16[48,64,128]{2,1,0:T(8,128)(2,1)S(1)}, bf16[96,64,128]{2,1,0:T(8,128)(2,1)S(1)}) custom-call(s32[32,8]{1,0:T(8,128)S(1)} %pad_add_fusion.ids, bf16[32,144,128]{2,1,0:T(8,128)(2,1)S(1)} %all-to-all-done.weights, bf16[3,384,128]{2,1,0:T(8,128)(2,1)S(1)} %pad_maximum_fusion.s0, ...), custom_call_target="tpu_custom_call" | custom-call | flops 400000000 | bytes 6291456 | tf_op jit(solution)/shard_map/pallas_call | solution.py:152
  82.1 3.3 %shard_map.86 = (bf16[3,384,128]{2,1,0:T(8,128)(2,1)S(1)}, bf16[3,384,128]{2,1,0:T(8,128)(2,1)S(1)}, bf16[3,384,128]{2,1,0:T(8,128)(2,1)S(1)}, bf16[3,384,128]{2...) custom-call(s32[32,8]{1,0:T(8,128)S(1)} %pad_add_fusion.ids, ...), custom_call_target="tpu_custom_call" | custom-call | flops 300000000 | bytes 6291456 | tf_op jit(solution)/shard_map/pallas_call | solution.py:162
  85.4 2.3 %collective-permute-start.7 = (bf16[3,384,128]{2,1,0:T(8,128)(2,1)S(1)}, bf16[3,384,128]{2,1,0:T(8,128)(2,1)S(1)}, u32[]{:S(2)}, u32[]{:S(2)}) collective-permute-start(bf16[3,384,128]{2,1,0:T(8,128)(2,1)S(1)} %get-tuple-element.16), channel_id=1, source_target_pairs={{0,1},{1,2},{2,3},{3,4},{4,5},{5,6},{6,7},{7,8},{8,9},{9,10},{10,1... | collective-permute-start | bytes 884744 | tf_op jit(solution)/shard_map/ppermute | solution.py:131
  87.8 4.5 %collective-permute-start.8 = (bf16[1,384,128]{2,1,0:T(8,128)(2,1)S(1)}, bf16[1,384,128]{2,1,0:T(8,128)(2,1)S(1)}, u32[]{:S(2)}, u32[]{:S(2)}) collective-permute-start(bf16[1,384,128]{2,1,0:T(8,128)(2,1)S(1)} %get-tuple-element.17), channel_id=1, source_target_pairs={{0,2},{1,3},{2,4},{3,5},{4,6},{5,7},{6,8},{7,9},{8,10},{9,11},{10,... | collective-permute-start | bytes 294920 | tf_op jit(solution)/shard_map/ppermute | solution.py:131
  92.3 3.5 %collective-permute-start.10 = (bf16[3,384,128]{2,1,0:T(8,128)(2,1)S(1)}, bf16[3,384,128]{2,1,0:T(8,128)(2,1)S(1)}, u32[]{:S(2)}, u32[]{:S(2)}) collective-permute-start(bf16[3,384,128]{2,1,0:T(8,128)(2,1)S(1)} %get-tuple-element.19), channel_id=1, source_target_pairs={{0,15},{1,0},{2,1},{3,2},{4,3},{5,4},{6,5},{7,6},{8,7},{9,8},{10,9... | collective-permute-start | bytes 884744 | tf_op jit(solution)/shard_map/ppermute | solution.py:131
  98.3 4.4 %collective-permute-start.9 = (bf16[3,384,128]{2,1,0:T(8,128)(2,1)S(1)}, bf16[3,384,128]{2,1,0:T(8,128)(2,1)S(1)}, u32[]{:S(2)}, u32[]{:S(2)}) collective-permute-start(bf16[3,384,128]{2,1,0:T(8,128)(2,1)S(1)} %add_convert_fusion.2), channel_id=1, source_target_pairs={{0,1},{1,2},{2,3},{3,4},{4,5},{5,6},{6,7},{7,8},{8,9},{9,10},{10,1... | collective-permute-start | bytes 884744 | tf_op jit(solution)/shard_map/ppermute | solution.py:131
  102.9 3.1 %collective-permute-start.11 = (bf16[3,384,128]{2,1,0:T(8,128)(2,1)S(1)}, bf16[3,384,128]{2,1,0:T(8,128)(2,1)S(1)}, u32[]{:S(2)}, u32[]{:S(2)}) collective-permute-start(bf16[3,384,128]{2,1,0:T(8,128)(2,1)S(1)} %add_convert_fusion.1), channel_id=1, source_target_pairs={{0,15},{1,0},{2,1},{3,2},{4,3},{5,4},{6,5},{7,6},{8,7},{9,8},{10,9... | collective-permute-start | bytes 884744 | tf_op jit(solution)/shard_map/ppermute | solution.py:131
  106.0 4.4 %shard_map.87 = bf16[32,128,128]{2,1,0:T(8,128)(2,1)} custom-call(s32[32,8]{1,0:T(8,128)S(1)} %pad_add_fusion.ids, bf16[96,64,128]{2,1,0:T(8,128)(2,1)S(1)} %get-tuple-element.20.whole, bf16[48,64,128]{2,1,0:T(8,128)(2,1)S(1)} %get-tuple-element.13.grad), custom_call_target="tpu_custom_call" | custom-call | flops 300000000 | bytes 6291456 | tf_op jit(solution)/shard_map/pallas_call | solution.py:182
  110.4 7.4 %all-to-all-start.1 = ((bf16[32,128,128]{2,1,0:T(8,128)(2,1)}), bf16[32,128,128]{2,1,0:T(8,128)(2,1)S(1)}, u32[]{:S(2)}, u32[]{:S(2)}) async-start(bf16[32,128,128]{2,1,0:T(8,128)(2,1)} %shard_map.87), calls=%async_computation.1 | async-start | bytes 2097152 | tf_op jit(solution)/shard_map/all_to_all | solution.py:183
  118.0 7.4 %collective-permute-start.12 = (bf16[384,128]{1,0:T(8,128)(2,1)S(1)}, bf16[384,128]{1,0:T(8,128)(2,1)S(1)}, u32[]{:S(2)}, u32[]{:S(2)}) collective-permute-start(bf16[384,128]{1,0:T(8,128)(2,1)S(1)} %get-tuple-element.36), channel_id=1, source_target_pairs={{0,5},{1,6},{2,7},{3,8},{4,9},{5,10},{6,11},{7,12},{8,13},{9,14},{... | collective-permute-start | bytes 294920 | tf_op jit(solution)/shard_map/ppermute | solution.py:131
  125.4 4.4 %collective-permute-start.13 = (bf16[384,128]{1,0:T(8,128)(2,1)S(1)}, bf16[384,128]{1,0:T(8,128)(2,1)S(1)}, u32[]{:S(2)}, u32[]{:S(2)}) collective-permute-start(bf16[384,128]{1,0:T(8,128)(2,1)S(1)} %get-tuple-element.37), channel_id=1, source_target_pairs={{0,11},{1,12},{2,13},{3,14},{4,15},{5,0},{6,1},{7,2},{8,3},{9,4},{... | collective-permute-start | bytes 294920 | tf_op jit(solution)/shard_map/ppermute | solution.py:131
  129.9 4.5 %collective-permute-done.12 = bf16[384,128]{1,0:T(8,128)(2,1)S(1)} collective-permute-done((bf16[384,128]{1,0:T(8,128)(2,1)S(1)}, bf16[384,128]{1,0:T(8,128)(2,1)S(1)}, u32[]{:S(2)}, u32[]{:S(2)}) %collective-permute-start.12) | collective-permute-done | bytes 98336 | tf_op jit(solution)/shard_map/ppermute | solution.py:131
  134.4 9.9 %collective-permute-done.13 = bf16[384,128]{1,0:T(8,128)(2,1)S(1)} collective-permute-done((bf16[384,128]{1,0:T(8,128)(2,1)S(1)}, bf16[384,128]{1,0:T(8,128)(2,1)S(1)}, u32[]{:S(2)}, u32[]{:S(2)}) %collective-permute-start.13) | collective-permute-done | bytes 98336 | tf_op jit(solution)/shard_map/ppermute | solution.py:131
  (44 shorter events, 11.3 us)
Async XLA Ops:
  5.0 9.6 %copy-start.1 = (bf16[128,384]{1,0:T(8,128)(2,1)S(1)}, bf16[128,384]{1,0:T(8,128)(2,1)}, u32[]{:S(2)}) copy-start(bf16[128,384]{1,0:T(8,128)(2,1)} %param.6) | copy-start | bytes 294916
  5.0 61.3 %all-to-all-start = ((bf16[32,144,128]{2,1,0:T(8,128)(2,1)}), bf16[32,144,128]{2,1,0:T(8,128)(2,1)S(1)}, u32[]{:S(2)}, u32[]{:S(2)}) async-start(bf16[32,144,128]{2,1,0:T(8,128)(2,1)} %broadcast_in_dim.36), calls=%async_computation | async-start | bytes 2359296 | tf_op jit(solution)/shard_map/all_to_all | solution.py:143
  14.7 58.0 %copy-start = (bf16[128,3072]{1,0:T(8,128)(2,1)S(1)}, bf16[128,3072]{1,0:T(8,128)(2,1)}, u32[]{:S(2)}) copy-start(bf16[128,3072]{1,0:T(8,128)(2,1)} %upstream.1) | copy-start | bytes 2359300
  14.8 22.8 %collective-permute-start = (bf16[384,128]{1,0:T(8,128)(2,1)S(1)}, bf16[384,128]{1,0:T(8,128)(2,1)S(1)}, u32[]{:S(2)}, u32[]{:S(2)}) collective-permute-start(bf16[384,128]{1,0:T(8,128)(2,1)S(1)} %bitcast.29), channel_id=1, source_target_pairs={{0,11},{1,12},{2,13},{3,14},{4,15},{5,0},{6,1},{7,2},{8,3},{9,4},{... | collective-permute-start | bytes 294920 | tf_op jit(solution)/shard_map/ppermute | solution.py:131
  27.4 20.2 %collective-permute-start.1 = (bf16[384,128]{1,0:T(8,128)(2,1)S(1)}, bf16[384,128]{1,0:T(8,128)(2,1)S(1)}, u32[]{:S(2)}, u32[]{:S(2)}) collective-permute-start(bf16[384,128]{1,0:T(8,128)(2,1)S(1)} %bitcast.30), channel_id=1, source_target_pairs={{0,5},{1,6},{2,7},{3,8},{4,9},{5,10},{6,11},{7,12},{8,13},{9,14},{... | collective-permute-start | bytes 294920 | tf_op jit(solution)/shard_map/ppermute | solution.py:131
  47.6 8.6 %collective-permute-start.2 = (bf16[3,384,128]{2,1,0:T(8,128)(2,1)S(1)}, bf16[3,384,128]{2,1,0:T(8,128)(2,1)S(1)}, u32[]{:S(2)}, u32[]{:S(2)}) collective-permute-start(bf16[3,384,128]{2,1,0:T(8,128)(2,1)S(1)} %pad_maximum_fusion.s0), channel_id=1, source_target_pairs={{0,15},{1,0},{2,1},{3,2},{4,3},{5,4},{6,5},{7,6},{8,7},{9,8},{10,9... | collective-permute-start | bytes 884744 | tf_op jit(solution)/shard_map/ppermute | solution.py:131
  50.1 12.6 %collective-permute-start.3 = (bf16[3,384,128]{2,1,0:T(8,128)(2,1)S(1)}, bf16[3,384,128]{2,1,0:T(8,128)(2,1)S(1)}, u32[]{:S(2)}, u32[]{:S(2)}) collective-permute-start(bf16[3,384,128]{2,1,0:T(8,128)(2,1)S(1)} %pad_maximum_fusion.s0), channel_id=1, source_target_pairs={{0,1},{1,2},{2,3},{3,4},{4,5},{5,6},{6,7},{7,8},{8,9},{9,10},{10,1... | collective-permute-start | bytes 884744 | tf_op jit(solution)/shard_map/ppermute | solution.py:131
  56.9 9.6 %collective-permute-start.6 = (bf16[1,384,128]{2,1,0:T(8,128)(2,1)}, bf16[1,384,128]{2,1,0:T(8,128)(2,1)S(1)}, u32[]{:S(2)}, u32[]{:S(2)}) collective-permute-start(bf16[1,384,128]{2,1,0:T(8,128)(2,1)} %slice.31), channel_id=1, source_target_pairs={{0,14},{1,15},{2,0},{3,1},{4,2},{5,3},{6,4},{7,5},{8,6},{9,7},{10,... | collective-permute-start | bytes 294920 | tf_op jit(solution)/shard_map/ppermute | solution.py:131
  60.5 12.2 %collective-permute-start.4 = (bf16[3,384,128]{2,1,0:T(8,128)(2,1)S(1)}, bf16[3,384,128]{2,1,0:T(8,128)(2,1)S(1)}, u32[]{:S(2)}, u32[]{:S(2)}) collective-permute-start(bf16[3,384,128]{2,1,0:T(8,128)(2,1)S(1)} %collective-permute-done.2.a1), channel_id=1, source_target_pairs={{0,15},{1,0},{2,1},{3,2},{4,3},{5,4},{6,5},{7,6},{8,7},{9,8},{10,9... | collective-permute-start | bytes 884744 | tf_op jit(solution)/shard_map/ppermute | solution.py:131
  62.7 9.9 %collective-permute-start.5 = (bf16[3,384,128]{2,1,0:T(8,128)(2,1)S(1)}, bf16[3,384,128]{2,1,0:T(8,128)(2,1)S(1)}, u32[]{:S(2)}, u32[]{:S(2)}) collective-permute-start(bf16[3,384,128]{2,1,0:T(8,128)(2,1)S(1)} %collective-permute-done.3.b1), channel_id=1, source_target_pairs={{0,1},{1,2},{2,3},{3,4},{4,5},{5,6},{6,7},{7,8},{8,9},{9,10},{10,1... | collective-permute-start | bytes 884744 | tf_op jit(solution)/shard_map/ppermute | solution.py:131
  85.4 12.8 %collective-permute-start.7 = (bf16[3,384,128]{2,1,0:T(8,128)(2,1)S(1)}, bf16[3,384,128]{2,1,0:T(8,128)(2,1)S(1)}, u32[]{:S(2)}, u32[]{:S(2)}) collective-permute-start(bf16[3,384,128]{2,1,0:T(8,128)(2,1)S(1)} %get-tuple-element.16), channel_id=1, source_target_pairs={{0,1},{1,2},{2,3},{3,4},{4,5},{5,6},{6,7},{7,8},{8,9},{9,10},{10,1... | collective-permute-start | bytes 884744 | tf_op jit(solution)/shard_map/ppermute | solution.py:131
  87.8 10.0 %collective-permute-start.8 = (bf16[1,384,128]{2,1,0:T(8,128)(2,1)S(1)}, bf16[1,384,128]{2,1,0:T(8,128)(2,1)S(1)}, u32[]{:S(2)}, u32[]{:S(2)}) collective-permute-start(bf16[1,384,128]{2,1,0:T(8,128)(2,1)S(1)} %get-tuple-element.17), channel_id=1, source_target_pairs={{0,2},{1,3},{2,4},{3,5},{4,6},{5,7},{6,8},{7,9},{8,10},{9,11},{10,... | collective-permute-start | bytes 294920 | tf_op jit(solution)/shard_map/ppermute | solution.py:131
  92.3 10.5 %collective-permute-start.10 = (bf16[3,384,128]{2,1,0:T(8,128)(2,1)S(1)}, bf16[3,384,128]{2,1,0:T(8,128)(2,1)S(1)}, u32[]{:S(2)}, u32[]{:S(2)}) collective-permute-start(bf16[3,384,128]{2,1,0:T(8,128)(2,1)S(1)} %get-tuple-element.19), channel_id=1, source_target_pairs={{0,15},{1,0},{2,1},{3,2},{4,3},{5,4},{6,5},{7,6},{8,7},{9,8},{10,9... | collective-permute-start | bytes 884744 | tf_op jit(solution)/shard_map/ppermute | solution.py:131
  98.3 19.5 %collective-permute-start.9 = (bf16[3,384,128]{2,1,0:T(8,128)(2,1)S(1)}, bf16[3,384,128]{2,1,0:T(8,128)(2,1)S(1)}, u32[]{:S(2)}, u32[]{:S(2)}) collective-permute-start(bf16[3,384,128]{2,1,0:T(8,128)(2,1)S(1)} %add_convert_fusion.2), channel_id=1, source_target_pairs={{0,1},{1,2},{2,3},{3,4},{4,5},{5,6},{6,7},{7,8},{8,9},{9,10},{10,1... | collective-permute-start | bytes 884744 | tf_op jit(solution)/shard_map/ppermute | solution.py:131
  102.9 14.9 %collective-permute-start.11 = (bf16[3,384,128]{2,1,0:T(8,128)(2,1)S(1)}, bf16[3,384,128]{2,1,0:T(8,128)(2,1)S(1)}, u32[]{:S(2)}, u32[]{:S(2)}) collective-permute-start(bf16[3,384,128]{2,1,0:T(8,128)(2,1)S(1)} %add_convert_fusion.1), channel_id=1, source_target_pairs={{0,15},{1,0},{2,1},{3,2},{4,3},{5,4},{6,5},{7,6},{8,7},{9,8},{10,9... | collective-permute-start | bytes 884744 | tf_op jit(solution)/shard_map/ppermute | solution.py:131
  110.4 34.7 %all-to-all-start.1 = ((bf16[32,128,128]{2,1,0:T(8,128)(2,1)}), bf16[32,128,128]{2,1,0:T(8,128)(2,1)S(1)}, u32[]{:S(2)}, u32[]{:S(2)}) async-start(bf16[32,128,128]{2,1,0:T(8,128)(2,1)} %shard_map.87), calls=%async_computation.1 | async-start | bytes 2097152 | tf_op jit(solution)/shard_map/all_to_all | solution.py:183
  118.0 16.4 %collective-permute-start.12 = (bf16[384,128]{1,0:T(8,128)(2,1)S(1)}, bf16[384,128]{1,0:T(8,128)(2,1)S(1)}, u32[]{:S(2)}, u32[]{:S(2)}) collective-permute-start(bf16[384,128]{1,0:T(8,128)(2,1)S(1)} %get-tuple-element.36), channel_id=1, source_target_pairs={{0,5},{1,6},{2,7},{3,8},{4,9},{5,10},{6,11},{7,12},{8,13},{9,14},{... | collective-permute-start | bytes 294920 | tf_op jit(solution)/shard_map/ppermute | solution.py:131
  125.4 18.9 %collective-permute-start.13 = (bf16[384,128]{1,0:T(8,128)(2,1)S(1)}, bf16[384,128]{1,0:T(8,128)(2,1)S(1)}, u32[]{:S(2)}, u32[]{:S(2)}) collective-permute-start(bf16[384,128]{1,0:T(8,128)(2,1)S(1)} %get-tuple-element.37), channel_id=1, source_target_pairs={{0,11},{1,12},{2,13},{3,14},{4,15},{5,0},{6,1},{7,2},{8,3},{9,4},{... | collective-permute-start | bytes 294920 | tf_op jit(solution)/shard_map/ppermute | solution.py:131

commit v2 on v1

--- a/solution.py
+++ b/solution.py
@@ -68,7 +68,7 @@
     lax.fori_loop(0, 24, some_columns, 0)
 
 
-def input_kernel(ids, weights, grad, v0, a1, b1, a2, b2, e8, total):
+def input_kernel(ids, weights, grad, out, total):
     total[...] = jnp.zeros_like(total)
 
     def some_slots(g, carry):
@@ -77,15 +77,15 @@
             for j in range(4):
                 half = (j % 2) * BLK
                 block = weights[d, (j // 2) * BLK : (j // 2 + 1) * BLK, half : half + BLK]
-                row, column = ids[d, j], ids[d, 4 + j]
+                row, column = ids[d, 8 + j], ids[d, 4 + j]
                 total[row] += dot(block, grad[column])
         return carry
 
     lax.fori_loop(0, 8, some_slots, 0)
-    for piece, offsets in ((v0, SEEDS), (a1, ABOVE1), (b1, BELOW1), (a2, ABOVE2), (b2, BELOW2), (e8, (8,))):
-        for k, offset in enumerate(offsets):
-            at = offset % 16 * 6
-            piece[k] = total[at : at + 6].reshape(384, 128).astype(BF)
+    for o in range(16):
+        out[400 * o : 400 * o + 384] = total[6 * o : 6 * o + 6].reshape(384, 128).astype(BF)
+        if o < 15:
+            out[400 * o + 384 : 400 * o + 400] = jnp.zeros((16, 128), BF)
 
 
 def weight_kernel(ids, whole, grad, out):
@@ -143,7 +143,7 @@
     parcels = lax.all_to_all(parcel, "row", 0, 0, tiled=True)
     ids = parcels[:, 128, :8].astype(jnp.int32)
     rows = (ids[:, :4] + (96 - 6 * me_col)) % 96
-    ids = jnp.concatenate([rows, ids[:, 4:]], axis=1)
+    ids = jnp.concatenate([rows, ids[:, 4:], ids[:, :4]], axis=1)
 
     above1, below1 = shift(far, -1), shift(far, 1)
     above2, below2 = shift(above1, -1), shift(below1, 1)
@@ -158,33 +158,14 @@
         24,
     )(ids, parcels, far, above1, below1, above2, below2, eight, hidden_grad)
 
-    three = shape(3, 384, 128)
-    v0, a1, b1, a2, b2, e8 = call(
-        input_kernel,
-        (three, three, three, three, three, shape(1, 384, 128)),
-        3,
-        [pltpu.VMEM((96, BLK, 128), F32)],
-        300_000_000,
-        24,
-    )(ids, parcels, grad)
-
-    def plus(a, *more):
-        total = a.astype(F32)
-        for m in more:
-            total = total + m.astype(F32)
-        return total.astype(BF)
-
-    from8 = shift(e8, 2)
-    up, down = shift(a2, 1), shift(b2, -1)
-    a1 = plus(a1, up, jnp.pad(from8, ((1, 1), (0, 0), (0, 0))))
-    b1 = plus(b1, down)
-
     terms = call(weight_kernel, shape(n_row, 128, 128), 3, [], 300_000_000, 16)(ids, whole, grad)
     back = lax.all_to_all(terms, "row", 0, 0, tiled=True)
 
-    v0 = plus(v0, shift(a1, 1), shift(b1, -1))
-    own = plus(v0[0], shift(v0[1], 5), shift(v0[2], -5))
-    input_grad = own.T
+    part = call(
+        input_kernel, shape(6384, 128), 3, [pltpu.VMEM((96, BLK, 128), F32)], 300_000_000, 24
+    )(ids, parcels, grad)
+    own = lax.optimization_barrier(lax.psum_scatter(part, "col", scatter_dimension=0, tiled=True))
+    input_grad = lax.dynamic_slice_in_dim(own, me_col, 384, 0).T
 
     sums = jnp.sum(back.astype(F32), axis=0).astype(BF)
     sums = sums.reshape(2, BLK, 2, BLK).transpose(0, 2, 1, 3).reshape(4, BLK * BLK)

time: 148 us -> 145 us (0.980)
  blocking collectives: 0 us -> 37.3 us
  starting transfers between devices: 76.5 us -> 48.5 us
  waiting for transfers between devices: 44 us -> 27.1 us
  local copies, waits for them, and re-layouts: 4.01 us -> 7.95 us
    unnamed x0 -> x1, blocking collectives: none -> 37.3 us
    ppermute x14 -> x7, starting transfers between devices: 59.5 us -> 29.6 us  [shift(): return lax.ppermute(a, 'col', [(i, (i + by) % n_col) for i in range(n_col)])]
    ppermute x14 -> x7, waiting for transfers between devices: 43.9 us -> 27.1 us  [shift(): return lax.ppermute(a, 'col', [(i, (i + by) % n_col) for i in range(n_col)])]
    unnamed x6 -> x14, local copies, waits for them, and re-layouts: 0.88 us -> 4.82 us
    unnamed x0 -> x1, starting transfers between devices: none -> 1.79 us
  transfers between devices with their start and end apart: 16 -> 10, of which waited for: 8 -> 5; matrix products, arithmetic and copies ran while one was open for 1% -> 28% of each run, Pallas kernels for 3% -> 2%
where the time goes in v2:
time: 145 us; the launch traced here: 144 us
  starting transfers between devices  48.5 us (33%)
  blocking collectives  37.3 us (26%)
  waiting for transfers between devices  27.1 us (19%)
  Pallas kernels  17.3 us (12%)
  local copies, waits for them, and re-layouts  7.95 us (5%)
  other arithmetic  3.78 us (3%)
  between operations  2.18 us (2%)
    unnamed x1, blocking collectives  37.3 us
    ppermute x7, starting transfers between devices, shift(): return lax.ppermute(a, 'col', [(i, (i + by) % n_col) for i in range(n_col)])  29.6 us
    ppermute x7, waiting for transfers between devices, shift(): return lax.ppermute(a, 'col', [(i, (i + by) % n_col) for i in range(n_col)])  27.1 us
    all_to_all x1, starting transfers between devices, on_device(): parcels = lax.all_to_all(parcel, 'row', 0, 0, tiled=True)  9.61 us
    pallas_call x1, Pallas kernels, on_device(): call(forward_kernel, (shape(128, 3072), shape(48, BLK, 128), shape(96, BL...  9.49 us
    all_to_all x1, starting transfers between devices, on_device(): back = lax.all_to_all(terms, 'row', 0, 0, tiled=True)  7.44 us
    unnamed x14, local copies, waits for them, and re-layouts  4.82 us
    pallas_call x1, Pallas kernels, on_device(): call(weight_kernel, shape(n_row, 128, 128), 3, [], 300000000, 16)  4.43 us
  transfers between devices with their start and end apart: 10, of which 5 were waited for; matrix products, arithmetic and copies ran while one was open for 28% of the time, Pallas kernels for 2%

profile of v2, /device:TPU:6, one launch (start us, length us, event | category | flops | bytes accessed | tf_op | source)
XLA Modules:
  0.0 144.0 jit_solution(16967962599240738680)
XLA Ops:
  3.8 1.2 broadcast_in_dim.36
  5.0 9.6 %all-to-all-start = ((bf16[32,144,128]{2,1,0:T(8,128)(2,1)}), bf16[32,144,128]{2,1,0:T(8,128)(2,1)S(1)}, u32[]{:S(2)}, u32[]{:S(2)}) async-start(bf16[32,144,128]{2,1,0:T(8,128)(2,1)} %broadcast_in_dim.36), calls=%async_computation | async-start | bytes 2359296 | tf_op jit(solution)/shard_map/all_to_all | solution.py:143
  14.8 12.5 %collective-permute-start = (bf16[384,128]{1,0:T(8,128)(2,1)S(1)}, bf16[384,128]{1,0:T(8,128)(2,1)S(1)}, u32[]{:S(2)}, u32[]{:S(2)}) collective-permute-start(bf16[384,128]{1,0:T(8,128)(2,1)S(1)} %bitcast.23), channel_id=1, source_target_pairs={{0,11},{1,12},{2,13},{3,14},{4,15},{5,0},{6,1},{7,2},{8,3},{9,4},{... | collective-permute-start | bytes 294920 | tf_op jit(solution)/shard_map/ppermute | solution.py:131
  27.3 1.9 %collective-permute-start.1 = (bf16[384,128]{1,0:T(8,128)(2,1)S(1)}, bf16[384,128]{1,0:T(8,128)(2,1)S(1)}, u32[]{:S(2)}, u32[]{:S(2)}) collective-permute-start(bf16[384,128]{1,0:T(8,128)(2,1)S(1)} %bitcast.24), channel_id=1, source_target_pairs={{0,5},{1,6},{2,7},{3,8},{4,9},{5,10},{6,11},{7,12},{8,13},{9,14},{... | collective-permute-start | bytes 294920 | tf_op jit(solution)/shard_map/ppermute | solution.py:131
  29.2 8.2 %collective-permute-done = bf16[384,128]{1,0:T(8,128)(2,1)S(1)} collective-permute-done((bf16[384,128]{1,0:T(8,128)(2,1)S(1)}, bf16[384,128]{1,0:T(8,128)(2,1)S(1)}, u32[]{:S(2)}, u32[]{:S(2)}) %collective-permute-start) | collective-permute-done | bytes 98336 | tf_op jit(solution)/shard_map/ppermute | solution.py:131
  37.4 10.0 %collective-permute-done.1 = bf16[384,128]{1,0:T(8,128)(2,1)S(1)} collective-permute-done((bf16[384,128]{1,0:T(8,128)(2,1)S(1)}, bf16[384,128]{1,0:T(8,128)(2,1)S(1)}, u32[]{:S(2)}, u32[]{:S(2)}) %collective-permute-start.1) | collective-permute-done | bytes 98336 | tf_op jit(solution)/shard_map/ppermute | solution.py:131
  47.5 2.4 %collective-permute-start.2 = (bf16[3,384,128]{2,1,0:T(8,128)(2,1)S(1)}, bf16[3,384,128]{2,1,0:T(8,128)(2,1)S(1)}, u32[]{:S(2)}, u32[]{:S(2)}) collective-permute-start(bf16[3,384,128]{2,1,0:T(8,128)(2,1)S(1)} %pad_maximum_fusion.s0), channel_id=1, source_target_pairs={{0,15},{1,0},{2,1},{3,2},{4,3},{5,4},{6,5},{7,6},{8,7},{9,8},{10,9... | collective-permute-start | bytes 884744 | tf_op jit(solution)/shard_map/ppermute | solution.py:131
  49.9 3.4 %collective-permute-start.3 = (bf16[3,384,128]{2,1,0:T(8,128)(2,1)S(1)}, bf16[3,384,128]{2,1,0:T(8,128)(2,1)S(1)}, u32[]{:S(2)}, u32[]{:S(2)}) collective-permute-start(bf16[3,384,128]{2,1,0:T(8,128)(2,1)S(1)} %pad_maximum_fusion.s0), channel_id=1, source_target_pairs={{0,1},{1,2},{2,3},{3,4},{4,5},{5,6},{6,7},{7,8},{8,9},{9,10},{10,1... | collective-permute-start | bytes 884744 | tf_op jit(solution)/shard_map/ppermute | solution.py:131
  53.4 2.8 %collective-permute-done.2.a1 = bf16[3,384,128]{2,1,0:T(8,128)(2,1)S(1)} collective-permute-done((bf16[3,384,128]{2,1,0:T(8,128)(2,1)S(1)}, bf16[3,384,128]{2,1,0:T(8,128)(2,1)S(1)}, u32[]{:S(2)}, u32[]{:S(2)}) %collective-permute-start.2) | collective-permute-done | bytes 294944 | tf_op jit(solution)/shard_map/ppermute | solution.py:131
  56.8 3.5 %collective-permute-start.6 = (bf16[1,384,128]{2,1,0:T(8,128)(2,1)}, bf16[1,384,128]{2,1,0:T(8,128)(2,1)S(1)}, u32[]{:S(2)}, u32[]{:S(2)}) collective-permute-start(bf16[1,384,128]{2,1,0:T(8,128)(2,1)} %slice.20), channel_id=1, source_target_pairs={{0,14},{1,15},{2,0},{3,1},{4,2},{5,3},{6,4},{7,5},{8,6},{9,7},{10,... | collective-permute-start | bytes 294920 | tf_op jit(solution)/shard_map/ppermute | solution.py:131
  60.3 2.2 %collective-permute-start.4 = (bf16[3,384,128]{2,1,0:T(8,128)(2,1)S(1)}, bf16[3,384,128]{2,1,0:T(8,128)(2,1)S(1)}, u32[]{:S(2)}, u32[]{:S(2)}) collective-permute-start(bf16[3,384,128]{2,1,0:T(8,128)(2,1)S(1)} %collective-permute-done.2.a1), channel_id=1, source_target_pairs={{0,15},{1,0},{2,1},{3,2},{4,3},{5,4},{6,5},{7,6},{8,7},{9,8},{10,9... | collective-permute-start | bytes 884744 | tf_op jit(solution)/shard_map/ppermute | solution.py:131
  62.5 3.6 %collective-permute-start.5 = (bf16[3,384,128]{2,1,0:T(8,128)(2,1)S(1)}, bf16[3,384,128]{2,1,0:T(8,128)(2,1)S(1)}, u32[]{:S(2)}, u32[]{:S(2)}) collective-permute-start(bf16[3,384,128]{2,1,0:T(8,128)(2,1)S(1)} %collective-permute-done.3.b1), channel_id=1, source_target_pairs={{0,1},{1,2},{2,3},{3,4},{4,5},{5,6},{6,7},{7,8},{8,9},{9,10},{10,1... | collective-permute-start | bytes 884744 | tf_op jit(solution)/shard_map/ppermute | solution.py:131
  66.4 4.8 %collective-permute-done.4.a2 = bf16[3,384,128]{2,1,0:T(8,128)(2,1)S(1)} collective-permute-done((bf16[3,384,128]{2,1,0:T(8,128)(2,1)S(1)}, bf16[3,384,128]{2,1,0:T(8,128)(2,1)S(1)}, u32[]{:S(2)}, u32[]{:S(2)}) %collective-permute-start.4) | collective-permute-done | bytes 294944 | tf_op jit(solution)/shard_map/ppermute | solution.py:131
  71.1 1.3 collective-permute-done.5.b2
  72.5 9.5 %shard_map.85 = (bf16[128,3072]{1,0:T(8,128)(2,1)}, bf16[48,64,128]{2,1,0:T(8,128)(2,1)S(1)}, bf16[96,64,128]{2,1,0:T(8,128)(2,1)S(1)}) custom-call(s32[32,12]{1,0:T(8,128)S(1)} %pad_add_fusion.ids, bf16[32,144,128]{2,1,0:T(8,128)(2,1)S(1)} %all-to-all-done.weights, bf16[3,384,128]{2,1,0:T(8,128)(2,1)S(1)} %pad_maximum_fusion.s0, ...), custom_call_target="tpu_custom_call" | custom-call | flops 400000000 | bytes 6291456 | tf_op jit(solution)/shard_map/pallas_call | solution.py:152
  82.0 4.4 %shard_map.87 = bf16[32,128,128]{2,1,0:T(8,128)(2,1)} custom-call(s32[32,12]{1,0:T(8,128)S(1)} %pad_add_fusion.ids, bf16[96,64,128]{2,1,0:T(8,128)(2,1)S(1)} %get-tuple-element.8.whole, bf16[48,64,128]{2,1,0:T(8,128)(2,1)S(1)} %get-tuple-element.7.grad), custom_call_target="tpu_custom_call" | custom-call | flops 300000000 | bytes 6291456 | tf_op jit(solution)/shard_map/pallas_call | solution.py:161
  86.4 0.9 copy-done
  87.3 7.4 %all-to-all-start.1 = ((bf16[32,128,128]{2,1,0:T(8,128)(2,1)}), bf16[32,128,128]{2,1,0:T(8,128)(2,1)}, u32[]{:S(2)}, u32[]{:S(2)}) async-start(bf16[32,128,128]{2,1,0:T(8,128)(2,1)} %shard_map.87), calls=%async_computation.1 | async-start | bytes 2097152 | tf_op jit(solution)/shard_map/all_to_all | solution.py:162
  94.7 1.1 copy-done.1
  95.9 3.3 %shard_map.86 = bf16[6384,128]{1,0:T(8,128)(2,1)S(1)} custom-call(s32[32,12]{1,0:T(8,128)S(1)} %pad_add_fusion.ids, bf16[32,144,128]{2,1,0:T(8,128)(2,1)S(1)} %all-to-all-done.weights, bf16[48,64,128]{2,1,0:T(8,128)(2,1)S(1)} %copy-done.1), custom_call_target="tpu_custom_call" | custom-call | flops 300000000 | bytes 6291456 | tf_op jit(solution)/shard_map/pallas_call | solution.py:164
  99.2 37.3 %fusion = bf16[400,128]{1,0:T(8,128)(2,1)S(1)} fusion(bf16[6384,128]{1,0:T(8,128)(2,1)S(1)} %shard_map.86), kind=kCustom, calls=%all-reduce-scatter | all-reduce-scatter fusion | flops 819201 | bytes 1738752
  136.5 1.8 %collective-permute-start.7 = (bf16[15,128]{1,0:T(8,128)(2,1)S(1)}, bf16[15,128]{1,0:T(8,128)(2,1)S(1)}, u32[]{:S(2)}, u32[]{:S(2)}) collective-permute-start(bf16[15,128]{1,0:T(8,128)(2,1)S(1)} %slice.21), channel_id=1, source_target_pairs={{0,1},{1,2},{2,3},{3,4},{4,5},{5,6},{6,7},{7,8},{8,9},{9,10},{10,1... | collective-permute-start | bytes 11528
  138.3 1.3 dynamic-slice.4
  141.7 1.4 reduce_sum.12
  (37 shorter events, 5.9 us)
Async XLA Ops:
  3.8 10.8 %copy-start.3 = (bf16[128,384]{1,0:T(8,128)(2,1)S(1)}, bf16[128,384]{1,0:T(8,128)(2,1)}, u32[]{:S(2)}) copy-start(bf16[128,384]{1,0:T(8,128)(2,1)} %param.6) | copy-start | bytes 294916
  5.0 67.4 %copy-start.2 = (bf16[128,3072]{1,0:T(8,128)(2,1)S(1)}, bf16[128,3072]{1,0:T(8,128)(2,1)}, u32[]{:S(2)}) copy-start(bf16[128,3072]{1,0:T(8,128)(2,1)} %upstream.1) | copy-start | bytes 2359300
  5.0 61.2 %all-to-all-start = ((bf16[32,144,128]{2,1,0:T(8,128)(2,1)}), bf16[32,144,128]{2,1,0:T(8,128)(2,1)S(1)}, u32[]{:S(2)}, u32[]{:S(2)}) async-start(bf16[32,144,128]{2,1,0:T(8,128)(2,1)} %broadcast_in_dim.36), calls=%async_computation | async-start | bytes 2359296 | tf_op jit(solution)/shard_map/all_to_all | solution.py:143
  14.8 22.6 %collective-permute-start = (bf16[384,128]{1,0:T(8,128)(2,1)S(1)}, bf16[384,128]{1,0:T(8,128)(2,1)S(1)}, u32[]{:S(2)}, u32[]{:S(2)}) collective-permute-start(bf16[384,128]{1,0:T(8,128)(2,1)S(1)} %bitcast.23), channel_id=1, source_target_pairs={{0,11},{1,12},{2,13},{3,14},{4,15},{5,0},{6,1},{7,2},{8,3},{9,4},{... | collective-permute-start | bytes 294920 | tf_op jit(solution)/shard_map/ppermute | solution.py:131
  27.3 20.2 %collective-permute-start.1 = (bf16[384,128]{1,0:T(8,128)(2,1)S(1)}, bf16[384,128]{1,0:T(8,128)(2,1)S(1)}, u32[]{:S(2)}, u32[]{:S(2)}) collective-permute-start(bf16[384,128]{1,0:T(8,128)(2,1)S(1)} %bitcast.24), channel_id=1, source_target_pairs={{0,5},{1,6},{2,7},{3,8},{4,9},{5,10},{6,11},{7,12},{8,13},{9,14},{... | collective-permute-start | bytes 294920 | tf_op jit(solution)/shard_map/ppermute | solution.py:131
  47.5 8.6 %collective-permute-start.2 = (bf16[3,384,128]{2,1,0:T(8,128)(2,1)S(1)}, bf16[3,384,128]{2,1,0:T(8,128)(2,1)S(1)}, u32[]{:S(2)}, u32[]{:S(2)}) collective-permute-start(bf16[3,384,128]{2,1,0:T(8,128)(2,1)S(1)} %pad_maximum_fusion.s0), channel_id=1, source_target_pairs={{0,15},{1,0},{2,1},{3,2},{4,3},{5,4},{6,5},{7,6},{8,7},{9,8},{10,9... | collective-permute-start | bytes 884744 | tf_op jit(solution)/shard_map/ppermute | solution.py:131
  49.9 12.6 %collective-permute-start.3 = (bf16[3,384,128]{2,1,0:T(8,128)(2,1)S(1)}, bf16[3,384,128]{2,1,0:T(8,128)(2,1)S(1)}, u32[]{:S(2)}, u32[]{:S(2)}) collective-permute-start(bf16[3,384,128]{2,1,0:T(8,128)(2,1)S(1)} %pad_maximum_fusion.s0), channel_id=1, source_target_pairs={{0,1},{1,2},{2,3},{3,4},{4,5},{5,6},{6,7},{7,8},{8,9},{9,10},{10,1... | collective-permute-start | bytes 884744 | tf_op jit(solution)/shard_map/ppermute | solution.py:131
  56.8 9.6 %collective-permute-start.6 = (bf16[1,384,128]{2,1,0:T(8,128)(2,1)}, bf16[1,384,128]{2,1,0:T(8,128)(2,1)S(1)}, u32[]{:S(2)}, u32[]{:S(2)}) collective-permute-start(bf16[1,384,128]{2,1,0:T(8,128)(2,1)} %slice.20), channel_id=1, source_target_pairs={{0,14},{1,15},{2,0},{3,1},{4,2},{5,3},{6,4},{7,5},{8,6},{9,7},{10,... | collective-permute-start | bytes 294920 | tf_op jit(solution)/shard_map/ppermute | solution.py:131
  60.3 10.8 %collective-permute-start.4 = (bf16[3,384,128]{2,1,0:T(8,128)(2,1)S(1)}, bf16[3,384,128]{2,1,0:T(8,128)(2,1)S(1)}, u32[]{:S(2)}, u32[]{:S(2)}) collective-permute-start(bf16[3,384,128]{2,1,0:T(8,128)(2,1)S(1)} %collective-permute-done.2.a1), channel_id=1, source_target_pairs={{0,15},{1,0},{2,1},{3,2},{4,3},{5,4},{6,5},{7,6},{8,7},{9,8},{10,9... | collective-permute-start | bytes 884744 | tf_op jit(solution)/shard_map/ppermute | solution.py:131
  62.5 9.9 %collective-permute-start.5 = (bf16[3,384,128]{2,1,0:T(8,128)(2,1)S(1)}, bf16[3,384,128]{2,1,0:T(8,128)(2,1)S(1)}, u32[]{:S(2)}, u32[]{:S(2)}) collective-permute-start(bf16[3,384,128]{2,1,0:T(8,128)(2,1)S(1)} %collective-permute-done.3.b1), channel_id=1, source_target_pairs={{0,1},{1,2},{2,3},{3,4},{4,5},{5,6},{6,7},{7,8},{8,9},{9,10},{10,1... | collective-permute-start | bytes 884744 | tf_op jit(solution)/shard_map/ppermute | solution.py:131
  86.4 0.9 copy-start
  87.3 54.4 %all-to-all-start.1 = ((bf16[32,128,128]{2,1,0:T(8,128)(2,1)}), bf16[32,128,128]{2,1,0:T(8,128)(2,1)}, u32[]{:S(2)}, u32[]{:S(2)}) async-start(bf16[32,128,128]{2,1,0:T(8,128)(2,1)} %shard_map.87), calls=%async_computation.1 | async-start | bytes 2097152 | tf_op jit(solution)/shard_map/all_to_all | solution.py:162
  94.7 1.1 copy-start.1
  136.5 3.7 %collective-permute-start.7 = (bf16[15,128]{1,0:T(8,128)(2,1)S(1)}, bf16[15,128]{1,0:T(8,128)(2,1)S(1)}, u32[]{:S(2)}, u32[]{:S(2)}) collective-permute-start(bf16[15,128]{1,0:T(8,128)(2,1)S(1)} %slice.21), channel_id=1, source_target_pairs={{0,1},{1,2},{2,3},{3,4},{4,5},{5,6},{6,7},{7,8},{8,9},{9,10},{10,1... | collective-permute-start | bytes 11528

commit v3 on v2

--- a/solution.py
+++ b/solution.py
@@ -3,6 +3,7 @@
 from jax import lax
 from jax.experimental import pallas as pl
 from jax.experimental.pallas import tpu as pltpu
+from jax.sharding import Mesh
 from jax.sharding import PartitionSpec as P
 
 root_two_pi = 0.7978845608028654
@@ -12,11 +13,7 @@
 BLK = 64
 NT = (((1,), (1,)), ((), ()))
 TN = (((0,), (0,)), ((), ()))
-SEEDS = (0, 5, -5)
-ABOVE1 = (1, 6, -4)
-BELOW1 = (-1, 4, -6)
-ABOVE2 = (2, 7, -3)
-BELOW2 = (-2, 3, -7)
+COL = ("half", "side")
 
 
 def dot(a, b, dims=(((1,), (0,)), ((), ()))):
@@ -30,12 +27,11 @@
 
 
 def forward_kernel(
-    ids, weights, s0, a1, b1, a2, b2, e8, upstream, hidden, grad, whole, pre
+    ids, weights, same, other_low, other_high, upstream, hidden, grad, whole, pre
 ):
-    for piece, offsets in ((s0, SEEDS), (a1, ABOVE1), (b1, BELOW1), (a2, ABOVE2), (b2, BELOW2), (e8, (8,))):
-        for k, offset in enumerate(offsets):
-            at = offset % 16 * 6
-            whole[at : at + 6] = piece[k].reshape(6, BLK, 128)
+    whole[:48] = same[...].reshape(48, BLK, 128)
+    whole[48:72] = other_low[...].reshape(24, BLK, 128)
+    whole[72:] = other_high[...].reshape(24, BLK, 128)
     pre[...] = jnp.zeros_like(pre)
 
     def some_slots(g, carry):
@@ -124,14 +120,11 @@
 
 
 def on_device(tokens, weight_blocks, block_rows, block_columns, panel_counts, hidden_grad):
-    n_col, n_row = lax.axis_size("col"), lax.axis_size("row")
-    me_col, me_row = lax.axis_index("col"), lax.axis_index("row")
+    n_row, n_col = lax.axis_size("row"), lax.axis_size(COL)
+    me_row, me_col, me_side = lax.axis_index("row"), lax.axis_index(COL), lax.axis_index("side")
 
     def shift(a, by):
-        return lax.ppermute(a, "col", [(i, (i + by) % n_col) for i in range(n_col)])
-
-    mine = tokens.T
-    far = jnp.stack([mine, shift(mine, -5), shift(mine, 5)])
+        return lax.ppermute(a, COL, [(i, (i + by) % n_col) for i in range(n_col)])
 
     slot = me_row * 4 + jnp.arange(4, dtype=jnp.int32)
     live = slot < panel_counts[0]
@@ -142,21 +135,22 @@
     parcel = jnp.broadcast_to(jnp.concatenate([blocks, named])[None], (n_row, 144, 128))
     parcels = lax.all_to_all(parcel, "row", 0, 0, tiled=True)
     ids = parcels[:, 128, :8].astype(jnp.int32)
-    rows = (ids[:, :4] + (96 - 6 * me_col)) % 96
+    owner = ids[:, :4] // 6
+    rows = jnp.where(owner % 2 == me_side, 0, 48) + owner // 2 * 6 + ids[:, :4] % 6
     ids = jnp.concatenate([rows, ids[:, 4:], ids[:, :4]], axis=1)
 
-    above1, below1 = shift(far, -1), shift(far, 1)
-    above2, below2 = shift(above1, -1), shift(below1, 1)
-    eight = shift(above1[1:2], -2)
+    same = lax.all_gather(tokens.T, "half", axis=0, tiled=True)
+    middle = same.shape[0] // 2
+    other_low, other_high = shift(same[:middle], 1), shift(same[middle:], -1)
 
     hidden, grad, whole = call(
         forward_kernel,
         (shape(128, 3072), shape(48, BLK, 128), shape(96, BLK, 128)),
-        9,
+        6,
         [pltpu.VMEM((48, BLK, 128), F32)],
         400_000_000,
         24,
-    )(ids, parcels, far, above1, below1, above2, below2, eight, hidden_grad)
+    )(ids, parcels, same, other_low, other_high, hidden_grad)
 
     terms = call(weight_kernel, shape(n_row, 128, 128), 3, [], 300_000_000, 16)(ids, whole, grad)
     back = lax.all_to_all(terms, "row", 0, 0, tiled=True)
@@ -164,7 +158,7 @@
     part = call(
         input_kernel, shape(6384, 128), 3, [pltpu.VMEM((96, BLK, 128), F32)], 300_000_000, 24
     )(ids, parcels, grad)
-    own = lax.optimization_barrier(lax.psum_scatter(part, "col", scatter_dimension=0, tiled=True))
+    own = lax.optimization_barrier(lax.psum_scatter(part, COL, scatter_dimension=0, tiled=True))
     input_grad = lax.dynamic_slice_in_dim(own, me_col, 384, 0).T
 
     sums = jnp.sum(back.astype(F32), axis=0).astype(BF)
@@ -174,18 +168,20 @@
 
 
 def solution(mesh):
+    n_row, n_col = mesh.devices.shape
+    fine = Mesh(mesh.devices.reshape(n_row, n_col // 2, 2), ("row", *COL))
     placed = (
-        P("row", "col"),
-        P("col", "row", None),
-        P("col", "row"),
-        P("col", "row"),
-        P("col"),
-        P("row", "col"),
+        P("row", COL),
+        P(COL, "row", None),
+        P(COL, "row"),
+        P(COL, "row"),
+        P(COL),
+        P("row", COL),
     )
     return jax.shard_map(
         on_device,
-        mesh=mesh,
+        mesh=fine,
         in_specs=placed,
-        out_specs=(P("row", "col"), P("row", "col"), P("col", "row", None)),
+        out_specs=(P("row", COL), P("row", COL), P(COL, "row", None)),
         check_vma=False,
     )

time: 145 us -> 140 us (0.966)
  blocking collectives: 37.3 us -> 74.8 us
  waiting for transfers between devices: 27.1 us -> 5.87 us
  starting transfers between devices: 48.5 us -> 27.3 us
    all_gather x0 -> x1, blocking collectives: none -> 36.9 us  [on_device(): same = lax.all_gather(tokens.T, 'half', axis=0, tiled=True)]
    ppermute x7 -> x2, starting transfers between devices: 29.6 us -> 7.04 us  [shift(): return lax.ppermute(a, COL, [(i, (i + by) % n_col) for i in range(n_col)])]
    ppermute x7 -> x2, waiting for transfers between devices: 27.1 us -> 5.86 us  [shift(): return lax.ppermute(a, COL, [(i, (i + by) % n_col) for i in range(n_col)])]
  transfers between devices with their start and end apart: 10 -> 5, of which waited for: 5 -> 2; matrix products, arithmetic and copies ran while one was open for 28% -> 30% of each run, Pallas kernels for 2% -> 2%
where the time goes in v3:
time: 140 us; the launch traced here: 139 us
  blocking collectives  74.8 us (53%)
  starting transfers between devices  27.3 us (20%)
  Pallas kernels  17.3 us (12%)
  local copies, waits for them, and re-layouts  8.25 us (6%)
  waiting for transfers between devices  5.87 us (4%)
  other arithmetic  3.75 us (3%)
  between operations  2.13 us (2%)
    unnamed x1, blocking collectives  37.9 us
    all_gather x1, blocking collectives, on_device(): same = lax.all_gather(tokens.T, 'half', axis=0, tiled=True)  36.9 us
    pallas_call x1, Pallas kernels, on_device(): call(forward_kernel, (shape(128, 3072), shape(48, BLK, 128), shape(96, BL...  9.49 us
    all_to_all x1, starting transfers between devices, on_device(): parcels = lax.all_to_all(parcel, 'row', 0, 0, tiled=True)  9.48 us
    all_to_all x1, starting transfers between devices, on_device(): back = lax.all_to_all(terms, 'row', 0, 0, tiled=True)  8.13 us
    ppermute x2, starting transfers between devices, shift(): return lax.ppermute(a, COL, [(i, (i + by) % n_col) for i in range(n_col)])  7.04 us
    ppermute x2, waiting for transfers between devices, shift(): return lax.ppermute(a, COL, [(i, (i + by) % n_col) for i in range(n_col)])  5.86 us
    unnamed x14, local copies, waits for them, and re-layouts  4.81 us
  transfers between devices with their start and end apart: 5, of which 2 were waited for; matrix products, arithmetic and copies ran while one was open for 30% of the time, Pallas kernels for 2%

profile of v3, /device:TPU:6, one launch (start us, length us, event | category | flops | bytes accessed | tf_op | source)
XLA Modules:
  0.0 139.4 jit_solution(11059917901981080534)
XLA Ops:
  1.3 0.9 reshape_squeeze.3
  2.4 0.7 convert.8
  3.1 0.7 convert.9
  3.8 1.2 broadcast_in_dim.42
  5.0 9.5 %all-to-all-start = ((bf16[32,144,128]{2,1,0:T(8,128)(2,1)}), bf16[32,144,128]{2,1,0:T(8,128)(2,1)S(1)}, u32[]{:S(2)}, u32[]{:S(2)}) async-start(bf16[32,144,128]{2,1,0:T(8,128)(2,1)} %broadcast_in_dim.42), calls=%async_computation | async-start | bytes 2359296 | tf_op jit(solution)/shard_map/all_to_all | solution.py:136
  14.7 36.9 %all_gather.3.same = bf16[3072,128]{1,0:T(8,128)(2,1)S(1)} all-gather(bf16[384,128]{1,0:T(8,128)(2,1)S(1)} %bitcast.19), channel_id=1, replica_groups=mesh['row'=32,'half'=8,'side'=2] {'half'}, dimensions={0}, use_global_device_ids=true | all-gather | bytes 884736 | tf_op jit(solution)/shard_map/all_gather | solution.py:142
  51.5 0.9 fusion.15
  52.5 3.2 %collective-permute-start = (bf16[1536,128]{1,0:T(8,128)(2,1)}, bf16[1536,128]{1,0:T(8,128)(2,1)S(1)}, u32[]{:S(2)}, u32[]{:S(2)}) collective-permute-start(bf16[1536,128]{1,0:T(8,128)(2,1)} %get-tuple-element.22), channel_id=1, source_target_pairs={{0,1},{1,2},{2,3},{3,4},{4,5},{5,6},{6,7},{7,8},{8,9},{9,10},{10,1... | collective-permute-start | bytes 1179656 | tf_op jit(solution)/shard_map/ppermute | solution.py:127
  55.7 3.8 %collective-permute-start.1 = (bf16[1536,128]{1,0:T(8,128)(2,1)}, bf16[1536,128]{1,0:T(8,128)(2,1)S(1)}, u32[]{:S(2)}, u32[]{:S(2)}) collective-permute-start(bf16[1536,128]{1,0:T(8,128)(2,1)} %get-tuple-element.21), channel_id=1, source_target_pairs={{0,15},{1,0},{2,1},{3,2},{4,3},{5,4},{6,5},{7,6},{8,7},{9,8},{10,9... | collective-permute-start | bytes 1179656 | tf_op jit(solution)/shard_map/ppermute | solution.py:127
  59.7 3.8 %collective-permute-done.other_low = bf16[1536,128]{1,0:T(8,128)(2,1)S(1)} collective-permute-done((bf16[1536,128]{1,0:T(8,128)(2,1)}, bf16[1536,128]{1,0:T(8,128)(2,1)S(1)}, u32[]{:S(2)}, u32[]{:S(2)}) %collective-permute-start) | collective-permute-done | bytes 393248 | tf_op jit(solution)/shard_map/ppermute | solution.py:127
  63.5 2.0 %collective-permute-done.1.other_high = bf16[1536,128]{1,0:T(8,128)(2,1)S(1)} collective-permute-done((bf16[1536,128]{1,0:T(8,128)(2,1)}, bf16[1536,128]{1,0:T(8,128)(2,1)S(1)}, u32[]{:S(2)}, u32[]{:S(2)}) %collective-permute-start.1) | collective-permute-done | bytes 393248 | tf_op jit(solution)/shard_map/ppermute | solution.py:127
  65.6 9.5 %shard_map.85 = (bf16[128,3072]{1,0:T(8,128)(2,1)}, bf16[48,64,128]{2,1,0:T(8,128)(2,1)S(1)}, bf16[96,64,128]{2,1,0:T(8,128)(2,1)S(1)}) custom-call(s32[32,12]{1,0:T(8,128)S(1)} %pad_add_fusion.ids, bf16[32,144,128]{2,1,0:T(8,128)(2,1)S(1)} %all-to-all-done.weights, bf16[3072,128]{1,0:T(8,128)(2,1)S(1)} %all_gather.3.same, ...), custom_call_target="tpu_custom_call" | custom-call | flops 400000000 | bytes 6291456 | tf_op jit(solution)/shard_map/pallas_call | solution.py:146
  75.1 4.4 %shard_map.87 = bf16[32,128,128]{2,1,0:T(8,128)(2,1)} custom-call(s32[32,12]{1,0:T(8,128)S(1)} %pad_add_fusion.ids, bf16[96,64,128]{2,1,0:T(8,128)(2,1)S(1)} %get-tuple-element.8.whole, bf16[48,64,128]{2,1,0:T(8,128)(2,1)S(1)} %get-tuple-element.7.grad), custom_call_target="tpu_custom_call" | custom-call | flops 300000000 | bytes 6291456 | tf_op jit(solution)/shard_map/pallas_call | solution.py:155
  79.5 0.9 copy-done
  80.4 8.1 %all-to-all-start.1 = ((bf16[32,128,128]{2,1,0:T(8,128)(2,1)}), bf16[32,128,128]{2,1,0:T(8,128)(2,1)}, u32[]{:S(2)}, u32[]{:S(2)}) async-start(bf16[32,128,128]{2,1,0:T(8,128)(2,1)} %shard_map.87), calls=%async_computation.1 | async-start | bytes 2097152 | tf_op jit(solution)/shard_map/all_to_all | solution.py:156
  88.5 1.1 copy-done.1
  89.6 3.3 %shard_map.86 = bf16[6384,128]{1,0:T(8,128)(2,1)S(1)} custom-call(s32[32,12]{1,0:T(8,128)S(1)} %pad_add_fusion.ids, bf16[32,144,128]{2,1,0:T(8,128)(2,1)S(1)} %all-to-all-done.weights, bf16[48,64,128]{2,1,0:T(8,128)(2,1)S(1)} %copy-done.1), custom_call_target="tpu_custom_call" | custom-call | flops 300000000 | bytes 6291456 | tf_op jit(solution)/shard_map/pallas_call | solution.py:158
  93.0 37.9 %fusion = bf16[400,128]{1,0:T(8,128)(2,1)S(1)} fusion(bf16[6384,128]{1,0:T(8,128)(2,1)S(1)} %shard_map.86), kind=kCustom, calls=%all-reduce-scatter | all-reduce-scatter fusion | flops 819201 | bytes 1738752
  130.9 2.7 %collective-permute-start.2 = (bf16[15,128]{1,0:T(8,128)(2,1)S(1)}, bf16[15,128]{1,0:T(8,128)(2,1)S(1)}, u32[]{:S(2)}, u32[]{:S(2)}) collective-permute-start(bf16[15,128]{1,0:T(8,128)(2,1)S(1)} %slice.27), channel_id=1, source_target_pairs={{0,1},{1,2},{2,3},{3,4},{4,5},{5,6},{6,7},{7,8},{8,9},{9,10},{10,1... | collective-permute-start | bytes 11528
  133.7 1.3 dynamic-slice.4
  135.6 0.6 concatenate.20
  136.3 0.8 copy.29
  137.1 1.4 reduce_sum.12
  138.7 0.7 broadcast_select_fusion
  (27 shorter events, 1.0 us)
Async XLA Ops:
  3.8 10.7 %copy-start.3 = (bf16[128,384]{1,0:T(8,128)(2,1)S(1)}, bf16[128,384]{1,0:T(8,128)(2,1)}, u32[]{:S(2)}) copy-start(bf16[128,384]{1,0:T(8,128)(2,1)} %param.6) | copy-start | bytes 294916
  5.0 54.5 %all-to-all-start = ((bf16[32,144,128]{2,1,0:T(8,128)(2,1)}), bf16[32,144,128]{2,1,0:T(8,128)(2,1)S(1)}, u32[]{:S(2)}, u32[]{:S(2)}) async-start(bf16[32,144,128]{2,1,0:T(8,128)(2,1)} %broadcast_in_dim.42), calls=%async_computation | async-start | bytes 2359296 | tf_op jit(solution)/shard_map/all_to_all | solution.py:136
  14.5 51.1 %copy-start.2 = (bf16[128,3072]{1,0:T(8,128)(2,1)S(1)}, bf16[128,3072]{1,0:T(8,128)(2,1)}, u32[]{:S(2)}) copy-start(bf16[128,3072]{1,0:T(8,128)(2,1)} %upstream.1) | copy-start | bytes 2359300
  52.5 11.1 %collective-permute-start = (bf16[1536,128]{1,0:T(8,128)(2,1)}, bf16[1536,128]{1,0:T(8,128)(2,1)S(1)}, u32[]{:S(2)}, u32[]{:S(2)}) collective-permute-start(bf16[1536,128]{1,0:T(8,128)(2,1)} %get-tuple-element.22), channel_id=1, source_target_pairs={{0,1},{1,2},{2,3},{3,4},{4,5},{5,6},{6,7},{7,8},{8,9},{9,10},{10,1... | collective-permute-start | bytes 1179656 | tf_op jit(solution)/shard_map/ppermute | solution.py:127
  55.7 9.9 %collective-permute-start.1 = (bf16[1536,128]{1,0:T(8,128)(2,1)}, bf16[1536,128]{1,0:T(8,128)(2,1)S(1)}, u32[]{:S(2)}, u32[]{:S(2)}) collective-permute-start(bf16[1536,128]{1,0:T(8,128)(2,1)} %get-tuple-element.21), channel_id=1, source_target_pairs={{0,15},{1,0},{2,1},{3,2},{4,3},{5,4},{6,5},{7,6},{8,7},{9,8},{10,9... | collective-permute-start | bytes 1179656 | tf_op jit(solution)/shard_map/ppermute | solution.py:127
  79.5 0.9 copy-start
  80.4 56.7 %all-to-all-start.1 = ((bf16[32,128,128]{2,1,0:T(8,128)(2,1)}), bf16[32,128,128]{2,1,0:T(8,128)(2,1)}, u32[]{:S(2)}, u32[]{:S(2)}) async-start(bf16[32,128,128]{2,1,0:T(8,128)(2,1)} %shard_map.87), calls=%async_computation.1 | async-start | bytes 2097152 | tf_op jit(solution)/shard_map/all_to_all | solution.py:156
  88.5 1.1 copy-start.1
  130.9 4.6 %collective-permute-start.2 = (bf16[15,128]{1,0:T(8,128)(2,1)S(1)}, bf16[15,128]{1,0:T(8,128)(2,1)S(1)}, u32[]{:S(2)}, u32[]{:S(2)}) collective-permute-start(bf16[15,128]{1,0:T(8,128)(2,1)S(1)} %slice.27), channel_id=1, source_target_pairs={{0,1},{1,2},{2,3},{3,4},{4,5},{5,6},{6,7},{7,8},{8,9},{9,10},{10,1... | collective-permute-start | bytes 11528

commit v4 on v3

v4 whole, which is shorter than its diff:
```python
import jax
import jax.numpy as jnp
from jax import lax
from jax.experimental import pallas as pl
from jax.experimental.pallas import tpu as pltpu
from jax.sharding import Mesh
from jax.sharding import PartitionSpec as P

root_two_pi = 0.7978845608028654
cubic_term = 0.044715
BF = jnp.bfloat16
F32 = jnp.float32
BLK = 64
NN = (((1,), (0,)), ((), ()))
NT = (((1,), (1,)), ((), ()))
TN = (((0,), (0,)), ((), ()))
COL = ("half", "side")
SM = pl.BlockSpec(memory_space=pltpu.SMEM)
VM = pl.BlockSpec(memory_space=pltpu.VMEM)
MIB = 1 << 20


def dot(a, b, dims=NN):
    return lax.dot_general(a, b, dims, preferred_element_type=F32)


def picker(parted):
    i = lax.broadcasted_iota(jnp.int32, (128, 128), 0)
    j = lax.broadcasted_iota(jnp.int32, (128, 128), 1)
    place = i // 64 * 64 + i % 32 * 2 + i % 64 // 32
    return ((place if parted else i) == j).astype(BF)


def prep_kernel(rows, columns, count, first, blocks, tokens, parcels, turned, spread):
    for i in range(32):
        spread[pl.ds(i, 4, stride=32), :] = blocks[0, :, i * 128 : (i + 1) * 128].astype(F32)
    slot = first[0] + lax.broadcasted_iota(jnp.int32, (128, 128), 0) // 32
    parcels[0, :128] = jnp.where(slot < count[0], spread[...], 0.0).astype(BF)
    lane = lax.broadcasted_iota(jnp.int32, (16, 128), 1)
    named = jnp.zeros((16, 128), jnp.int32)
    for j in range(4):
        named = jnp.where(lane == j, rows[0, j], named)
        named = jnp.where(lane == 4 + j, columns[0, j], named)
    parcels[0, 128:] = named.astype(F32).astype(BF)

    def again(d, carry):
        parcels[d] = parcels[0]
        return carry

    lax.fori_loop(1, parcels.shape[0], again, 0)
    parted = picker(True)
    for k in range(3):
        at = k * 128
        turned[at : at + 128] = dot(parted, tokens[:, at : at + 128], NT).astype(BF)


def main_kernel(
    ids, weights, same, other_low, other_high, upstream, hidden, part, terms, whole, pre, grad, total
):
    whole[:48] = same[...].reshape(48, BLK, 128)
    whole[48:72] = other_low[...].reshape(24, BLK, 128)
    whole[72:] = other_high[...].reshape(24, BLK, 128)
    pre[...] = jnp.zeros_like(pre)
    total[...] = jnp.zeros_like(total)

    def slots(visit):
        def some(g, carry):
            for q in range(8):
                for j in range(4):
                    visit(g * 8 + q, j)
            return carry

        lax.fori_loop(0, 4, some, 0)

    def block(d, j):
        lines = weights[d, j * 32 : (j + 1) * 32]
        return jnp.concatenate([lines[:, :BLK], lines[:, BLK:]], axis=0)

    def forward(d, j):
        pre[ids[d, 4 + j]] += dot(block(d, j), whole[ids[d, j]], TN)

    slots(forward)
    unit = picker(False)

    def some_columns(g, carry):
        at = pl.multiple_of(g * 128, 128)
        v = pre[pl.ds(g * 2, 2)].reshape(128, 128)
        tangent = jnp.tanh(root_two_pi * (v + cubic_term * v * v * v))
        value = 0.5 * v * (1.0 + tangent)
        slope = 0.5 * (1.0 + tangent) + 0.5 * v * (1.0 - tangent * tangent) * root_two_pi * (
            1.0 + 3.0 * cubic_term * v * v
        )
        turned = dot(unit, upstream[:, pl.ds(at, 128)], NT)
        grad[pl.ds(g * 2, 2)] = (turned * slope).astype(BF).reshape(2, BLK, 128)
        hidden[:, pl.ds(at, 128)] = dot(unit, value.astype(BF), NT).astype(BF)
        return carry

    lax.fori_loop(0, 24, some_columns, 0, unroll=4)

    def weight(d, j):
        product = dot(whole[ids[d, j]], grad[ids[d, 4 + j]], NT).astype(BF)
        terms[d, j * 32 : (j + 1) * 32] = jnp.concatenate([product[:32], product[32:]], axis=1)

    slots(weight)

    def backward(d, j):
        total[ids[d, 8 + j]] += dot(block(d, j), grad[ids[d, 4 + j]])

    slots(backward)
    for o in range(16):
        part[400 * o : 400 * o + 384] = total[6 * o : 6 * o + 6].reshape(384, 128).astype(BF)
        if o < 15:
            part[400 * o + 384 : 400 * o + 400] = jnp.zeros((16, 128), BF)


def weight_end_kernel(count, first, terms, out, total):
    def some(d, kept):
        return kept + terms[d].astype(F32)

    kept = lax.fori_loop(1, terms.shape[0], some, terms[0].astype(F32))
    slot = first[0] + lax.broadcasted_iota(jnp.int32, (128, 128), 0) // 32
    total[...] = jnp.where(slot < count[0], kept, 0.0)
    for i in range(32):
        out[0, :, i * 128 : (i + 1) * 128] = total[pl.ds(i, 4, stride=32), :].astype(BF)


def input_end_kernel(own, out):
    parted = picker(True)
    for k in range(3):
        at = k * 128
        out[:, at : at + 128] = dot(own[at : at + 128], parted, TN).astype(BF)


def shape(*dims):
    return jax.ShapeDtypeStruct(dims, BF)


def call(kernel, outs, n_scalar, n_array, scratch, flops, limit):
    return pl.pallas_call(
        kernel,
        out_shape=outs,
        in_specs=[SM] * n_scalar + [VM] * n_array,
        out_specs=jax.tree.map(lambda _: VM, outs),
        scratch_shapes=scratch,
        compiler_params=pltpu.CompilerParams(vmem_limit_bytes=limit * MIB),
        cost_estimate=pl.CostEstimate(flops=flops, bytes_accessed=2 * MIB, transcendentals=0),
    )


def on_device(tokens, weight_blocks, block_rows, block_columns, panel_counts, hidden_grad):
    n_row, n_col = lax.axis_size("row"), lax.axis_size(COL)
    me_row, me_col, me_side = lax.axis_index("row"), lax.axis_index(COL), lax.axis_index("side")
    first = (me_row * 4).reshape(1)

    def shift(a, by):
        return lax.ppermute(a, COL, [(i, (i + by) % n_col) for i in range(n_col)])

    parcels, turned = call(
        prep_kernel,
        (shape(n_row, 144, 128), shape(384, 128)),
        4,
        2,
        [pltpu.VMEM((128, 128), F32)],
        10_000_000,
        8,
    )(block_rows, block_columns, panel_counts, first, weight_blocks, tokens)
    parcels = lax.all_to_all(parcels, "row", 0, 0, tiled=True)
    ids = parcels[:, 128, :8].astype(jnp.int32)
    owner = ids[:, :4] // 6
    rows = jnp.where(owner % 2 == me_side, 0, 48) + owner // 2 * 6 + ids[:, :4] % 6
    ids = jnp.concatenate([rows, ids[:, 4:], ids[:, :4]], axis=1)

    same = lax.all_gather(turned, "half", axis=0, tiled=True)
    middle = same.shape[0] // 2
    other_low, other_high = shift(same[:middle], 1), shift(same[middle:], -1)

    hidden, part, terms = call(
        main_kernel,
        (shape(128, 3072), shape(6384, 128), shape(n_row, 128, 128)),
        1,
        5,
        [
            pltpu.VMEM((96, BLK, 128), BF),
            pltpu.VMEM((48, BLK, 128), F32),
            pltpu.VMEM((48, BLK, 128), BF),
            pltpu.VMEM((96, BLK, 128), F32),
        ],
        1_000_000_000,
        24,
    )(ids, parcels, same, other_low, other_high, hidden_grad)

    terms = lax.all_to_all(terms, "row", 0, 0, tiled=True)
    own = lax.optimization_barrier(lax.psum_scatter(part, COL, scatter_dimension=0, tiled=True))
    own = lax.dynamic_slice_in_dim(own, me_col, 384, 0)
    input_grad = call(input_end_kernel, shape(128, 384), 0, 1, [], 10_000_000, 4)(own)
    weight_grad = call(
        weight_end_kernel,
        shape(1, 4, 4096),
        2,
        1,
        [pltpu.VMEM((128, 128), F32)],
        500_000_000,
        4,
    )(panel_counts, first, terms)
    return hidden, input_grad, weight_grad


def solution(mesh):
    n_row, n_col = mesh.devices.shape
    fine = Mesh(mesh.devices.reshape(n_row, n_col // 2, 2), ("row", *COL))
    placed = (
        P("row", COL),
        P(COL, "row", None),
        P(COL, "row"),
        P(COL, "row"),
        P(COL),
        P("row", COL),
    )
    return jax.shard_map(
        on_device,
        mesh=fine,
        in_specs=placed,
        out_specs=(P("row", COL), P("row", COL), P(COL, "row", None)),
        check_vma=False,
    )
```

time: 140 us -> 134 us (0.957)
  other arithmetic: 3.75 us -> 0.17 us
  Pallas kernels: 17.3 us -> 15 us
  local copies, waits for them, and re-layouts: 8.25 us -> 9.9 us
  waiting for transfers between devices: 5.87 us -> 4.45 us
    unnamed x14 -> x22, local copies, waits for them, and re-layouts: 4.81 us -> 8.93 us
    pallas_call x3 -> x4, Pallas kernels: 17.3 us -> 15 us  [the longest x1 11.1 us: on_device(): call(main_kernel, (shape(128, 3072), shape(6384, 128), shape(n_row, 128,...]
    ppermute x2, waiting for transfers between devices: 5.86 us -> 4.44 us  [shift(): return lax.ppermute(a, COL, [(i, (i + by) % n_col) for i in range(n_col)])]
  transfers between devices with their start and end apart: 5 -> 5, of which waited for: 2 -> 2; matrix products, arithmetic and copies ran while one was open for 30% -> 31% of each run, Pallas kernels for 2% -> 1%
where the time goes in v4:
time: 134 us
  blocking collectives  74.9 us (56%)
  starting transfers between devices  27.1 us (20%)
  Pallas kernels  15 us (11%)
  local copies, waits for them, and re-layouts  9.9 us (7%)
  waiting for transfers between devices  4.45 us (3%)
  between operations  2.08 us (2%)
    unnamed x1, blocking collectives  38 us
    all_gather x1, blocking collectives, on_device(): same = lax.all_gather(turned, 'half', axis=0, tiled=True)  36.9 us
    pallas_call x1, Pallas kernels, on_device(): call(main_kernel, (shape(128, 3072), shape(6384, 128), shape(n_row, 128,...  11.1 us
    all_to_all x1, starting transfers between devices, on_device(): parcels = lax.all_to_all(parcels, 'row', 0, 0, tiled=True)  9.48 us
    unnamed x22, local copies, waits for them, and re-layouts  8.93 us
    all_to_all x1, starting transfers between devices, on_device(): terms = lax.all_to_all(terms, 'row', 0, 0, tiled=True)  7.71 us
    ppermute x2, starting transfers between devices, shift(): return lax.ppermute(a, COL, [(i, (i + by) % n_col) for i in range(n_col)])  7.04 us
    ppermute x2, waiting for transfers between devices, shift(): return lax.ppermute(a, COL, [(i, (i + by) % n_col) for i in range(n_col)])  4.44 us
  transfers between devices with their start and end apart: 5, of which 2 were waited for; matrix products, arithmetic and copies ran while one was open for 31% of the time, Pallas kernels for 1%

profile of v4, /device:TPU:6, one launch (start us, length us, event | category | flops | bytes accessed | tf_op | source)
XLA Modules:
  0.0 133.5 jit_solution(7370630081535887759)
XLA Ops:
  1.3 0.9 copy-done.2
  2.2 0.8 copy-done.3
  2.9 0.7 copy-done.4
  3.6 0.7 copy-done.5
  4.2 2.1 %shard_map.85 = (bf16[32,144,128]{2,1,0:T(8,128)(2,1)}, bf16[384,128]{1,0:T(8,128)(2,1)S(1)}) custom-call(s32[1,4]{1,0:T(1,128)S(1)} %copy-done.4, s32[1,4]{1,0:T(1,128)S(1)} %copy-done.5, s32[1]{0:T(128)S(6)} %copy.9.count, s32[1]{0:T(128)} %bitcast.first, bf16[1,4,4096]{2,1,0:T(4,128)(2,1)S(1)} %copy-done.3, bf16[128,384]{1,0:T(8,128)(2,1)S(1)} %copy-done.2), custom_call_target="tpu_custom_call" | custom-call | flops 10000000 | bytes 2097152 | tf_op jit(solution)/shard_map/pallas_call | solution.py:158
  6.3 9.5 %all-to-all-start = ((bf16[32,144,128]{2,1,0:T(8,128)(2,1)}), bf16[32,144,128]{2,1,0:T(8,128)(2,1)S(1)}, u32[]{:S(2)}, u32[]{:S(2)}) async-start(bf16[32,144,128]{2,1,0:T(8,128)(2,1)} %get-tuple-element.8), calls=%async_computation | async-start | bytes 2359296 | tf_op jit(solution)/shard_map/all_to_all | solution.py:167
  15.8 36.9 %all_gather.3.same = bf16[3072,128]{1,0:T(8,128)(2,1)S(1)} all-gather(bf16[384,128]{1,0:T(8,128)(2,1)S(1)} %get-tuple-element.9), channel_id=1, replica_groups=mesh['row'=32,'half'=8,'side'=2] {'half'}, dimensions={0}, use_global_device_ids=true | all-gather | bytes 884736 | tf_op jit(solution)/shard_map/all_gather | solution.py:173
  52.7 0.9 fusion.8
  53.6 3.5 %collective-permute-start = (bf16[1536,128]{1,0:T(8,128)(2,1)}, bf16[1536,128]{1,0:T(8,128)(2,1)S(1)}, u32[]{:S(2)}, u32[]{:S(2)}) collective-permute-start(bf16[1536,128]{1,0:T(8,128)(2,1)} %get-tuple-element.14), channel_id=1, source_target_pairs={{0,1},{1,2},{2,3},{3,4},{4,5},{5,6},{6,7},{7,8},{8,9},{9,10},{10,1... | collective-permute-start | bytes 1179656 | tf_op jit(solution)/shard_map/ppermute | solution.py:156
  57.1 3.6 %collective-permute-start.1 = (bf16[1536,128]{1,0:T(8,128)(2,1)}, bf16[1536,128]{1,0:T(8,128)(2,1)}, u32[]{:S(2)}, u32[]{:S(2)}) collective-permute-start(bf16[1536,128]{1,0:T(8,128)(2,1)} %get-tuple-element.13), channel_id=1, source_target_pairs={{0,15},{1,0},{2,1},{3,2},{4,3},{5,4},{6,5},{7,6},{8,7},{9,8},{10,9... | collective-permute-start | bytes 1179656 | tf_op jit(solution)/shard_map/ppermute | solution.py:156
  60.7 1.0 copy-done
  61.9 2.8 %collective-permute-done.other_low = bf16[1536,128]{1,0:T(8,128)(2,1)S(1)} collective-permute-done((bf16[1536,128]{1,0:T(8,128)(2,1)}, bf16[1536,128]{1,0:T(8,128)(2,1)S(1)}, u32[]{:S(2)}, u32[]{:S(2)}) %collective-permute-start) | collective-permute-done | bytes 393248 | tf_op jit(solution)/shard_map/ppermute | solution.py:156
  64.7 0.7 copy-done.7
  65.4 1.7 %collective-permute-done.1.other_high = bf16[1536,128]{1,0:T(8,128)(2,1)} collective-permute-done((bf16[1536,128]{1,0:T(8,128)(2,1)}, bf16[1536,128]{1,0:T(8,128)(2,1)}, u32[]{:S(2)}, u32[]{:S(2)}) %collective-permute-start.1) | collective-permute-done | bytes 393248 | tf_op jit(solution)/shard_map/ppermute | solution.py:156
  67.1 1.3 copy-done.1
  68.4 1.0 copy-done.8
  69.4 11.1 %shard_map.86 = (bf16[128,3072]{1,0:T(8,128)(2,1)}, bf16[6384,128]{1,0:T(8,128)(2,1)S(1)}, bf16[32,128,128]{2,1,0:T(8,128)(2,1)}) custom-call(s32[32,12]{1,0:T(8,128)S(1)} %pad_add_fusion.ids, bf16[32,144,128]{2,1,0:T(8,128)(2,1)S(1)} %copy-done.1, bf16[3072,128]{1,0:T(8,128)(2,1)S(1)} %all_gather.3.same, bf16[1536,128]{1,0:T(8,128)(2,1)S(1)} %copy-done.8, ...), custom_call_target="tpu_custom_call" | custom-call | flops 1000000000 | bytes 2097152 | tf_op jit(solution)/shard_map/pallas_call | solution.py:177
  80.4 7.7 %all-to-all-start.1 = ((bf16[32,128,128]{2,1,0:T(8,128)(2,1)}), bf16[32,128,128]{2,1,0:T(8,128)(2,1)S(1)}, u32[]{:S(2)}, u32[]{:S(2)}) async-start(bf16[32,128,128]{2,1,0:T(8,128)(2,1)} %get-tuple-element.12), calls=%async_computation.1 | async-start | bytes 2097152 | tf_op jit(solution)/shard_map/all_to_all | solution.py:192
  88.2 38.0 %fusion = bf16[400,128]{1,0:T(8,128)(2,1)S(1)} fusion(bf16[6384,128]{1,0:T(8,128)(2,1)S(1)} %get-tuple-element.11), kind=kCustom, calls=%all-reduce-scatter | all-reduce-scatter fusion | flops 819201 | bytes 1738752
  126.2 2.8 %collective-permute-start.2 = (bf16[15,128]{1,0:T(8,128)(2,1)S(1)}, bf16[15,128]{1,0:T(8,128)(2,1)S(1)}, u32[]{:S(2)}, u32[]{:S(2)}) collective-permute-start(bf16[15,128]{1,0:T(8,128)(2,1)S(1)} %slice.27), channel_id=1, source_target_pairs={{0,1},{1,2},{2,3},{3,4},{4,5},{5,6},{6,7},{7,8},{8,9},{9,10},{10,1... | collective-permute-start | bytes 11528
  129.0 1.3 dynamic-slice.4
  130.9 0.6 concatenate.4
  131.6 0.9 shard_map.87
  132.5 1.0 shard_map.88
  (19 shorter events, 0.3 us)
Async XLA Ops:
  1.3 0.9 copy-start.2
  2.2 0.8 copy-start.3
  2.9 0.7 copy-start.4
  3.6 0.7 copy-start.5
  6.3 54.4 %all-to-all-start = ((bf16[32,144,128]{2,1,0:T(8,128)(2,1)}), bf16[32,144,128]{2,1,0:T(8,128)(2,1)S(1)}, u32[]{:S(2)}, u32[]{:S(2)}) async-start(bf16[32,144,128]{2,1,0:T(8,128)(2,1)} %get-tuple-element.8), calls=%async_computation | async-start | bytes 2359296 | tf_op jit(solution)/shard_map/all_to_all | solution.py:167
  15.8 51.3 %copy-start.6 = (bf16[128,3072]{1,0:T(8,128)(2,1)S(1)}, bf16[128,3072]{1,0:T(8,128)(2,1)}, u32[]{:S(2)}) copy-start(bf16[128,3072]{1,0:T(8,128)(2,1)} %upstream.1) | copy-start | bytes 2359300
  53.6 11.1 %collective-permute-start = (bf16[1536,128]{1,0:T(8,128)(2,1)}, bf16[1536,128]{1,0:T(8,128)(2,1)S(1)}, u32[]{:S(2)}, u32[]{:S(2)}) collective-permute-start(bf16[1536,128]{1,0:T(8,128)(2,1)} %get-tuple-element.14), channel_id=1, source_target_pairs={{0,1},{1,2},{2,3},{3,4},{4,5},{5,6},{6,7},{7,8},{8,9},{9,10},{10,1... | collective-permute-start | bytes 1179656 | tf_op jit(solution)/shard_map/ppermute | solution.py:156
  57.1 10.0 %collective-permute-start.1 = (bf16[1536,128]{1,0:T(8,128)(2,1)}, bf16[1536,128]{1,0:T(8,128)(2,1)}, u32[]{:S(2)}, u32[]{:S(2)}) collective-permute-start(bf16[1536,128]{1,0:T(8,128)(2,1)} %get-tuple-element.13), channel_id=1, source_target_pairs={{0,15},{1,0},{2,1},{3,2},{4,3},{5,4},{6,5},{7,6},{8,7},{9,8},{10,9... | collective-permute-start | bytes 1179656 | tf_op jit(solution)/shard_map/ppermute | solution.py:156
  60.7 1.0 copy-start
  64.7 0.7 copy-start.7
  67.1 1.3 copy-start.1
  68.4 1.0 copy-start.8
  80.4 52.1 %all-to-all-start.1 = ((bf16[32,128,128]{2,1,0:T(8,128)(2,1)}), bf16[32,128,128]{2,1,0:T(8,128)(2,1)S(1)}, u32[]{:S(2)}, u32[]{:S(2)}) async-start(bf16[32,128,128]{2,1,0:T(8,128)(2,1)} %get-tuple-element.12), calls=%async_computation.1 | async-start | bytes 2097152 | tf_op jit(solution)/shard_map/all_to_all | solution.py:192
  126.2 4.8 %collective-permute-start.2 = (bf16[15,128]{1,0:T(8,128)(2,1)S(1)}, bf16[15,128]{1,0:T(8,128)(2,1)S(1)}, u32[]{:S(2)}, u32[]{:S(2)}) collective-permute-start(bf16[15,128]{1,0:T(8,128)(2,1)S(1)} %slice.27), channel_id=1, source_target_pairs={{0,1},{1,2},{2,3},{3,4},{4,5},{5,6},{6,7},{7,8},{8,9},{9,10},{10,1... | collective-permute-start | bytes 11528

commit v5 on v4

--- a/solution.py
+++ b/solution.py
@@ -17,6 +17,7 @@
 COL = ("half", "side")
 SM = pl.BlockSpec(memory_space=pltpu.SMEM)
 VM = pl.BlockSpec(memory_space=pltpu.VMEM)
+ANY = pl.BlockSpec(memory_space=pl.ANY)
 MIB = 1 << 20
 
 
@@ -31,7 +32,20 @@
     return ((place if parted else i) == j).astype(BF)
 
 
-def prep_kernel(rows, columns, count, first, blocks, tokens, parcels, turned, spread):
+def fetch(sems, *pairs):
+    copies = [pltpu.make_async_copy(a, b, sems.at[i]) for i, (a, b) in enumerate(pairs)]
+    for copy in copies:
+        copy.start()
+    return copies
+
+
+def prep_kernel(
+    first, rows_at, columns_at, count_at, blocks_at, tokens_at, parcels, turned, rows, columns, count, blocks, tokens, spread, sems
+):
+    for copy in fetch(
+        sems, (blocks_at, blocks), (tokens_at, tokens), (rows_at, rows), (columns_at, columns), (count_at, count)
+    ):
+        copy.wait()
     for i in range(32):
         spread[pl.ds(i, 4, stride=32), :] = blocks[0, :, i * 128 : (i + 1) * 128].astype(F32)
     slot = first[0] + lax.broadcasted_iota(jnp.int32, (128, 128), 0) // 32
@@ -55,13 +69,20 @@
 
 
 def main_kernel(
-    ids, weights, same, other_low, other_high, upstream, hidden, part, terms, whole, pre, grad, total
+    ids, weights_at, same, other_low, other_high, upstream_at, hidden, part, terms, weights, whole, upstream, pre, grad, total, sems
 ):
-    whole[:48] = same[...].reshape(48, BLK, 128)
-    whole[48:72] = other_low[...].reshape(24, BLK, 128)
-    whole[72:] = other_high[...].reshape(24, BLK, 128)
+    copies = fetch(
+        sems,
+        (weights_at, weights),
+        (same, whole.at[:48]),
+        (other_low, whole.at[48:72]),
+        (other_high, whole.at[72:]),
+        (upstream_at, upstream),
+    )
     pre[...] = jnp.zeros_like(pre)
     total[...] = jnp.zeros_like(total)
+    for copy in copies[:4]:
+        copy.wait()
 
     def slots(visit):
         def some(g, carry):
@@ -80,6 +101,7 @@
         pre[ids[d, 4 + j]] += dot(block(d, j), whole[ids[d, j]], TN)
 
     slots(forward)
+    copies[4].wait()
     unit = picker(False)
 
     def some_columns(g, carry):
@@ -135,11 +157,11 @@
     return jax.ShapeDtypeStruct(dims, BF)
 
 
-def call(kernel, outs, n_scalar, n_array, scratch, flops, limit):
+def call(kernel, outs, n_scalar, n_array, scratch, flops, limit, place=VM):
     return pl.pallas_call(
         kernel,
         out_shape=outs,
-        in_specs=[SM] * n_scalar + [VM] * n_array,
+        in_specs=[SM] * n_scalar + [place] * n_array,
         out_specs=jax.tree.map(lambda _: VM, outs),
         scratch_shapes=scratch,
         compiler_params=pltpu.CompilerParams(vmem_limit_bytes=limit * MIB),
@@ -158,12 +180,21 @@
     parcels, turned = call(
         prep_kernel,
         (shape(n_row, 144, 128), shape(384, 128)),
-        4,
-        2,
-        [pltpu.VMEM((128, 128), F32)],
+        1,
+        5,
+        [
+            pltpu.SMEM((1, 4), jnp.int32),
+            pltpu.SMEM((1, 4), jnp.int32),
+            pltpu.SMEM((1,), jnp.int32),
+            pltpu.VMEM((1, 4, 4096), BF),
+            pltpu.VMEM((128, 384), BF),
+            pltpu.VMEM((128, 128), F32),
+            pltpu.SemaphoreType.DMA((5,)),
+        ],
         10_000_000,
-        8,
-    )(block_rows, block_columns, panel_counts, first, weight_blocks, tokens)
+        60,
+        ANY,
+    )(first, block_rows, block_columns, panel_counts, weight_blocks, tokens)
     parcels = lax.all_to_all(parcels, "row", 0, 0, tiled=True)
     ids = parcels[:, 128, :8].astype(jnp.int32)
     owner = ids[:, :4] // 6
@@ -180,14 +211,18 @@
         1,
         5,
         [
+            pltpu.VMEM((n_row, 144, 128), BF),
             pltpu.VMEM((96, BLK, 128), BF),
+            pltpu.VMEM((128, 3072), BF),
             pltpu.VMEM((48, BLK, 128), F32),
             pltpu.VMEM((48, BLK, 128), BF),
             pltpu.VMEM((96, BLK, 128), F32),
+            pltpu.SemaphoreType.DMA((5,)),
         ],
         1_000_000_000,
-        24,
-    )(ids, parcels, same, other_low, other_high, hidden_grad)
+        52,
+        ANY,
+    )(ids, parcels, *(a.reshape(-1, BLK, 128) for a in (same, other_low, other_high)), hidden_grad)
 
     terms = lax.all_to_all(terms, "row", 0, 0, tiled=True)
     own = lax.optimization_barrier(lax.psum_scatter(part, COL, scatter_dimension=0, tiled=True))

time: 134 us -> 130 us (0.970)
  local copies, waits for them, and re-layouts: 9.9 us -> 2.03 us
  Pallas kernels: 15 us -> 16.7 us
  waiting for transfers between devices: 4.45 us -> 6.06 us
    unnamed x22 -> x10, local copies, waits for them, and re-layouts: 8.93 us -> 1.94 us
    ppermute x2, waiting for transfers between devices: 4.44 us -> 6.06 us  [shift(): return lax.ppermute(a, COL, [(i, (i + by) % n_col) for i in range(n_col)])]
where the time goes in v5:
time: 130 us; the launch traced here: 129 us
  blocking collectives  74.4 us (57%)
  starting transfers between devices  27.6 us (21%)
  Pallas kernels  16.7 us (13%)
  waiting for transfers between devices  6.06 us (5%)
  between operations  2.11 us (2%)
  local copies, waits for them, and re-layouts  2.03 us (2%)
    unnamed x1, blocking collectives  38 us
    all_gather x1, blocking collectives, on_device(): same = lax.all_gather(turned, 'half', axis=0, tiled=True)  36.5 us
    pallas_call x1, Pallas kernels, on_device(): call(main_kernel, (shape(128, 3072), shape(6384, 128), shape(n_row, 128,...  12.4 us
    all_to_all x1, starting transfers between devices, on_device(): parcels = lax.all_to_all(parcels, 'row', 0, 0, tiled=True)  9.62 us
    all_to_all x1, starting transfers between devices, on_device(): terms = lax.all_to_all(terms, 'row', 0, 0, tiled=True)  8.17 us
    ppermute x2, starting transfers between devices, shift(): return lax.ppermute(a, COL, [(i, (i + by) % n_col) for i in range(n_col)])  7.05 us
    ppermute x2, waiting for transfers between devices, shift(): return lax.ppermute(a, COL, [(i, (i + by) % n_col) for i in range(n_col)])  6.06 us
    unnamed x1, starting transfers between devices  2.75 us
  transfers between devices with their start and end apart: 5, of which 2 were waited for; matrix products, arithmetic and copies ran while one was open for 31% of the time, Pallas kernels for 1%

profile of v5, /device:TPU:6, one launch (start us, length us, event | category | flops | bytes accessed | tf_op | source)
XLA Modules:
  0.0 129.1 jit_solution(16142681002617369531)
XLA Ops:
  1.3 2.4 %shard_map.85 = (bf16[32,144,128]{2,1,0:T(8,128)(2,1)}, bf16[384,128]{1,0:T(8,128)(2,1)}) custom-call(s32[1]{0:T(128)} %bitcast.first, s32[1,4]{1,0:T(1,128)} %rows_at.1, s32[1,4]{1,0:T(1,128)} %columns_at.1, s32[1]{0:T(128)S(6)} %copy.9.count_at.count, bf16[1,4,4096]{2,1,0:T(4,128)(2,1)} %blocks_at.1, bf16[128,384]{1,0:T(8,128)(2,1)} %tokens_at.1), custom_call_target="tpu_custom_call" | custom-call | flops 10000000 | bytes 2097152 | tf_op jit(solution)/shard_map/pallas_call | solution.py:180
  3.7 0.0 copy-start.2
  3.8 9.6 %all-to-all-start = ((bf16[32,144,128]{2,1,0:T(8,128)(2,1)}), bf16[32,144,128]{2,1,0:T(8,128)(2,1)S(1)}, u32[]{:S(2)}, u32[]{:S(2)}) async-start(bf16[32,144,128]{2,1,0:T(8,128)(2,1)} %get-tuple-element.8), calls=%async_computation | async-start | bytes 2359296 | tf_op jit(solution)/shard_map/all_to_all | solution.py:198
  13.4 0.0 copy-done.2
  13.4 36.5 %all_gather.3 = bf16[3072,128]{1,0:T(8,128)(2,1)S(1)} all-gather(bf16[384,128]{1,0:T(8,128)(2,1)S(1)} %copy-done.2), channel_id=1, replica_groups=mesh['row'=32,'half'=8,'side'=2] {'half'}, dimensions={0}, use_global_device_ids=true | all-gather | bytes 884736 | tf_op jit(solution)/shard_map/all_gather | solution.py:204
  49.9 0.1 fusion.8
  49.9 3.7 %collective-permute-start = (bf16[1536,128]{1,0:T(8,128)(2,1)S(1)}, bf16[1536,128]{1,0:T(8,128)(2,1)S(1)}, u32[]{:S(2)}, u32[]{:S(2)}) collective-permute-start(bf16[1536,128]{1,0:T(8,128)(2,1)S(1)} %get-tuple-element.14), channel_id=1, source_target_pairs={{0,1},{1,2},{2,3},{3,4},{4,5},{5,6},{6,7},{7,8},{8,9},{9,10},{10,1... | collective-permute-start | bytes 1179656 | tf_op jit(solution)/shard_map/ppermute | solution.py:178
  53.6 3.4 %collective-permute-start.1 = (bf16[1536,128]{1,0:T(8,128)(2,1)S(1)}, bf16[1536,128]{1,0:T(8,128)(2,1)S(1)}, u32[]{:S(2)}, u32[]{:S(2)}) collective-permute-start(bf16[1536,128]{1,0:T(8,128)(2,1)S(1)} %get-tuple-element.13), channel_id=1, source_target_pairs={{0,15},{1,0},{2,1},{3,2},{4,3},{5,4},{6,5},{7,6},{8,7},{9,8},{10,9... | collective-permute-start | bytes 1179656 | tf_op jit(solution)/shard_map/ppermute | solution.py:178
  57.0 0.0 all-to-all-done.weights_at
  57.0 0.1 fusion.4
  57.1 0.1 pad_add_fusion.ids
  57.2 3.6 %collective-permute-done = bf16[1536,128]{1,0:T(8,128)(2,1)S(1)} collective-permute-done((bf16[1536,128]{1,0:T(8,128)(2,1)S(1)}, bf16[1536,128]{1,0:T(8,128)(2,1)S(1)}, u32[]{:S(2)}, u32[]{:S(2)}) %collective-permute-start) | collective-permute-done | bytes 393248 | tf_op jit(solution)/shard_map/ppermute | solution.py:178
  60.8 2.4 %collective-permute-done.1 = bf16[1536,128]{1,0:T(8,128)(2,1)S(1)} collective-permute-done((bf16[1536,128]{1,0:T(8,128)(2,1)S(1)}, bf16[1536,128]{1,0:T(8,128)(2,1)S(1)}, u32[]{:S(2)}, u32[]{:S(2)}) %collective-permute-start.1) | collective-permute-done | bytes 393248 | tf_op jit(solution)/shard_map/ppermute | solution.py:178
  63.2 12.4 %shard_map.86 = (bf16[128,3072]{1,0:T(8,128)(2,1)}, bf16[6384,128]{1,0:T(8,128)(2,1)}, bf16[32,128,128]{2,1,0:T(8,128)(2,1)}) custom-call(s32[32,12]{1,0:T(8,128)S(1)} %pad_add_fusion.ids, bf16[32,144,128]{2,1,0:T(8,128)(2,1)} %copy-done.1, bf16[48,64,128]{2,1,0:T(8,128)(2,1)S(1)} %bitcast.8, bf16[24,64,128]{2,1,0:T(8,128)(2,1)S(1)} %bitcast.9, ...), custom_call_target="tpu_custom_call" | custom-call | flops 1000000000 | bytes 2097152 | tf_op jit(solution)/shard_map/pallas_call | solution.py:208
  75.6 0.0 copy-start
  75.6 8.2 %all-to-all-start.1 = ((bf16[32,128,128]{2,1,0:T(8,128)(2,1)}), bf16[32,128,128]{2,1,0:T(8,128)(2,1)S(1)}, u32[]{:S(2)}, u32[]{:S(2)}) async-start(bf16[32,128,128]{2,1,0:T(8,128)(2,1)} %get-tuple-element.12), calls=%async_computation.1 | async-start | bytes 2097152 | tf_op jit(solution)/shard_map/all_to_all | solution.py:227
  83.8 38.0 %fusion = bf16[400,128]{1,0:T(8,128)(2,1)S(1)} fusion(bf16[6384,128]{1,0:T(8,128)(2,1)S(1)} %copy-done), kind=kCustom, calls=%all-reduce-scatter | all-reduce-scatter fusion | flops 819201 | bytes 1738752
  121.8 2.7 %collective-permute-start.2 = (bf16[15,128]{1,0:T(8,128)(2,1)S(1)}, bf16[15,128]{1,0:T(8,128)(2,1)S(1)}, u32[]{:S(2)}, u32[]{:S(2)}) collective-permute-start(bf16[15,128]{1,0:T(8,128)(2,1)S(1)} %slice.27), channel_id=1, source_target_pairs={{0,1},{1,2},{2,3},{3,4},{4,5},{5,6},{6,7},{7,8},{8,9},{9,10},{10,1... | collective-permute-start | bytes 11528
  124.6 1.3 dynamic-slice.4
  126.5 0.0 collective-permute-done.2
  126.5 0.6 concatenate.4
  127.2 0.9 shard_map.87
  128.1 0.0 all-to-all-done.1.terms
  128.1 1.0 shard_map.88
  (7 shorter events, 0.1 us)
Async XLA Ops:
  3.7 9.6 %copy-start.2 = (bf16[384,128]{1,0:T(8,128)(2,1)S(1)}, bf16[384,128]{1,0:T(8,128)(2,1)}, u32[]{:S(2)}) copy-start(bf16[384,128]{1,0:T(8,128)(2,1)} %get-tuple-element.9) | copy-start | bytes 294916
  3.8 53.2 %all-to-all-start = ((bf16[32,144,128]{2,1,0:T(8,128)(2,1)}), bf16[32,144,128]{2,1,0:T(8,128)(2,1)S(1)}, u32[]{:S(2)}, u32[]{:S(2)}) async-start(bf16[32,144,128]{2,1,0:T(8,128)(2,1)} %get-tuple-element.8), calls=%async_computation | async-start | bytes 2359296 | tf_op jit(solution)/shard_map/all_to_all | solution.py:198
  49.9 10.9 %collective-permute-start = (bf16[1536,128]{1,0:T(8,128)(2,1)S(1)}, bf16[1536,128]{1,0:T(8,128)(2,1)S(1)}, u32[]{:S(2)}, u32[]{:S(2)}) collective-permute-start(bf16[1536,128]{1,0:T(8,128)(2,1)S(1)} %get-tuple-element.14), channel_id=1, source_target_pairs={{0,1},{1,2},{2,3},{3,4},{4,5},{5,6},{6,7},{7,8},{8,9},{9,10},{10,1... | collective-permute-start | bytes 1179656 | tf_op jit(solution)/shard_map/ppermute | solution.py:178
  53.6 9.7 %collective-permute-start.1 = (bf16[1536,128]{1,0:T(8,128)(2,1)S(1)}, bf16[1536,128]{1,0:T(8,128)(2,1)S(1)}, u32[]{:S(2)}, u32[]{:S(2)}) collective-permute-start(bf16[1536,128]{1,0:T(8,128)(2,1)S(1)} %get-tuple-element.13), channel_id=1, source_target_pairs={{0,15},{1,0},{2,1},{3,2},{4,3},{5,4},{6,5},{7,6},{8,7},{9,8},{10,9... | collective-permute-start | bytes 1179656 | tf_op jit(solution)/shard_map/ppermute | solution.py:178
  57.0 6.3 %copy-start.1 = (bf16[32,144,128]{2,1,0:T(8,128)(2,1)}, bf16[32,144,128]{2,1,0:T(8,128)(2,1)S(1)}, u32[]{:S(2)}) copy-start(bf16[32,144,128]{2,1,0:T(8,128)(2,1)S(1)} %all-to-all-done.weights_at) | copy-start | bytes 3538948
  75.6 8.2 %copy-start = (bf16[6384,128]{1,0:T(8,128)(2,1)S(1)}, bf16[6384,128]{1,0:T(8,128)(2,1)}, u32[]{:S(2)}) copy-start(bf16[6384,128]{1,0:T(8,128)(2,1)} %get-tuple-element.11) | copy-start | bytes 4902916
  75.6 52.4 %all-to-all-start.1 = ((bf16[32,128,128]{2,1,0:T(8,128)(2,1)}), bf16[32,128,128]{2,1,0:T(8,128)(2,1)S(1)}, u32[]{:S(2)}, u32[]{:S(2)}) async-start(bf16[32,128,128]{2,1,0:T(8,128)(2,1)} %get-tuple-element.12), calls=%async_computation.1 | async-start | bytes 2097152 | tf_op jit(solution)/shard_map/all_to_all | solution.py:227
  121.8 4.7 %collective-permute-start.2 = (bf16[15,128]{1,0:T(8,128)(2,1)S(1)}, bf16[15,128]{1,0:T(8,128)(2,1)S(1)}, u32[]{:S(2)}, u32[]{:S(2)}) collective-permute-start(bf16[15,128]{1,0:T(8,128)(2,1)S(1)} %slice.27), channel_id=1, source_target_pairs={{0,1},{1,2},{2,3},{3,4},{4,5},{5,6},{6,7},{7,8},{8,9},{9,10},{10,1... | collective-permute-start | bytes 11528

commit v6 on v5

--- a/solution.py
+++ b/solution.py
@@ -40,7 +40,7 @@
 
 
 def prep_kernel(
-    first, rows_at, columns_at, count_at, blocks_at, tokens_at, parcels, turned, rows, columns, count, blocks, tokens, spread, sems
+    first, rows_at, columns_at, count_at, blocks_at, tokens_at, parcels, turned, rows, columns, count, blocks, tokens, spread, parcel, sems
 ):
     for copy in fetch(
         sems, (blocks_at, blocks), (tokens_at, tokens), (rows_at, rows), (columns_at, columns), (count_at, count)
@@ -49,27 +49,43 @@
     for i in range(32):
         spread[pl.ds(i, 4, stride=32), :] = blocks[0, :, i * 128 : (i + 1) * 128].astype(F32)
     slot = first[0] + lax.broadcasted_iota(jnp.int32, (128, 128), 0) // 32
-    parcels[0, :128] = jnp.where(slot < count[0], spread[...], 0.0).astype(BF)
+    parcel[:128] = jnp.where(slot < count[0], spread[...], 0.0).astype(BF)
     lane = lax.broadcasted_iota(jnp.int32, (16, 128), 1)
     named = jnp.zeros((16, 128), jnp.int32)
     for j in range(4):
         named = jnp.where(lane == j, rows[0, j], named)
         named = jnp.where(lane == 4 + j, columns[0, j], named)
-    parcels[0, 128:] = named.astype(F32).astype(BF)
-
-    def again(d, carry):
-        parcels[d] = parcels[0]
-        return carry
-
-    lax.fori_loop(1, parcels.shape[0], again, 0)
+    parcel[128:] = named.astype(F32).astype(BF)
+    copies = fetch(sems, *((parcel, parcels.at[d]) for d in range(parcels.shape[0])))
     parted = picker(True)
     for k in range(3):
         at = k * 128
         turned[at : at + 128] = dot(parted, tokens[:, at : at + 128], NT).astype(BF)
+    for copy in copies:
+        copy.wait()
 
 
 def main_kernel(
-    ids, weights_at, same, other_low, other_high, upstream_at, hidden, part, terms, weights, whole, upstream, pre, grad, total, sems
+    ids,
+    weights_at,
+    same,
+    other_low,
+    other_high,
+    upstream_at,
+    hidden_at,
+    part_at,
+    terms_at,
+    weights,
+    whole,
+    upstream,
+    hidden,
+    part,
+    terms,
+    pre,
+    grad,
+    total,
+    sems,
+    out_sems,
 ):
     copies = fetch(
         sems,
@@ -81,17 +97,18 @@
     )
     pre[...] = jnp.zeros_like(pre)
     total[...] = jnp.zeros_like(total)
+    part[:, 384:] = jnp.zeros((16, 16, 128), BF)
     for copy in copies[:4]:
         copy.wait()
 
-    def slots(visit):
+    def slots(visit, step):
         def some(g, carry):
-            for q in range(8):
+            for q in range(step):
                 for j in range(4):
-                    visit(g * 8 + q, j)
+                    visit(g * step + q, j)
             return carry
 
-        lax.fori_loop(0, 4, some, 0)
+        lax.fori_loop(0, 32 // step, some, 0)
 
     def block(d, j):
         lines = weights[d, j * 32 : (j + 1) * 32]
@@ -100,7 +117,7 @@
     def forward(d, j):
         pre[ids[d, 4 + j]] += dot(block(d, j), whole[ids[d, j]], TN)
 
-    slots(forward)
+    slots(forward, 8)
     copies[4].wait()
     unit = picker(False)
 
@@ -118,24 +135,31 @@
         return carry
 
     lax.fori_loop(0, 24, some_columns, 0, unroll=4)
+    sent = [pltpu.make_async_copy(hidden, hidden_at, out_sems.at[16])]
+    sent[-1].start()
 
     def weight(d, j):
         product = dot(whole[ids[d, j]], grad[ids[d, 4 + j]], NT).astype(BF)
         terms[d, j * 32 : (j + 1) * 32] = jnp.concatenate([product[:32], product[32:]], axis=1)
 
-    slots(weight)
+    slots(weight, 16)
+    sent.append(pltpu.make_async_copy(terms, terms_at, out_sems.at[17]))
+    sent[-1].start()
 
     def backward(d, j):
         total[ids[d, 8 + j]] += dot(block(d, j), grad[ids[d, 4 + j]])
 
-    slots(backward)
+    slots(backward, 16)
     for o in range(16):
-        part[400 * o : 400 * o + 384] = total[6 * o : 6 * o + 6].reshape(384, 128).astype(BF)
-        if o < 15:
-            part[400 * o + 384 : 400 * o + 400] = jnp.zeros((16, 128), BF)
-
-
-def weight_end_kernel(count, first, terms, out, total):
+        part[o, :384] = total[6 * o : 6 * o + 6].reshape(384, 128).astype(BF)
+        here, size = (part.at[o], 400) if o < 15 else (part.at[o, :384], 384)
+        sent.append(pltpu.make_async_copy(here, part_at.at[400 * o : 400 * o + size], out_sems.at[o]))
+        sent[-1].start()
+    for copy in sent:
+        copy.wait()
+
+
+def end_kernel(count, first, terms, own, weights, inputs, total):
     def some(d, kept):
         return kept + terms[d].astype(F32)
 
@@ -143,26 +167,23 @@
     slot = first[0] + lax.broadcasted_iota(jnp.int32, (128, 128), 0) // 32
     total[...] = jnp.where(slot < count[0], kept, 0.0)
     for i in range(32):
-        out[0, :, i * 128 : (i + 1) * 128] = total[pl.ds(i, 4, stride=32), :].astype(BF)
-
-
-def input_end_kernel(own, out):
+        weights[0, :, i * 128 : (i + 1) * 128] = total[pl.ds(i, 4, stride=32), :].astype(BF)
     parted = picker(True)
     for k in range(3):
         at = k * 128
-        out[:, at : at + 128] = dot(own[at : at + 128], parted, TN).astype(BF)
+        inputs[:, at : at + 128] = dot(own[at : at + 128], parted, TN).astype(BF)
 
 
 def shape(*dims):
     return jax.ShapeDtypeStruct(dims, BF)
 
 
-def call(kernel, outs, n_scalar, n_array, scratch, flops, limit, place=VM):
+def call(kernel, outs, n_scalar, n_array, scratch, flops, limit, place, leave):
     return pl.pallas_call(
         kernel,
         out_shape=outs,
         in_specs=[SM] * n_scalar + [place] * n_array,
-        out_specs=jax.tree.map(lambda _: VM, outs),
+        out_specs=leave,
         scratch_shapes=scratch,
         compiler_params=pltpu.CompilerParams(vmem_limit_bytes=limit * MIB),
         cost_estimate=pl.CostEstimate(flops=flops, bytes_accessed=2 * MIB, transcendentals=0),
@@ -189,11 +210,13 @@
             pltpu.VMEM((1, 4, 4096), BF),
             pltpu.VMEM((128, 384), BF),
             pltpu.VMEM((128, 128), F32),
-            pltpu.SemaphoreType.DMA((5,)),
+            pltpu.VMEM((144, 128), BF),
+            pltpu.SemaphoreType.DMA((n_row,)),
         ],
         10_000_000,
         60,
         ANY,
+        (ANY, VM),
     )(first, block_rows, block_columns, panel_counts, weight_blocks, tokens)
     parcels = lax.all_to_all(parcels, "row", 0, 0, tiled=True)
     ids = parcels[:, 128, :8].astype(jnp.int32)
@@ -214,29 +237,35 @@
             pltpu.VMEM((n_row, 144, 128), BF),
             pltpu.VMEM((96, BLK, 128), BF),
             pltpu.VMEM((128, 3072), BF),
+            pltpu.VMEM((128, 3072), BF),
+            pltpu.VMEM((16, 400, 128), BF),
+            pltpu.VMEM((n_row, 128, 128), BF),
             pltpu.VMEM((48, BLK, 128), F32),
             pltpu.VMEM((48, BLK, 128), BF),
             pltpu.VMEM((96, BLK, 128), F32),
             pltpu.SemaphoreType.DMA((5,)),
+            pltpu.SemaphoreType.DMA((18,)),
         ],
         1_000_000_000,
         52,
         ANY,
+        (ANY, ANY, ANY),
     )(ids, parcels, *(a.reshape(-1, BLK, 128) for a in (same, other_low, other_high)), hidden_grad)
 
     terms = lax.all_to_all(terms, "row", 0, 0, tiled=True)
     own = lax.optimization_barrier(lax.psum_scatter(part, COL, scatter_dimension=0, tiled=True))
     own = lax.dynamic_slice_in_dim(own, me_col, 384, 0)
-    input_grad = call(input_end_kernel, shape(128, 384), 0, 1, [], 10_000_000, 4)(own)
-    weight_grad = call(
-        weight_end_kernel,
-        shape(1, 4, 4096),
+    weight_grad, input_grad = call(
+        end_kernel,
+        (shape(1, 4, 4096), shape(128, 384)),
         2,
-        1,
+        2,
         [pltpu.VMEM((128, 128), F32)],
-        500_000_000,
+        10_000_000,
         4,
-    )(panel_counts, first, terms)
+        VM,
+        (VM, VM),
+    )(panel_counts, first, terms, own)
     return hidden, input_grad, weight_grad
 
 

time: 130 us -> 128 us (0.985)
  transfers between devices with their start and end apart: 5 -> 5, of which waited for: 2 -> 2; matrix products, arithmetic and copies ran while one was open for 31% -> 31% of each run, Pallas kernels for 1% -> 0%
where the time goes in v6:
time: 128 us
  blocking collectives  74.4 us (58%)
  starting transfers between devices  27.6 us (22%)
  Pallas kernels  15.4 us (12%)
  waiting for transfers between devices  6.05 us (5%)
  between operations  2.11 us (2%)
  local copies, waits for them, and re-layouts  2.03 us (2%)
    unnamed x1, blocking collectives  38 us
    all_gather x1, blocking collectives, on_device(): same = lax.all_gather(turned, 'half', axis=0, tiled=True)  36.5 us
    pallas_call x1, Pallas kernels, on_device(): call(main_kernel, (shape(128, 3072), shape(6384, 128), shape(n_row, 128,...  11.2 us
    all_to_all x1, starting transfers between devices, on_device(): parcels = lax.all_to_all(parcels, 'row', 0, 0, tiled=True)  9.62 us
    all_to_all x1, starting transfers between devices, on_device(): terms = lax.all_to_all(terms, 'row', 0, 0, tiled=True)  8.17 us
    ppermute x2, starting transfers between devices, shift(): return lax.ppermute(a, COL, [(i, (i + by) % n_col) for i in range(n_col)])  7.05 us
    ppermute x2, waiting for transfers between devices, shift(): return lax.ppermute(a, COL, [(i, (i + by) % n_col) for i in range(n_col)])  6.04 us
    pallas_call x1, Pallas kernels, on_device(): call(prep_kernel, (shape(n_row, 144, 128), shape(384, 128)), 1, 5, [pltpu...  3 us
  transfers between devices with their start and end apart: 5, of which 2 were waited for; matrix products, arithmetic and copies ran while one was open for 31% of the time, Pallas kernels for 0%

profile of v6, /device:TPU:6, one launch (start us, length us, event | category | flops | bytes accessed | tf_op | source)
XLA Modules:
  0.0 127.8 jit_solution(15239020762406114777)
XLA Ops:
  1.3 3.0 %shard_map.85 = (bf16[32,144,128]{2,1,0:T(8,128)(2,1)}, bf16[384,128]{1,0:T(8,128)(2,1)}) custom-call(s32[1]{0:T(128)} %bitcast.first, s32[1,4]{1,0:T(1,128)} %rows_at.1, s32[1,4]{1,0:T(1,128)} %columns_at.1, s32[1]{0:T(128)S(6)} %copy.9.count_at.count, bf16[1,4,4096]{2,1,0:T(4,128)(2,1)} %blocks_at.1, bf16[128,384]{1,0:T(8,128)(2,1)} %tokens_at.1), custom_call_target="tpu_custom_call" | custom-call | flops 10000000 | bytes 2097152 | tf_op jit(solution)/shard_map/pallas_call | solution.py:201
  4.3 0.0 copy-start.2
  4.3 9.6 %all-to-all-start = ((bf16[32,144,128]{2,1,0:T(8,128)(2,1)}), bf16[32,144,128]{2,1,0:T(8,128)(2,1)S(1)}, u32[]{:S(2)}, u32[]{:S(2)}) async-start(bf16[32,144,128]{2,1,0:T(8,128)(2,1)} %get-tuple-element.10), calls=%async_computation | async-start | bytes 2359296 | tf_op jit(solution)/shard_map/all_to_all | solution.py:221
  13.9 0.0 copy-done.2
  13.9 36.5 %all_gather.3 = bf16[3072,128]{1,0:T(8,128)(2,1)S(1)} all-gather(bf16[384,128]{1,0:T(8,128)(2,1)S(1)} %copy-done.2), channel_id=1, replica_groups=mesh['row'=32,'half'=8,'side'=2] {'half'}, dimensions={0}, use_global_device_ids=true | all-gather | bytes 884736 | tf_op jit(solution)/shard_map/all_gather | solution.py:227
  50.4 0.1 fusion.8
  50.5 3.6 %collective-permute-start = (bf16[1536,128]{1,0:T(8,128)(2,1)S(1)}, bf16[1536,128]{1,0:T(8,128)(2,1)S(1)}, u32[]{:S(2)}, u32[]{:S(2)}) collective-permute-start(bf16[1536,128]{1,0:T(8,128)(2,1)S(1)} %get-tuple-element.18), channel_id=1, source_target_pairs={{0,1},{1,2},{2,3},{3,4},{4,5},{5,6},{6,7},{7,8},{8,9},{9,10},{10,1... | collective-permute-start | bytes 1179656 | tf_op jit(solution)/shard_map/ppermute | solution.py:199
  54.1 3.4 %collective-permute-start.1 = (bf16[1536,128]{1,0:T(8,128)(2,1)S(1)}, bf16[1536,128]{1,0:T(8,128)(2,1)S(1)}, u32[]{:S(2)}, u32[]{:S(2)}) collective-permute-start(bf16[1536,128]{1,0:T(8,128)(2,1)S(1)} %get-tuple-element.17), channel_id=1, source_target_pairs={{0,15},{1,0},{2,1},{3,2},{4,3},{5,4},{6,5},{7,6},{8,7},{9,8},{10,9... | collective-permute-start | bytes 1179656 | tf_op jit(solution)/shard_map/ppermute | solution.py:199
  57.5 0.0 all-to-all-done.weights_at
  57.6 0.0 copy-start.1
  57.6 0.1 fusion.4
  57.7 0.1 pad_add_fusion.ids
  57.7 3.6 %collective-permute-done = bf16[1536,128]{1,0:T(8,128)(2,1)S(1)} collective-permute-done((bf16[1536,128]{1,0:T(8,128)(2,1)S(1)}, bf16[1536,128]{1,0:T(8,128)(2,1)S(1)}, u32[]{:S(2)}, u32[]{:S(2)}) %collective-permute-start) | collective-permute-done | bytes 393248 | tf_op jit(solution)/shard_map/ppermute | solution.py:199
  61.4 2.4 %collective-permute-done.1 = bf16[1536,128]{1,0:T(8,128)(2,1)S(1)} collective-permute-done((bf16[1536,128]{1,0:T(8,128)(2,1)S(1)}, bf16[1536,128]{1,0:T(8,128)(2,1)S(1)}, u32[]{:S(2)}, u32[]{:S(2)}) %collective-permute-start.1) | collective-permute-done | bytes 393248 | tf_op jit(solution)/shard_map/ppermute | solution.py:199
  63.8 0.0 copy-done.1
  63.8 11.2 %shard_map.86 = (bf16[128,3072]{1,0:T(8,128)(2,1)}, bf16[6384,128]{1,0:T(8,128)(2,1)}, bf16[32,128,128]{2,1,0:T(8,128)(2,1)}) custom-call(s32[32,12]{1,0:T(8,128)S(1)} %pad_add_fusion.ids, bf16[32,144,128]{2,1,0:T(8,128)(2,1)} %copy-done.1, bf16[48,64,128]{2,1,0:T(8,128)(2,1)S(1)} %bitcast.8, bf16[24,64,128]{2,1,0:T(8,128)(2,1)S(1)} %bitcast.9, ...), custom_call_target="tpu_custom_call" | custom-call | flops 1000000000 | bytes 2097152 | tf_op jit(solution)/shard_map/pallas_call | solution.py:231
  75.0 8.2 %all-to-all-start.1 = ((bf16[32,128,128]{2,1,0:T(8,128)(2,1)}), bf16[32,128,128]{2,1,0:T(8,128)(2,1)S(1)}, u32[]{:S(2)}, u32[]{:S(2)}) async-start(bf16[32,128,128]{2,1,0:T(8,128)(2,1)} %get-tuple-element.13), calls=%async_computation.1 | async-start | bytes 2097152 | tf_op jit(solution)/shard_map/all_to_all | solution.py:255
  83.2 38.0 %fusion = bf16[400,128]{1,0:T(8,128)(2,1)S(1)} fusion(bf16[6384,128]{1,0:T(8,128)(2,1)S(1)} %copy-done), kind=kCustom, calls=%all-reduce-scatter | all-reduce-scatter fusion | flops 819201 | bytes 1738752
  121.2 2.7 %collective-permute-start.2 = (bf16[15,128]{1,0:T(8,128)(2,1)S(1)}, bf16[15,128]{1,0:T(8,128)(2,1)S(1)}, u32[]{:S(2)}, u32[]{:S(2)}) collective-permute-start(bf16[15,128]{1,0:T(8,128)(2,1)S(1)} %slice.27), channel_id=1, source_target_pairs={{0,1},{1,2},{2,3},{3,4},{4,5},{5,6},{6,7},{7,8},{8,9},{9,10},{10,1... | collective-permute-start | bytes 11528
  124.0 1.3 dynamic-slice.4
  125.9 0.0 collective-permute-done.2
  125.9 0.6 concatenate.4
  126.6 0.0 all-to-all-done.1.terms
  126.6 1.2 shard_map.87
  (6 shorter events, 0.1 us)
Async XLA Ops:
  4.3 9.6 %copy-start.2 = (bf16[384,128]{1,0:T(8,128)(2,1)S(1)}, bf16[384,128]{1,0:T(8,128)(2,1)}, u32[]{:S(2)}) copy-start(bf16[384,128]{1,0:T(8,128)(2,1)} %get-tuple-element.11) | copy-start | bytes 294916
  4.3 53.2 %all-to-all-start = ((bf16[32,144,128]{2,1,0:T(8,128)(2,1)}), bf16[32,144,128]{2,1,0:T(8,128)(2,1)S(1)}, u32[]{:S(2)}, u32[]{:S(2)}) async-start(bf16[32,144,128]{2,1,0:T(8,128)(2,1)} %get-tuple-element.10), calls=%async_computation | async-start | bytes 2359296 | tf_op jit(solution)/shard_map/all_to_all | solution.py:221
  50.5 10.9 %collective-permute-start = (bf16[1536,128]{1,0:T(8,128)(2,1)S(1)}, bf16[1536,128]{1,0:T(8,128)(2,1)S(1)}, u32[]{:S(2)}, u32[]{:S(2)}) collective-permute-start(bf16[1536,128]{1,0:T(8,128)(2,1)S(1)} %get-tuple-element.18), channel_id=1, source_target_pairs={{0,1},{1,2},{2,3},{3,4},{4,5},{5,6},{6,7},{7,8},{8,9},{9,10},{10,1... | collective-permute-start | bytes 1179656 | tf_op jit(solution)/shard_map/ppermute | solution.py:199
  54.1 9.7 %collective-permute-start.1 = (bf16[1536,128]{1,0:T(8,128)(2,1)S(1)}, bf16[1536,128]{1,0:T(8,128)(2,1)S(1)}, u32[]{:S(2)}, u32[]{:S(2)}) collective-permute-start(bf16[1536,128]{1,0:T(8,128)(2,1)S(1)} %get-tuple-element.17), channel_id=1, source_target_pairs={{0,15},{1,0},{2,1},{3,2},{4,3},{5,4},{6,5},{7,6},{8,7},{9,8},{10,9... | collective-permute-start | bytes 1179656 | tf_op jit(solution)/shard_map/ppermute | solution.py:199
  57.6 6.2 %copy-start.1 = (bf16[32,144,128]{2,1,0:T(8,128)(2,1)}, bf16[32,144,128]{2,1,0:T(8,128)(2,1)S(1)}, u32[]{:S(2)}) copy-start(bf16[32,144,128]{2,1,0:T(8,128)(2,1)S(1)} %all-to-all-done.weights_at) | copy-start | bytes 3538948
  75.0 8.2 %copy-start = (bf16[6384,128]{1,0:T(8,128)(2,1)S(1)}, bf16[6384,128]{1,0:T(8,128)(2,1)}, u32[]{:S(2)}) copy-start(bf16[6384,128]{1,0:T(8,128)(2,1)} %get-tuple-element.14) | copy-start | bytes 4902916
  75.0 51.6 %all-to-all-start.1 = ((bf16[32,128,128]{2,1,0:T(8,128)(2,1)}), bf16[32,128,128]{2,1,0:T(8,128)(2,1)S(1)}, u32[]{:S(2)}, u32[]{:S(2)}) async-start(bf16[32,128,128]{2,1,0:T(8,128)(2,1)} %get-tuple-element.13), calls=%async_computation.1 | async-start | bytes 2097152 | tf_op jit(solution)/shard_map/all_to_all | solution.py:255
  121.2 4.7 %collective-permute-start.2 = (bf16[15,128]{1,0:T(8,128)(2,1)S(1)}, bf16[15,128]{1,0:T(8,128)(2,1)S(1)}, u32[]{:S(2)}, u32[]{:S(2)}) collective-permute-start(bf16[15,128]{1,0:T(8,128)(2,1)S(1)} %slice.27), channel_id=1, source_target_pairs={{0,1},{1,2},{2,3},{3,4},{4,5},{5,6},{6,7},{7,8},{8,9},{9,10},{10,1... | collective-permute-start | bytes 11528

commit v7 on v6

--- a/solution.py
+++ b/solution.py
@@ -40,7 +40,7 @@
 
 
 def prep_kernel(
-    first, rows_at, columns_at, count_at, blocks_at, tokens_at, parcels, turned, rows, columns, count, blocks, tokens, spread, parcel, sems
+    first, rows_at, columns_at, count_at, blocks_at, tokens_at, parcels, turned, rows, columns, count, blocks, tokens, spread, sems
 ):
     for copy in fetch(
         sems, (blocks_at, blocks), (tokens_at, tokens), (rows_at, rows), (columns_at, columns), (count_at, count)
@@ -49,35 +49,114 @@
     for i in range(32):
         spread[pl.ds(i, 4, stride=32), :] = blocks[0, :, i * 128 : (i + 1) * 128].astype(F32)
     slot = first[0] + lax.broadcasted_iota(jnp.int32, (128, 128), 0) // 32
-    parcel[:128] = jnp.where(slot < count[0], spread[...], 0.0).astype(BF)
+    parcels[0, :128] = jnp.where(slot < count[0], spread[...], 0.0).astype(BF)
     lane = lax.broadcasted_iota(jnp.int32, (16, 128), 1)
     named = jnp.zeros((16, 128), jnp.int32)
     for j in range(4):
         named = jnp.where(lane == j, rows[0, j], named)
         named = jnp.where(lane == 4 + j, columns[0, j], named)
-    parcel[128:] = named.astype(F32).astype(BF)
-    copies = fetch(sems, *((parcel, parcels.at[d]) for d in range(parcels.shape[0])))
+    parcels[0, 128:] = named.astype(F32).astype(BF)
+
+    def again(d, carry):
+        parcels[d] = parcels[0]
+        return carry
+
+    lax.fori_loop(1, parcels.shape[0], again, 0)
     parted = picker(True)
     for k in range(3):
         at = k * 128
         turned[at : at + 128] = dot(parted, tokens[:, at : at + 128], NT).astype(BF)
-    for copy in copies:
+
+
+def forward(entry, weights, whole, pre):
+    slot = jnp.bitwise_and(entry, 127)
+    column = jnp.bitwise_and(jnp.right_shift(entry, 7), 63)
+    row = jnp.right_shift(entry, 13)
+    start = pl.multiple_of(jnp.bitwise_and(slot, 3) * 32, 32)
+    lines = weights[jnp.right_shift(slot, 2), pl.ds(start, 32)]
+    block = jnp.concatenate([lines[:, :BLK], lines[:, BLK:]], axis=0)
+    pre[column] += dot(block, whole[row], TN)
+
+
+def forward_all(count, at, entries, weights, whole, pre):
+    def some(g, carry):
+        for i in range(16):
+            forward(entries[at + g * 16 + i], weights, whole, pre)
+        return carry
+
+    lax.fori_loop(0, jnp.right_shift(count + 15, 4), some, 0)
+
+
+def early_kernel(
+    ids,
+    weights_at,
+    same,
+    upstream_at,
+    early_at,
+    turned_at,
+    later,
+    weights,
+    whole,
+    upstream,
+    pre,
+    turned,
+    now,
+    sems,
+    out_sems,
+):
+    copies = fetch(sems, (upstream_at, upstream), (weights_at, weights), (same, whole))
+    pre[...] = jnp.zeros_like(pre)
+
+    def sort(d, counts):
+        n, m = counts
+        for j in range(4):
+            row = ids[d, j]
+            entry = (row * 64 + ids[d, 4 + j]) * 128 + d * 4 + j
+            far = (row >= 48).astype(jnp.int32)
+            now[n] = entry
+            later[1 + m] = entry
+            n, m = n + 1 - far, m + far
+        return n, m
+
+    n, m = lax.fori_loop(0, 32, sort, (jnp.int32(0), jnp.int32(0)))
+    for i in range(16):
+        now[n + i] = 48 * 128
+        later[1 + m + i] = (48 * 64 + 48) * 128
+    later[0] = m
+    unit = picker(False)
+    copies[0].wait()
+
+    def some_columns(g, carry):
+        at = pl.multiple_of(g * 128, 128)
+        turned[pl.ds(g * 2, 2)] = dot(unit, upstream[:, pl.ds(at, 128)], NT).astype(BF).reshape(2, BLK, 128)
+        return carry
+
+    lax.fori_loop(0, 24, some_columns, 0, unroll=4)
+    sent = fetch(out_sems.at[:1], (turned, turned_at))
+    for copy in copies[1:]:
+        copy.wait()
+    forward_all(n, 0, now, weights, whole, pre)
+    sent += fetch(out_sems.at[1:], (pre.at[:48], early_at))
+    for copy in sent:
         copy.wait()
 
 
 def main_kernel(
     ids,
+    entries,
     weights_at,
     same,
     other_low,
     other_high,
-    upstream_at,
+    early_at,
+    turned_at,
     hidden_at,
     part_at,
     terms_at,
     weights,
     whole,
-    upstream,
+    early,
+    turned,
     hidden,
     part,
     terms,
@@ -90,15 +169,16 @@
     copies = fetch(
         sems,
         (weights_at, weights),
-        (same, whole.at[:48]),
         (other_low, whole.at[48:72]),
         (other_high, whole.at[72:]),
-        (upstream_at, upstream),
+        (early_at, early),
+        (turned_at, turned),
+        (same, whole.at[:48]),
     )
     pre[...] = jnp.zeros_like(pre)
     total[...] = jnp.zeros_like(total)
     part[:, 384:] = jnp.zeros((16, 16, 128), BF)
-    for copy in copies[:4]:
+    for copy in copies[:3]:
         copy.wait()
 
     def slots(visit, step):
@@ -114,23 +194,21 @@
         lines = weights[d, j * 32 : (j + 1) * 32]
         return jnp.concatenate([lines[:, :BLK], lines[:, BLK:]], axis=0)
 
-    def forward(d, j):
-        pre[ids[d, 4 + j]] += dot(block(d, j), whole[ids[d, j]], TN)
-
-    slots(forward, 8)
-    copies[4].wait()
+    forward_all(entries[0], 1, entries, weights, whole, pre)
+    for copy in copies[3:]:
+        copy.wait()
     unit = picker(False)
 
     def some_columns(g, carry):
         at = pl.multiple_of(g * 128, 128)
-        v = pre[pl.ds(g * 2, 2)].reshape(128, 128)
+        v = (pre[pl.ds(g * 2, 2)] + early[pl.ds(g * 2, 2)]).reshape(128, 128)
         tangent = jnp.tanh(root_two_pi * (v + cubic_term * v * v * v))
         value = 0.5 * v * (1.0 + tangent)
         slope = 0.5 * (1.0 + tangent) + 0.5 * v * (1.0 - tangent * tangent) * root_two_pi * (
             1.0 + 3.0 * cubic_term * v * v
         )
-        turned = dot(unit, upstream[:, pl.ds(at, 128)], NT)
-        grad[pl.ds(g * 2, 2)] = (turned * slope).astype(BF).reshape(2, BLK, 128)
+        upstream = turned[pl.ds(g * 2, 2)].reshape(128, 128).astype(F32)
+        grad[pl.ds(g * 2, 2)] = (upstream * slope).astype(BF).reshape(2, BLK, 128)
         hidden[:, pl.ds(at, 128)] = dot(unit, value.astype(BF), NT).astype(BF)
         return carry
 
@@ -210,13 +288,12 @@
             pltpu.VMEM((1, 4, 4096), BF),
             pltpu.VMEM((128, 384), BF),
             pltpu.VMEM((128, 128), F32),
-            pltpu.VMEM((144, 128), BF),
-            pltpu.SemaphoreType.DMA((n_row,)),
+            pltpu.SemaphoreType.DMA((5,)),
         ],
         10_000_000,
         60,
         ANY,
-        (ANY, VM),
+        (VM, VM),
     )(first, block_rows, block_columns, panel_counts, weight_blocks, tokens)
     parcels = lax.all_to_all(parcels, "row", 0, 0, tiled=True)
     ids = parcels[:, 128, :8].astype(jnp.int32)
@@ -228,29 +305,56 @@
     middle = same.shape[0] // 2
     other_low, other_high = shift(same[:middle], 1), shift(same[middle:], -1)
 
+    same, other_low, other_high = (a.reshape(-1, BLK, 128) for a in (same, other_low, other_high))
+    early, turned, entries = call(
+        early_kernel,
+        (
+            jax.ShapeDtypeStruct((48, BLK, 128), F32),
+            shape(48, BLK, 128),
+            jax.ShapeDtypeStruct((160,), jnp.int32),
+        ),
+        1,
+        3,
+        [
+            pltpu.VMEM((n_row, 144, 128), BF),
+            pltpu.VMEM((48, BLK, 128), BF),
+            pltpu.VMEM((128, 3072), BF),
+            pltpu.VMEM((49, BLK, 128), F32),
+            pltpu.VMEM((48, BLK, 128), BF),
+            pltpu.SMEM((160,), jnp.int32),
+            pltpu.SemaphoreType.DMA((3,)),
+            pltpu.SemaphoreType.DMA((2,)),
+        ],
+        500_000_000,
+        52,
+        ANY,
+        (ANY, ANY, SM),
+    )(ids, parcels, same, hidden_grad)
+
     hidden, part, terms = call(
         main_kernel,
         (shape(128, 3072), shape(6384, 128), shape(n_row, 128, 128)),
-        1,
-        5,
+        2,
+        6,
         [
             pltpu.VMEM((n_row, 144, 128), BF),
             pltpu.VMEM((96, BLK, 128), BF),
-            pltpu.VMEM((128, 3072), BF),
+            pltpu.VMEM((48, BLK, 128), F32),
+            pltpu.VMEM((48, BLK, 128), BF),
             pltpu.VMEM((128, 3072), BF),
             pltpu.VMEM((16, 400, 128), BF),
             pltpu.VMEM((n_row, 128, 128), BF),
-            pltpu.VMEM((48, BLK, 128), F32),
+            pltpu.VMEM((49, BLK, 128), F32),
             pltpu.VMEM((48, BLK, 128), BF),
             pltpu.VMEM((96, BLK, 128), F32),
-            pltpu.SemaphoreType.DMA((5,)),
+            pltpu.SemaphoreType.DMA((6,)),
             pltpu.SemaphoreType.DMA((18,)),
         ],
         1_000_000_000,
         52,
         ANY,
         (ANY, ANY, ANY),
-    )(ids, parcels, *(a.reshape(-1, BLK, 128) for a in (same, other_low, other_high)), hidden_grad)
+    )(ids, entries, parcels, same, other_low, other_high, early, turned)
 
     terms = lax.all_to_all(terms, "row", 0, 0, tiled=True)
     own = lax.optimization_barrier(lax.psum_scatter(part, COL, scatter_dimension=0, tiled=True))

time: 128 us -> 128 us (level)
  waiting for transfers between devices: 6.05 us -> 0.01 us
  Pallas kernels: 15.4 us -> 20.7 us
  local copies, waits for them, and re-layouts: 2.03 us -> 3.73 us
  starting transfers between devices: 27.6 us -> 26 us
    pallas_call x0 -> x1, Pallas kernels: none -> 6.32 us  [on_device(): call(early_kernel, (jax.ShapeDtypeStruct((48, BLK, 128), F32), shape(48,...]
    ppermute x2, waiting for transfers between devices: 6.04 us -> 0.01 us  [shift(): return lax.ppermute(a, COL, [(i, (i + by) % n_col) for i in range(n_col)])]
    unnamed x10 -> x12, local copies, waits for them, and re-layouts: 1.94 us -> 3.64 us
    unnamed x1, starting transfers between devices: 2.75 us -> 1.44 us
  transfers between devices with their start and end apart: 5 -> 5, of which waited for: 2 -> 0; matrix products, arithmetic and copies ran while one was open for 31% -> 32% of each run, Pallas kernels for 0% -> 5%
where the time goes in v7:
time: 128 us; the launch traced here: 127 us
  blocking collectives  74.4 us (58%)
  starting transfers between devices  26 us (20%)
  Pallas kernels  20.7 us (16%)
  local copies, waits for them, and re-layouts  3.73 us (3%)
  between operations  2.13 us (2%)
    unnamed x1, blocking collectives  38 us
    all_gather x1, blocking collectives, on_device(): same = lax.all_gather(turned, 'half', axis=0, tiled=True)  36.5 us
    pallas_call x1, Pallas kernels, on_device(): call(main_kernel, (shape(128, 3072), shape(6384, 128), shape(n_row, 128,...  10.8 us
    all_to_all x1, starting transfers between devices, on_device(): parcels = lax.all_to_all(parcels, 'row', 0, 0, tiled=True)  9.62 us
    all_to_all x1, starting transfers between devices, on_device(): terms = lax.all_to_all(terms, 'row', 0, 0, tiled=True)  7.92 us
    ppermute x2, starting transfers between devices, shift(): return lax.ppermute(a, COL, [(i, (i + by) % n_col) for i in range(n_col)])  7.05 us
    pallas_call x1, Pallas kernels, on_device(): call(early_kernel, (jax.ShapeDtypeStruct((48, BLK, 128), F32), shape(48,...  6.32 us
    unnamed x12, local copies, waits for them, and re-layouts  3.64 us
  transfers between devices with their start and end apart: 5, of which 0 were waited for; matrix products, arithmetic and copies ran while one was open for 32% of the time, Pallas kernels for 5%

profile of v7, /device:TPU:6, one launch (start us, length us, event | category | flops | bytes accessed | tf_op | source)
XLA Modules:
  0.0 127.3 jit_solution(17048210878153685733)
XLA Ops:
  1.3 2.5 %shard_map.85 = (bf16[32,144,128]{2,1,0:T(8,128)(2,1)}, bf16[384,128]{1,0:T(8,128)(2,1)}) custom-call(s32[1]{0:T(128)} %bitcast.first, s32[1,4]{1,0:T(1,128)} %rows_at.1, s32[1,4]{1,0:T(1,128)} %columns_at.1, s32[1]{0:T(128)S(6)} %copy.9.count_at.count, bf16[1,4,4096]{2,1,0:T(4,128)(2,1)} %blocks_at.1, bf16[128,384]{1,0:T(8,128)(2,1)} %tokens_at.1), custom_call_target="tpu_custom_call" | custom-call | flops 10000000 | bytes 2097152 | tf_op jit(solution)/shard_map/pallas_call | solution.py:279
  3.8 0.0 copy-start.3
  3.8 9.6 %all-to-all-start = ((bf16[32,144,128]{2,1,0:T(8,128)(2,1)}), bf16[32,144,128]{2,1,0:T(8,128)(2,1)S(1)}, u32[]{:S(2)}, u32[]{:S(2)}) async-start(bf16[32,144,128]{2,1,0:T(8,128)(2,1)} %get-tuple-element.13), calls=%async_computation | async-start | bytes 2359296 | tf_op jit(solution)/shard_map/all_to_all | solution.py:298
  13.4 36.5 %all_gather.3 = bf16[3072,128]{1,0:T(8,128)(2,1)S(1)} all-gather(bf16[384,128]{1,0:T(8,128)(2,1)S(1)} %copy-done.3), channel_id=1, replica_groups=mesh['row'=32,'half'=8,'side'=2] {'half'}, dimensions={0}, use_global_device_ids=true | all-gather | bytes 884736 | tf_op jit(solution)/shard_map/all_gather | solution.py:304
  49.9 0.1 fusion.8
  49.9 3.7 %collective-permute-start = (bf16[1536,128]{1,0:T(8,128)(2,1)S(1)}, bf16[1536,128]{1,0:T(8,128)(2,1)S(1)}, u32[]{:S(2)}, u32[]{:S(2)}) collective-permute-start(bf16[1536,128]{1,0:T(8,128)(2,1)S(1)} %get-tuple-element.24), channel_id=1, source_target_pairs={{0,1},{1,2},{2,3},{3,4},{4,5},{5,6},{6,7},{7,8},{8,9},{9,10},{10,1... | collective-permute-start | bytes 1179656 | tf_op jit(solution)/shard_map/ppermute | solution.py:277
  53.6 3.4 %collective-permute-start.1 = (bf16[1536,128]{1,0:T(8,128)(2,1)S(1)}, bf16[1536,128]{1,0:T(8,128)(2,1)S(1)}, u32[]{:S(2)}, u32[]{:S(2)}) collective-permute-start(bf16[1536,128]{1,0:T(8,128)(2,1)S(1)} %get-tuple-element.23), channel_id=1, source_target_pairs={{0,15},{1,0},{2,1},{3,2},{4,3},{5,4},{6,5},{7,6},{8,7},{9,8},{10,9... | collective-permute-start | bytes 1179656 | tf_op jit(solution)/shard_map/ppermute | solution.py:277
  57.0 0.0 all-to-all-done.weights_at
  57.0 0.1 fusion.4
  57.1 0.1 pad_add_fusion.ids
  57.2 0.8 copy-done.1
  58.0 6.3 %shard_map.86 = (f32[48,64,128]{2,1,0:T(8,128)}, bf16[48,64,128]{2,1,0:T(8,128)(2,1)S(1)}, s32[160]{0:T(256)S(1)}) custom-call(s32[32,12]{1,0:T(8,128)S(1)} %pad_add_fusion.ids, bf16[32,144,128]{2,1,0:T(8,128)(2,1)} %copy-done.1, bf16[48,64,128]{2,1,0:T(8,128)(2,1)S(1)} %bitcast.8, bf16[128,3072]{1,0:T(8,128)(2,1)} %upstream_at.1), custom_call_target="tpu_custom_call" | custom-call | flops 500000000 | bytes 2097152 | tf_op jit(solution)/shard_map/pallas_call | solution.py:309
  64.4 0.9 copy-done
  65.2 0.0 collective-permute-done
  65.2 0.0 collective-permute-done.1
  65.2 10.8 %shard_map.87 = (bf16[128,3072]{1,0:T(8,128)(2,1)}, bf16[6384,128]{1,0:T(8,128)(2,1)}, bf16[32,128,128]{2,1,0:T(8,128)(2,1)}) custom-call(s32[32,12]{1,0:T(8,128)S(1)} %pad_add_fusion.ids, s32[160]{0:T(256)S(1)} %get-tuple-element.15.entries, bf16[32,144,128]{2,1,0:T(8,128)(2,1)} %copy-done.1, bf16[48,64,128]{2,1,0:T(8,128)(2,1)S(1)} %bitcast.9, ...), custom_call_target="tpu_custom_call" | custom-call | flops 1000000000 | bytes 2097152 | tf_op jit(solution)/shard_map/pallas_call | solution.py:334
  76.0 7.9 %all-to-all-start.1 = ((bf16[32,128,128]{2,1,0:T(8,128)(2,1)}), bf16[32,128,128]{2,1,0:T(8,128)(2,1)S(1)}, u32[]{:S(2)}, u32[]{:S(2)}) async-start(bf16[32,128,128]{2,1,0:T(8,128)(2,1)} %get-tuple-element.19), calls=%async_computation.1 | async-start | bytes 2097152 | tf_op jit(solution)/shard_map/all_to_all | solution.py:359
  84.0 38.0 %fusion = bf16[400,128]{1,0:T(8,128)(2,1)S(1)} fusion(bf16[6384,128]{1,0:T(8,128)(2,1)S(1)} %copy-done.2), kind=kCustom, calls=%all-reduce-scatter | all-reduce-scatter fusion | flops 819201 | bytes 1738752
  122.0 1.4 %collective-permute-start.2 = (bf16[15,128]{1,0:T(8,128)(2,1)S(1)}, bf16[15,128]{1,0:T(8,128)(2,1)S(1)}, u32[]{:S(2)}, u32[]{:S(2)}) collective-permute-start(bf16[15,128]{1,0:T(8,128)(2,1)S(1)} %slice.27), channel_id=1, source_target_pairs={{0,1},{1,2},{2,3},{3,4},{4,5},{5,6},{6,7},{7,8},{8,9},{9,10},{10,1... | collective-permute-start | bytes 11528
  123.4 1.3 dynamic-slice.4
  125.3 0.0 collective-permute-done.2
  125.3 0.6 concatenate.4
  126.0 0.0 all-to-all-done.1.terms
  126.1 1.2 shard_map.88
  (9 shorter events, 0.1 us)
Async XLA Ops:
  3.8 9.6 %copy-start.3 = (bf16[384,128]{1,0:T(8,128)(2,1)S(1)}, bf16[384,128]{1,0:T(8,128)(2,1)}, u32[]{:S(2)}) copy-start(bf16[384,128]{1,0:T(8,128)(2,1)} %get-tuple-element.14) | copy-start | bytes 294916
  3.8 53.2 %all-to-all-start = ((bf16[32,144,128]{2,1,0:T(8,128)(2,1)}), bf16[32,144,128]{2,1,0:T(8,128)(2,1)S(1)}, u32[]{:S(2)}, u32[]{:S(2)}) async-start(bf16[32,144,128]{2,1,0:T(8,128)(2,1)} %get-tuple-element.13), calls=%async_computation | async-start | bytes 2359296 | tf_op jit(solution)/shard_map/all_to_all | solution.py:298
  49.9 15.3 %collective-permute-start = (bf16[1536,128]{1,0:T(8,128)(2,1)S(1)}, bf16[1536,128]{1,0:T(8,128)(2,1)S(1)}, u32[]{:S(2)}, u32[]{:S(2)}) collective-permute-start(bf16[1536,128]{1,0:T(8,128)(2,1)S(1)} %get-tuple-element.24), channel_id=1, source_target_pairs={{0,1},{1,2},{2,3},{3,4},{4,5},{5,6},{6,7},{7,8},{8,9},{9,10},{10,1... | collective-permute-start | bytes 1179656 | tf_op jit(solution)/shard_map/ppermute | solution.py:277
  53.6 11.7 %collective-permute-start.1 = (bf16[1536,128]{1,0:T(8,128)(2,1)S(1)}, bf16[1536,128]{1,0:T(8,128)(2,1)S(1)}, u32[]{:S(2)}, u32[]{:S(2)}) collective-permute-start(bf16[1536,128]{1,0:T(8,128)(2,1)S(1)} %get-tuple-element.23), channel_id=1, source_target_pairs={{0,15},{1,0},{2,1},{3,2},{4,3},{5,4},{6,5},{7,6},{8,7},{9,8},{10,9... | collective-permute-start | bytes 1179656 | tf_op jit(solution)/shard_map/ppermute | solution.py:277
  57.0 1.0 copy-start.1
  64.3 0.9 copy-start
  76.0 7.9 %copy-start.2 = (bf16[6384,128]{1,0:T(8,128)(2,1)S(1)}, bf16[6384,128]{1,0:T(8,128)(2,1)}, u32[]{:S(2)}) copy-start(bf16[6384,128]{1,0:T(8,128)(2,1)} %get-tuple-element.20) | copy-start | bytes 4902916
  76.0 50.0 %all-to-all-start.1 = ((bf16[32,128,128]{2,1,0:T(8,128)(2,1)}), bf16[32,128,128]{2,1,0:T(8,128)(2,1)S(1)}, u32[]{:S(2)}, u32[]{:S(2)}) async-start(bf16[32,128,128]{2,1,0:T(8,128)(2,1)} %get-tuple-element.19), calls=%async_computation.1 | async-start | bytes 2097152 | tf_op jit(solution)/shard_map/all_to_all | solution.py:359
  122.0 3.4 %collective-permute-start.2 = (bf16[15,128]{1,0:T(8,128)(2,1)S(1)}, bf16[15,128]{1,0:T(8,128)(2,1)S(1)}, u32[]{:S(2)}, u32[]{:S(2)}) collective-permute-start(bf16[15,128]{1,0:T(8,128)(2,1)S(1)} %slice.27), channel_id=1, source_target_pairs={{0,1},{1,2},{2,3},{3,4},{4,5},{5,6},{6,7},{7,8},{8,9},{9,10},{10,1... | collective-permute-start | bytes 11528

commit v8 on v7

--- a/solution.py
+++ b/solution.py
@@ -326,7 +326,7 @@
             pltpu.SemaphoreType.DMA((2,)),
         ],
         500_000_000,
-        52,
+        8,
         ANY,
         (ANY, ANY, SM),
     )(ids, parcels, same, hidden_grad)
@@ -351,7 +351,7 @@
             pltpu.SemaphoreType.DMA((18,)),
         ],
         1_000_000_000,
-        52,
+        48,
         ANY,
         (ANY, ANY, ANY),
     )(ids, entries, parcels, same, other_low, other_high, early, turned)

time: 128 us -> 128 us (level)
  starting transfers between devices: 26 us -> 27.3 us
    unnamed x12 -> x10, local copies, waits for them, and re-layouts: 3.64 us -> 1.94 us
    unnamed x1, starting transfers between devices: 1.44 us -> 2.84 us
  transfers between devices with their start and end apart: 5 -> 5, of which waited for: 0 -> 1; matrix products, arithmetic and copies ran while one was open for 32% -> 32% of each run, Pallas kernels for 5% -> 5%
where the time goes in v8:
time: 128 us; the launch traced here: 127 us
  blocking collectives  74.9 us (59%)
  starting transfers between devices  27.3 us (21%)
  Pallas kernels  19.7 us (15%)
  local copies, waits for them, and re-layouts  2.92 us (2%)
  between operations  2.12 us (2%)
    unnamed x1, blocking collectives  38 us
    all_gather x1, blocking collectives, on_device(): same = lax.all_gather(turned, 'half', axis=0, tiled=True)  36.9 us
    pallas_call x1, Pallas kernels, on_device(): call(main_kernel, (shape(128, 3072), shape(6384, 128), shape(n_row, 128,...  10.2 us
    all_to_all x1, starting transfers between devices, on_device(): parcels = lax.all_to_all(parcels, 'row', 0, 0, tiled=True)  9.62 us
    all_to_all x1, starting transfers between devices, on_device(): terms = lax.all_to_all(terms, 'row', 0, 0, tiled=True)  7.84 us
    ppermute x2, starting transfers between devices, shift(): return lax.ppermute(a, COL, [(i, (i + by) % n_col) for i in range(n_col)])  7.04 us
    pallas_call x1, Pallas kernels, on_device(): call(early_kernel, (jax.ShapeDtypeStruct((48, BLK, 128), F32), shape(48,...  5.82 us
    unnamed x1, starting transfers between devices  2.84 us
  transfers between devices with their start and end apart: 5, of which 1 were waited for; matrix products, arithmetic and copies ran while one was open for 32% of the time, Pallas kernels for 5%

profile of v8, /device:TPU:6, one launch (start us, length us, event | category | flops | bytes accessed | tf_op | source)
XLA Modules:
  0.0 127.4 jit_solution(1790113980748248492)
XLA Ops:
  1.3 2.4 %shard_map.85 = (bf16[32,144,128]{2,1,0:T(8,128)(2,1)}, bf16[384,128]{1,0:T(8,128)(2,1)}) custom-call(s32[1]{0:T(128)} %bitcast.first, s32[1,4]{1,0:T(1,128)} %rows_at.1, s32[1,4]{1,0:T(1,128)} %columns_at.1, s32[1]{0:T(128)S(6)} %copy.9.count_at.count, bf16[1,4,4096]{2,1,0:T(4,128)(2,1)} %blocks_at.1, bf16[128,384]{1,0:T(8,128)(2,1)} %tokens_at.1), custom_call_target="tpu_custom_call" | custom-call | flops 10000000 | bytes 2097152 | tf_op jit(solution)/shard_map/pallas_call | solution.py:279
  3.7 0.0 copy-start.2
  3.8 9.6 %all-to-all-start = ((bf16[32,144,128]{2,1,0:T(8,128)(2,1)}), bf16[32,144,128]{2,1,0:T(8,128)(2,1)S(1)}, u32[]{:S(2)}, u32[]{:S(2)}) async-start(bf16[32,144,128]{2,1,0:T(8,128)(2,1)} %get-tuple-element.13), calls=%async_computation | async-start | bytes 2359296 | tf_op jit(solution)/shard_map/all_to_all | solution.py:298
  13.4 0.0 copy-start
  13.4 36.9 %all_gather.3 = bf16[3072,128]{1,0:T(8,128)(2,1)S(1)} all-gather(bf16[384,128]{1,0:T(8,128)(2,1)S(1)} %copy-done.2), channel_id=1, replica_groups=mesh['row'=32,'half'=8,'side'=2] {'half'}, dimensions={0}, use_global_device_ids=true | all-gather | bytes 884736 | tf_op jit(solution)/shard_map/all_gather | solution.py:304
  50.3 0.9 fusion.8
  51.2 3.5 %collective-permute-start = (bf16[1536,128]{1,0:T(8,128)(2,1)}, bf16[1536,128]{1,0:T(8,128)(2,1)S(1)}, u32[]{:S(2)}, u32[]{:S(2)}) collective-permute-start(bf16[1536,128]{1,0:T(8,128)(2,1)} %get-tuple-element.24), channel_id=1, source_target_pairs={{0,1},{1,2},{2,3},{3,4},{4,5},{5,6},{6,7},{7,8},{8,9},{9,10},{10,1... | collective-permute-start | bytes 1179656 | tf_op jit(solution)/shard_map/ppermute | solution.py:277
  54.7 3.6 %collective-permute-start.1 = (bf16[1536,128]{1,0:T(8,128)(2,1)}, bf16[1536,128]{1,0:T(8,128)(2,1)S(1)}, u32[]{:S(2)}, u32[]{:S(2)}) collective-permute-start(bf16[1536,128]{1,0:T(8,128)(2,1)} %get-tuple-element.23), channel_id=1, source_target_pairs={{0,15},{1,0},{2,1},{3,2},{4,3},{5,4},{6,5},{7,6},{8,7},{9,8},{10,9... | collective-permute-start | bytes 1179656 | tf_op jit(solution)/shard_map/ppermute | solution.py:277
  58.3 0.0 all-to-all-done.weights_at
  58.3 0.1 fusion.4
  58.4 0.1 pad_add_fusion.ids
  58.5 0.0 copy-done
  58.5 5.8 %shard_map.86 = (f32[48,64,128]{2,1,0:T(8,128)S(1)}, bf16[48,64,128]{2,1,0:T(8,128)(2,1)S(1)}, s32[160]{0:T(256)S(1)}) custom-call(s32[32,12]{1,0:T(8,128)S(1)} %pad_add_fusion.ids, bf16[32,144,128]{2,1,0:T(8,128)(2,1)S(1)} %all-to-all-done.weights_at, bf16[48,64,128]{2,1,0:T(8,128)(2,1)S(1)} %bitcast.8, bf16[128,3072]{1,0:T(8,128)(2,1)S(1)} %copy-done), custom_call_target="tpu_custom_call" | custom-call | flops 500000000 | bytes 2097152 | tf_op jit(solution)/shard_map/pallas_call | solution.py:309
  64.3 0.0 collective-permute-done
  64.3 0.3 collective-permute-done.1
  64.6 10.2 %shard_map.87 = (bf16[128,3072]{1,0:T(8,128)(2,1)}, bf16[6384,128]{1,0:T(8,128)(2,1)}, bf16[32,128,128]{2,1,0:T(8,128)(2,1)}) custom-call(s32[32,12]{1,0:T(8,128)S(1)} %pad_add_fusion.ids, s32[160]{0:T(256)S(1)} %get-tuple-element.15.entries, bf16[32,144,128]{2,1,0:T(8,128)(2,1)S(1)} %all-to-all-done.weights_at, bf16[48,64,128]{2,1,0:T(8,128)(2,1)S(1)} %bitcast.9, ...), custom_call_target="tpu_custom_call" | custom-call | flops 1000000000 | bytes 2097152 | tf_op jit(solution)/shard_map/pallas_call | solution.py:334
  74.9 7.8 %all-to-all-start.1 = ((bf16[32,128,128]{2,1,0:T(8,128)(2,1)}), bf16[32,128,128]{2,1,0:T(8,128)(2,1)S(1)}, u32[]{:S(2)}, u32[]{:S(2)}) async-start(bf16[32,128,128]{2,1,0:T(8,128)(2,1)} %get-tuple-element.19), calls=%async_computation.1 | async-start | bytes 2097152 | tf_op jit(solution)/shard_map/all_to_all | solution.py:359
  82.7 38.0 %fusion = bf16[400,128]{1,0:T(8,128)(2,1)S(1)} fusion(bf16[6384,128]{1,0:T(8,128)(2,1)S(1)} %copy-done.1), kind=kCustom, calls=%all-reduce-scatter | all-reduce-scatter fusion | flops 819201 | bytes 1738752
  120.7 2.8 %collective-permute-start.2 = (bf16[15,128]{1,0:T(8,128)(2,1)S(1)}, bf16[15,128]{1,0:T(8,128)(2,1)S(1)}, u32[]{:S(2)}, u32[]{:S(2)}) collective-permute-start(bf16[15,128]{1,0:T(8,128)(2,1)S(1)} %slice.27), channel_id=1, source_target_pairs={{0,1},{1,2},{2,3},{3,4},{4,5},{5,6},{6,7},{7,8},{8,9},{9,10},{10,1... | collective-permute-start | bytes 11528
  123.6 1.3 dynamic-slice.4
  125.5 0.0 collective-permute-done.2
  125.5 0.6 concatenate.4
  126.2 0.0 all-to-all-done.1.terms
  126.2 1.2 shard_map.88
  (7 shorter events, 0.1 us)
Async XLA Ops:
  3.7 9.7 %copy-start.2 = (bf16[384,128]{1,0:T(8,128)(2,1)S(1)}, bf16[384,128]{1,0:T(8,128)(2,1)}, u32[]{:S(2)}) copy-start(bf16[384,128]{1,0:T(8,128)(2,1)} %get-tuple-element.14) | copy-start | bytes 294916
  3.8 54.5 %all-to-all-start = ((bf16[32,144,128]{2,1,0:T(8,128)(2,1)}), bf16[32,144,128]{2,1,0:T(8,128)(2,1)S(1)}, u32[]{:S(2)}, u32[]{:S(2)}) async-start(bf16[32,144,128]{2,1,0:T(8,128)(2,1)} %get-tuple-element.13), calls=%async_computation | async-start | bytes 2359296 | tf_op jit(solution)/shard_map/all_to_all | solution.py:298
  13.4 45.1 %copy-start = (bf16[128,3072]{1,0:T(8,128)(2,1)S(1)}, bf16[128,3072]{1,0:T(8,128)(2,1)}, u32[]{:S(2)}) copy-start(bf16[128,3072]{1,0:T(8,128)(2,1)} %upstream_at.1) | copy-start | bytes 2359300
  51.2 13.1 %collective-permute-start = (bf16[1536,128]{1,0:T(8,128)(2,1)}, bf16[1536,128]{1,0:T(8,128)(2,1)S(1)}, u32[]{:S(2)}, u32[]{:S(2)}) collective-permute-start(bf16[1536,128]{1,0:T(8,128)(2,1)} %get-tuple-element.24), channel_id=1, source_target_pairs={{0,1},{1,2},{2,3},{3,4},{4,5},{5,6},{6,7},{7,8},{8,9},{9,10},{10,1... | collective-permute-start | bytes 1179656 | tf_op jit(solution)/shard_map/ppermute | solution.py:277
  54.7 9.9 %collective-permute-start.1 = (bf16[1536,128]{1,0:T(8,128)(2,1)}, bf16[1536,128]{1,0:T(8,128)(2,1)S(1)}, u32[]{:S(2)}, u32[]{:S(2)}) collective-permute-start(bf16[1536,128]{1,0:T(8,128)(2,1)} %get-tuple-element.23), channel_id=1, source_target_pairs={{0,15},{1,0},{2,1},{3,2},{4,3},{5,4},{6,5},{7,6},{8,7},{9,8},{10,9... | collective-permute-start | bytes 1179656 | tf_op jit(solution)/shard_map/ppermute | solution.py:277
  74.9 7.9 %copy-start.1 = (bf16[6384,128]{1,0:T(8,128)(2,1)S(1)}, bf16[6384,128]{1,0:T(8,128)(2,1)}, u32[]{:S(2)}) copy-start(bf16[6384,128]{1,0:T(8,128)(2,1)} %get-tuple-element.20) | copy-start | bytes 4902916
  74.9 51.4 %all-to-all-start.1 = ((bf16[32,128,128]{2,1,0:T(8,128)(2,1)}), bf16[32,128,128]{2,1,0:T(8,128)(2,1)S(1)}, u32[]{:S(2)}, u32[]{:S(2)}) async-start(bf16[32,128,128]{2,1,0:T(8,128)(2,1)} %get-tuple-element.19), calls=%async_computation.1 | async-start | bytes 2097152 | tf_op jit(solution)/shard_map/all_to_all | solution.py:359
  120.7 4.8 %collective-permute-start.2 = (bf16[15,128]{1,0:T(8,128)(2,1)S(1)}, bf16[15,128]{1,0:T(8,128)(2,1)S(1)}, u32[]{:S(2)}, u32[]{:S(2)}) collective-permute-start(bf16[15,128]{1,0:T(8,128)(2,1)S(1)} %slice.27), channel_id=1, source_target_pairs={{0,1},{1,2},{2,3},{3,4},{4,5},{5,6},{6,7},{7,8},{8,9},{9,10},{10,1... | collective-permute-start | bytes 11528

commit v9 on v8

--- a/solution.py
+++ b/solution.py
@@ -212,7 +212,7 @@
         hidden[:, pl.ds(at, 128)] = dot(unit, value.astype(BF), NT).astype(BF)
         return carry
 
-    lax.fori_loop(0, 24, some_columns, 0, unroll=4)
+    lax.fori_loop(0, 24, some_columns, 0, unroll=12)
     sent = [pltpu.make_async_copy(hidden, hidden_at, out_sems.at[16])]
     sent[-1].start()
 
@@ -220,14 +220,14 @@
         product = dot(whole[ids[d, j]], grad[ids[d, 4 + j]], NT).astype(BF)
         terms[d, j * 32 : (j + 1) * 32] = jnp.concatenate([product[:32], product[32:]], axis=1)
 
-    slots(weight, 16)
+    slots(weight, 32)
     sent.append(pltpu.make_async_copy(terms, terms_at, out_sems.at[17]))
     sent[-1].start()
 
     def backward(d, j):
         total[ids[d, 8 + j]] += dot(block(d, j), grad[ids[d, 4 + j]])
 
-    slots(backward, 16)
+    slots(backward, 32)
     for o in range(16):
         part[o, :384] = total[6 * o : 6 * o + 6].reshape(384, 128).astype(BF)
         here, size = (part.at[o], 400) if o < 15 else (part.at[o, :384], 384)
@@ -237,11 +237,13 @@
         copy.wait()
 
 
-def end_kernel(count, first, terms, own, weights, inputs, total):
+def end_kernel(first, count_at, terms, own, weights, inputs, count, total, sems):
+    [copy] = fetch(sems, (count_at, count))
     def some(d, kept):
         return kept + terms[d].astype(F32)
 
     kept = lax.fori_loop(1, terms.shape[0], some, terms[0].astype(F32))
+    copy.wait()
     slot = first[0] + lax.broadcasted_iota(jnp.int32, (128, 128), 0) // 32
     total[...] = jnp.where(slot < count[0], kept, 0.0)
     for i in range(32):
@@ -260,7 +262,7 @@
     return pl.pallas_call(
         kernel,
         out_shape=outs,
-        in_specs=[SM] * n_scalar + [place] * n_array,
+        in_specs=[SM] * n_scalar + list(place if isinstance(place, tuple) else [place] * n_array),
         out_specs=leave,
         scratch_shapes=scratch,
         compiler_params=pltpu.CompilerParams(vmem_limit_bytes=limit * MIB),
@@ -362,14 +364,18 @@
     weight_grad, input_grad = call(
         end_kernel,
         (shape(1, 4, 4096), shape(128, 384)),
-        2,
-        2,
-        [pltpu.VMEM((128, 128), F32)],
+        1,
+        3,
+        [
+            pltpu.SMEM((1,), jnp.int32),
+            pltpu.VMEM((128, 128), F32),
+            pltpu.SemaphoreType.DMA((1,)),
+        ],
         10_000_000,
         4,
-        VM,
+        (ANY, VM, VM),
         (VM, VM),
-    )(panel_counts, first, terms, own)
+    )(first, panel_counts, terms, own)
     return hidden, input_grad, weight_grad
 
 

time: 128 us -> 127 us (level)
  transfers between devices with their start and end apart: 5 -> 5, of which waited for: 1 -> 0; matrix products, arithmetic and copies ran while one was open for 32% -> 32% of each run, Pallas kernels for 5% -> 5%
where the time goes in v9:
time: 127 us; the launch traced here: 126 us
  blocking collectives  74.9 us (59%)
  starting transfers between devices  27.1 us (21%)
  Pallas kernels  19.3 us (15%)
  local copies, waits for them, and re-layouts  2.92 us (2%)
  between operations  2.13 us (2%)
    unnamed x1, blocking collectives  38 us
    all_gather x1, blocking collectives, on_device(): same = lax.all_gather(turned, 'half', axis=0, tiled=True)  36.9 us
    all_to_all x1, starting transfers between devices, on_device(): parcels = lax.all_to_all(parcels, 'row', 0, 0, tiled=True)  9.62 us
    pallas_call x1, Pallas kernels, on_device(): call(main_kernel, (shape(128, 3072), shape(6384, 128), shape(n_row, 128,...  9.17 us
    all_to_all x1, starting transfers between devices, on_device(): terms = lax.all_to_all(terms, 'row', 0, 0, tiled=True)  7.69 us
    ppermute x2, starting transfers between devices, shift(): return lax.ppermute(a, COL, [(i, (i + by) % n_col) for i in range(n_col)])  7.04 us
    pallas_call x1, Pallas kernels, on_device(): call(early_kernel, (jax.ShapeDtypeStruct((48, BLK, 128), F32), shape(48,...  6.24 us
    unnamed x1, starting transfers between devices  2.75 us
  transfers between devices with their start and end apart: 5, of which 0 were waited for; matrix products, arithmetic and copies ran while one was open for 32% of the time, Pallas kernels for 5%

profile of v9, /device:TPU:6, one launch (start us, length us, event | category | flops | bytes accessed | tf_op | source)
XLA Modules:
  0.0 126.5 jit_solution(15691225250430870102)
XLA Ops:
  1.3 2.4 %shard_map.85 = (bf16[32,144,128]{2,1,0:T(8,128)(2,1)}, bf16[384,128]{1,0:T(8,128)(2,1)}) custom-call(s32[1]{0:T(128)} %bitcast.first, s32[1,4]{1,0:T(1,128)} %rows_at.1, s32[1,4]{1,0:T(1,128)} %columns_at.1, s32[1]{0:T(128)S(6)} %copy.9.count_at, bf16[1,4,4096]{2,1,0:T(4,128)(2,1)} %blocks_at.1, bf16[128,384]{1,0:T(8,128)(2,1)} %tokens_at.1), custom_call_target="tpu_custom_call" | custom-call | flops 10000000 | bytes 2097152 | tf_op jit(solution)/shard_map/pallas_call | solution.py:281
  3.7 0.0 copy-start.2
  3.8 9.6 %all-to-all-start = ((bf16[32,144,128]{2,1,0:T(8,128)(2,1)}), bf16[32,144,128]{2,1,0:T(8,128)(2,1)S(1)}, u32[]{:S(2)}, u32[]{:S(2)}) async-start(bf16[32,144,128]{2,1,0:T(8,128)(2,1)} %get-tuple-element.13), calls=%async_computation | async-start | bytes 2359296 | tf_op jit(solution)/shard_map/all_to_all | solution.py:300
  13.4 0.0 copy-start
  13.4 36.9 %all_gather.3 = bf16[3072,128]{1,0:T(8,128)(2,1)S(1)} all-gather(bf16[384,128]{1,0:T(8,128)(2,1)S(1)} %copy-done.2), channel_id=1, replica_groups=mesh['row'=32,'half'=8,'side'=2] {'half'}, dimensions={0}, use_global_device_ids=true | all-gather | bytes 884736 | tf_op jit(solution)/shard_map/all_gather | solution.py:306
  50.3 0.9 fusion.8
  51.2 3.5 %collective-permute-start = (bf16[1536,128]{1,0:T(8,128)(2,1)}, bf16[1536,128]{1,0:T(8,128)(2,1)S(1)}, u32[]{:S(2)}, u32[]{:S(2)}) collective-permute-start(bf16[1536,128]{1,0:T(8,128)(2,1)} %get-tuple-element.24), channel_id=1, source_target_pairs={{0,1},{1,2},{2,3},{3,4},{4,5},{5,6},{6,7},{7,8},{8,9},{9,10},{10,1... | collective-permute-start | bytes 1179656 | tf_op jit(solution)/shard_map/ppermute | solution.py:279
  54.7 3.6 %collective-permute-start.1 = (bf16[1536,128]{1,0:T(8,128)(2,1)}, bf16[1536,128]{1,0:T(8,128)(2,1)S(1)}, u32[]{:S(2)}, u32[]{:S(2)}) collective-permute-start(bf16[1536,128]{1,0:T(8,128)(2,1)} %get-tuple-element.23), channel_id=1, source_target_pairs={{0,15},{1,0},{2,1},{3,2},{4,3},{5,4},{6,5},{7,6},{8,7},{9,8},{10,9... | collective-permute-start | bytes 1179656 | tf_op jit(solution)/shard_map/ppermute | solution.py:279
  58.3 0.0 all-to-all-done.weights_at
  58.3 0.1 fusion.4
  58.4 0.1 pad_add_fusion.ids
  58.5 0.0 copy-done
  58.5 6.2 %shard_map.86 = (f32[48,64,128]{2,1,0:T(8,128)S(1)}, bf16[48,64,128]{2,1,0:T(8,128)(2,1)S(1)}, s32[160]{0:T(256)S(1)}) custom-call(s32[32,12]{1,0:T(8,128)S(1)} %pad_add_fusion.ids, bf16[32,144,128]{2,1,0:T(8,128)(2,1)S(1)} %all-to-all-done.weights_at, bf16[48,64,128]{2,1,0:T(8,128)(2,1)S(1)} %bitcast.8, bf16[128,3072]{1,0:T(8,128)(2,1)S(1)} %copy-done), custom_call_target="tpu_custom_call" | custom-call | flops 500000000 | bytes 2097152 | tf_op jit(solution)/shard_map/pallas_call | solution.py:311
  64.7 0.0 collective-permute-done
  64.7 0.0 collective-permute-done.1
  64.8 9.2 %shard_map.87 = (bf16[128,3072]{1,0:T(8,128)(2,1)}, bf16[6384,128]{1,0:T(8,128)(2,1)}, bf16[32,128,128]{2,1,0:T(8,128)(2,1)}) custom-call(s32[32,12]{1,0:T(8,128)S(1)} %pad_add_fusion.ids, s32[160]{0:T(256)S(1)} %get-tuple-element.15.entries, bf16[32,144,128]{2,1,0:T(8,128)(2,1)S(1)} %all-to-all-done.weights_at, bf16[48,64,128]{2,1,0:T(8,128)(2,1)S(1)} %bitcast.9, ...), custom_call_target="tpu_custom_call" | custom-call | flops 1000000000 | bytes 2097152 | tf_op jit(solution)/shard_map/pallas_call | solution.py:336
  73.9 7.7 %all-to-all-start.1 = ((bf16[32,128,128]{2,1,0:T(8,128)(2,1)}), bf16[32,128,128]{2,1,0:T(8,128)(2,1)S(1)}, u32[]{:S(2)}, u32[]{:S(2)}) async-start(bf16[32,128,128]{2,1,0:T(8,128)(2,1)} %get-tuple-element.19), calls=%async_computation.1 | async-start | bytes 2097152 | tf_op jit(solution)/shard_map/all_to_all | solution.py:361
  81.7 38.0 %fusion = bf16[400,128]{1,0:T(8,128)(2,1)S(1)} fusion(bf16[6384,128]{1,0:T(8,128)(2,1)S(1)} %copy-done.1), kind=kCustom, calls=%all-reduce-scatter | all-reduce-scatter fusion | flops 819201 | bytes 1738752
  119.7 2.7 %collective-permute-start.2 = (bf16[15,128]{1,0:T(8,128)(2,1)S(1)}, bf16[15,128]{1,0:T(8,128)(2,1)S(1)}, u32[]{:S(2)}, u32[]{:S(2)}) collective-permute-start(bf16[15,128]{1,0:T(8,128)(2,1)S(1)} %slice.27), channel_id=1, source_target_pairs={{0,1},{1,2},{2,3},{3,4},{4,5},{5,6},{6,7},{7,8},{8,9},{9,10},{10,1... | collective-permute-start | bytes 11528
  122.4 1.3 %dynamic-slice.4 = u32[1]{0:T(128)} dynamic-slice(u32[512]{0:T(512)} %constant.66, u32[]{:S(6)} %partition-id.4), dynamic_slice_sizes={1} | dynamic-slice | bytes 12
  124.3 0.0 collective-permute-done.2
  124.3 0.6 concatenate.4
  125.1 0.0 all-to-all-done.1.terms
  125.1 1.4 %shard_map.88 = (bf16[1,4,4096]{2,1,0:T(4,128)(2,1)}, bf16[128,384]{1,0:T(8,128)(2,1)}) custom-call(s32[1]{0:T(128)} %bitcast.first, s32[1]{0:T(128)S(6)} %copy.9.count_at, bf16[32,128,128]{2,1,0:T(8,128)(2,1)S(1)} %all-to-all-done.1.terms, bf16[384,128]{1,0:T(8,128)(2,1)S(1)} %constant_dynamic-slice_fusion.1.own), custom_call_target="tpu_custom_call" | custom-call | flops 10000000 | bytes 2097152 | tf_op jit(solution)/shard_map/pallas_call | solution.py:364
  (7 shorter events, 0.1 us)
Async XLA Ops:
  3.7 9.7 %copy-start.2 = (bf16[384,128]{1,0:T(8,128)(2,1)S(1)}, bf16[384,128]{1,0:T(8,128)(2,1)}, u32[]{:S(2)}) copy-start(bf16[384,128]{1,0:T(8,128)(2,1)} %get-tuple-element.14) | copy-start | bytes 294916
  3.8 54.5 %all-to-all-start = ((bf16[32,144,128]{2,1,0:T(8,128)(2,1)}), bf16[32,144,128]{2,1,0:T(8,128)(2,1)S(1)}, u32[]{:S(2)}, u32[]{:S(2)}) async-start(bf16[32,144,128]{2,1,0:T(8,128)(2,1)} %get-tuple-element.13), calls=%async_computation | async-start | bytes 2359296 | tf_op jit(solution)/shard_map/all_to_all | solution.py:300
  13.4 45.1 %copy-start = (bf16[128,3072]{1,0:T(8,128)(2,1)S(1)}, bf16[128,3072]{1,0:T(8,128)(2,1)}, u32[]{:S(2)}) copy-start(bf16[128,3072]{1,0:T(8,128)(2,1)} %upstream_at.1) | copy-start | bytes 2359300
  51.2 13.5 %collective-permute-start = (bf16[1536,128]{1,0:T(8,128)(2,1)}, bf16[1536,128]{1,0:T(8,128)(2,1)S(1)}, u32[]{:S(2)}, u32[]{:S(2)}) collective-permute-start(bf16[1536,128]{1,0:T(8,128)(2,1)} %get-tuple-element.24), channel_id=1, source_target_pairs={{0,1},{1,2},{2,3},{3,4},{4,5},{5,6},{6,7},{7,8},{8,9},{9,10},{10,1... | collective-permute-start | bytes 1179656 | tf_op jit(solution)/shard_map/ppermute | solution.py:279
  54.7 10.0 %collective-permute-start.1 = (bf16[1536,128]{1,0:T(8,128)(2,1)}, bf16[1536,128]{1,0:T(8,128)(2,1)S(1)}, u32[]{:S(2)}, u32[]{:S(2)}) collective-permute-start(bf16[1536,128]{1,0:T(8,128)(2,1)} %get-tuple-element.23), channel_id=1, source_target_pairs={{0,15},{1,0},{2,1},{3,2},{4,3},{5,4},{6,5},{7,6},{8,7},{9,8},{10,9... | collective-permute-start | bytes 1179656 | tf_op jit(solution)/shard_map/ppermute | solution.py:279
  73.9 7.7 %copy-start.1 = (bf16[6384,128]{1,0:T(8,128)(2,1)S(1)}, bf16[6384,128]{1,0:T(8,128)(2,1)}, u32[]{:S(2)}) copy-start(bf16[6384,128]{1,0:T(8,128)(2,1)} %get-tuple-element.20) | copy-start | bytes 4902916
  73.9 51.1 %all-to-all-start.1 = ((bf16[32,128,128]{2,1,0:T(8,128)(2,1)}), bf16[32,128,128]{2,1,0:T(8,128)(2,1)S(1)}, u32[]{:S(2)}, u32[]{:S(2)}) async-start(bf16[32,128,128]{2,1,0:T(8,128)(2,1)} %get-tuple-element.19), calls=%async_computation.1 | async-start | bytes 2097152 | tf_op jit(solution)/shard_map/all_to_all | solution.py:361
  119.7 4.7 %collective-permute-start.2 = (bf16[15,128]{1,0:T(8,128)(2,1)S(1)}, bf16[15,128]{1,0:T(8,128)(2,1)S(1)}, u32[]{:S(2)}, u32[]{:S(2)}) collective-permute-start(bf16[15,128]{1,0:T(8,128)(2,1)S(1)} %slice.27), channel_id=1, source_target_pairs={{0,1},{1,2},{2,3},{3,4},{4,5},{5,6},{6,7},{7,8},{8,9},{9,10},{10,1... | collective-permute-start | bytes 11528

commit v10 on v8

--- a/solution.py
+++ b/solution.py
@@ -15,6 +15,7 @@
 NT = (((1,), (1,)), ((), ()))
 TN = (((0,), (0,)), ((), ()))
 COL = ("half", "side")
+ALL = ("row", *COL)
 SM = pl.BlockSpec(memory_space=pltpu.SMEM)
 VM = pl.BlockSpec(memory_space=pltpu.VMEM)
 ANY = pl.BlockSpec(memory_space=pl.ANY)
@@ -276,6 +277,12 @@
     def shift(a, by):
         return lax.ppermute(a, COL, [(i, (i + by) % n_col) for i in range(n_col)])
 
+    def turn(group, row):
+        return group[::-1] if row % 2 else group
+
+    def mirrored(place, size):
+        return jnp.where(me_row % 2 == 1, size - 1 - place, place)
+
     parcels, turned = call(
         prep_kernel,
         (shape(n_row, 144, 128), shape(384, 128)),
@@ -298,10 +305,16 @@
     parcels = lax.all_to_all(parcels, "row", 0, 0, tiled=True)
     ids = parcels[:, 128, :8].astype(jnp.int32)
     owner = ids[:, :4] // 6
-    rows = jnp.where(owner % 2 == me_side, 0, 48) + owner // 2 * 6 + ids[:, :4] % 6
-    ids = jnp.concatenate([rows, ids[:, 4:], ids[:, :4]], axis=1)
-
-    same = lax.all_gather(turned, "half", axis=0, tiled=True)
+    within = ids[:, :4] % 6
+    near = mirrored(owner // 2, n_col // 2)
+    rows = jnp.where(owner % 2 == me_side, 0, 48) + near * 6 + within
+    sums = mirrored(owner, n_col) * 6 + within
+    ids = jnp.concatenate([rows, ids[:, 4:], sums], axis=1)
+
+    sides = [[r * n_col + h * 2 + s for h in range(n_col // 2)] for r in range(n_row) for s in range(2)]
+    same = lax.all_gather(
+        turned, ALL, axis=0, tiled=True, axis_index_groups=[turn(g, i // 2) for i, g in enumerate(sides)]
+    )
     middle = same.shape[0] // 2
     other_low, other_high = shift(same[:middle], 1), shift(same[middle:], -1)
 
@@ -357,8 +370,11 @@
     )(ids, entries, parcels, same, other_low, other_high, early, turned)
 
     terms = lax.all_to_all(terms, "row", 0, 0, tiled=True)
-    own = lax.optimization_barrier(lax.psum_scatter(part, COL, scatter_dimension=0, tiled=True))
-    own = lax.dynamic_slice_in_dim(own, me_col, 384, 0)
+    lines = [turn(list(range(r * n_col, (r + 1) * n_col)), r) for r in range(n_row)]
+    own = lax.optimization_barrier(
+        lax.psum_scatter(part, ALL, scatter_dimension=0, tiled=True, axis_index_groups=lines)
+    )
+    own = lax.dynamic_slice_in_dim(own, mirrored(me_col, n_col), 384, 0)
     weight_grad, input_grad = call(
         end_kernel,
         (shape(1, 4, 4096), shape(128, 384)),

time: 128 us -> 127 us (level)
  transfers between devices with their start and end apart: 5 -> 5, of which waited for: 1 -> 0; matrix products, arithmetic and copies ran while one was open for 32% -> 32% of each run, Pallas kernels for 5% -> 5%
where the time goes in v10:
time: 127 us
  blocking collectives  74.7 us (59%)
  starting transfers between devices  27.1 us (21%)
  Pallas kernels  19.7 us (16%)
  local copies, waits for them, and re-layouts  2.92 us (2%)
  between operations  2.15 us (2%)
    unnamed x1, blocking collectives  38 us
    all_gather x1, blocking collectives, on_device(): lax.all_gather(turned, ALL, axis=0, tiled=True, axis_index_groups=[turn(g...  36.7 us
    pallas_call x1, Pallas kernels, on_device(): call(main_kernel, (shape(128, 3072), shape(6384, 128), shape(n_row, 128,...  9.85 us
    all_to_all x1, starting transfers between devices, on_device(): parcels = lax.all_to_all(parcels, 'row', 0, 0, tiled=True)  9.62 us
    all_to_all x1, starting transfers between devices, on_device(): terms = lax.all_to_all(terms, 'row', 0, 0, tiled=True)  7.79 us
    ppermute x2, starting transfers between devices, shift(): return lax.ppermute(a, COL, [(i, (i + by) % n_col) for i in range(n_col)])  7.04 us
    pallas_call x1, Pallas kernels, on_device(): call(early_kernel, (jax.ShapeDtypeStruct((48, BLK, 128), F32), shape(48,...  6.24 us
    unnamed x1, starting transfers between devices  2.68 us
  transfers between devices with their start and end apart: 5, of which 0 were waited for; matrix products, arithmetic and copies ran while one was open for 32% of the time, Pallas kernels for 5%

profile of v10, /device:TPU:6, one launch (start us, length us, event | category | flops | bytes accessed | tf_op | source)
XLA Modules:
  0.0 126.8 jit_solution(9002263123046891883)
XLA Ops:
  1.3 2.4 %shard_map.85 = (bf16[32,144,128]{2,1,0:T(8,128)(2,1)}, bf16[384,128]{1,0:T(8,128)(2,1)}) custom-call(s32[1]{0:T(128)} %bitcast.first, s32[1,4]{1,0:T(1,128)} %rows_at.1, s32[1,4]{1,0:T(1,128)} %columns_at.1, s32[1]{0:T(128)S(6)} %copy.9.count_at.count, bf16[1,4,4096]{2,1,0:T(4,128)(2,1)} %blocks_at.1, bf16[128,384]{1,0:T(8,128)(2,1)} %tokens_at.1), custom_call_target="tpu_custom_call" | custom-call | flops 10000000 | bytes 2097152 | tf_op jit(solution)/shard_map/pallas_call | solution.py:286
  3.7 0.0 copy-start.2
  3.8 9.6 %all-to-all-start = ((bf16[32,144,128]{2,1,0:T(8,128)(2,1)}), bf16[32,144,128]{2,1,0:T(8,128)(2,1)S(1)}, u32[]{:S(2)}, u32[]{:S(2)}) async-start(bf16[32,144,128]{2,1,0:T(8,128)(2,1)} %get-tuple-element.13), calls=%async_computation | async-start | bytes 2359296 | tf_op jit(solution)/shard_map/all_to_all | solution.py:305
  13.4 0.0 copy-start
  13.4 0.0 copy-done.2
  13.4 36.7 %all_gather.3 = bf16[3072,128]{1,0:T(8,128)(2,1)S(1)} all-gather(bf16[384,128]{1,0:T(8,128)(2,1)S(1)} %copy-done.2), channel_id=1, replica_groups={{0,2,4,6,8,10,12,14},{1,3,5,7,9,11,13,15},{30,28,26,24,22,20,18,16},{31..., dimensions={0}, use_global_device_ids=true | all-gather | bytes 884736 | tf_op jit(solution)/shard_map/all_gather | solution.py:315
  50.1 0.9 fusion.12
  51.1 3.6 %collective-permute-start = (bf16[1536,128]{1,0:T(8,128)(2,1)}, bf16[1536,128]{1,0:T(8,128)(2,1)S(1)}, u32[]{:S(2)}, u32[]{:S(2)}) collective-permute-start(bf16[1536,128]{1,0:T(8,128)(2,1)} %get-tuple-element.26), channel_id=1, source_target_pairs={{0,1},{1,2},{2,3},{3,4},{4,5},{5,6},{6,7},{7,8},{8,9},{9,10},{10,1... | collective-permute-start | bytes 1179656 | tf_op jit(solution)/shard_map/ppermute | solution.py:278
  54.7 3.4 %collective-permute-start.1 = (bf16[1536,128]{1,0:T(8,128)(2,1)}, bf16[1536,128]{1,0:T(8,128)(2,1)S(1)}, u32[]{:S(2)}, u32[]{:S(2)}) collective-permute-start(bf16[1536,128]{1,0:T(8,128)(2,1)} %get-tuple-element.25), channel_id=1, source_target_pairs={{0,15},{1,0},{2,1},{3,2},{4,3},{5,4},{6,5},{7,6},{8,7},{9,8},{10,9... | collective-permute-start | bytes 1179656 | tf_op jit(solution)/shard_map/ppermute | solution.py:278
  58.1 0.0 all-to-all-done.weights_at
  58.2 0.1 fusion.4
  58.3 0.1 pad_add_fusion.ids
  58.4 6.2 %shard_map.86 = (f32[48,64,128]{2,1,0:T(8,128)S(1)}, bf16[48,64,128]{2,1,0:T(8,128)(2,1)S(1)}, s32[160]{0:T(256)S(1)}) custom-call(s32[32,12]{1,0:T(8,128)S(1)} %pad_add_fusion.ids, bf16[32,144,128]{2,1,0:T(8,128)(2,1)S(1)} %all-to-all-done.weights_at, bf16[48,64,128]{2,1,0:T(8,128)(2,1)S(1)} %bitcast.8, bf16[128,3072]{1,0:T(8,128)(2,1)S(1)} %copy-done), custom_call_target="tpu_custom_call" | custom-call | flops 500000000 | bytes 2097152 | tf_op jit(solution)/shard_map/pallas_call | solution.py:322
  64.6 0.0 collective-permute-done
  64.6 0.0 collective-permute-done.1
  64.6 9.8 %shard_map.87 = (bf16[128,3072]{1,0:T(8,128)(2,1)}, bf16[6384,128]{1,0:T(8,128)(2,1)}, bf16[32,128,128]{2,1,0:T(8,128)(2,1)}) custom-call(s32[32,12]{1,0:T(8,128)S(1)} %pad_add_fusion.ids, s32[160]{0:T(256)S(1)} %get-tuple-element.15.entries, bf16[32,144,128]{2,1,0:T(8,128)(2,1)S(1)} %all-to-all-done.weights_at, bf16[48,64,128]{2,1,0:T(8,128)(2,1)S(1)} %bitcast.9, ...), custom_call_target="tpu_custom_call" | custom-call | flops 1000000000 | bytes 2097152 | tf_op jit(solution)/shard_map/pallas_call | solution.py:347
  74.5 7.8 %all-to-all-start.1 = ((bf16[32,128,128]{2,1,0:T(8,128)(2,1)}), bf16[32,128,128]{2,1,0:T(8,128)(2,1)S(1)}, u32[]{:S(2)}, u32[]{:S(2)}) async-start(bf16[32,128,128]{2,1,0:T(8,128)(2,1)} %get-tuple-element.19), calls=%async_computation.1 | async-start | bytes 2097152 | tf_op jit(solution)/shard_map/all_to_all | solution.py:372
  82.3 38.0 %fusion = bf16[400,128]{1,0:T(8,128)(2,1)S(1)} fusion(bf16[6384,128]{1,0:T(8,128)(2,1)S(1)} %copy-done.1), kind=kCustom, calls=%all-reduce-scatter | all-reduce-scatter fusion | flops 819201 | bytes 1738752
  120.3 2.7 %collective-permute-start.2 = (bf16[15,128]{1,0:T(8,128)(2,1)S(1)}, bf16[15,128]{1,0:T(8,128)(2,1)S(1)}, u32[]{:S(2)}, u32[]{:S(2)}) collective-permute-start(bf16[15,128]{1,0:T(8,128)(2,1)S(1)} %slice.26), channel_id=1, source_target_pairs={{0,1},{1,2},{2,3},{3,4},{4,5},{5,6},{6,7},{7,8},{8,9},{9,10},{10,1... | collective-permute-start | bytes 11528
  123.0 1.3 %dynamic-slice.4 = u32[1]{0:T(128)} dynamic-slice(u32[512]{0:T(512)} %constant.82, u32[]{:S(6)} %partition-id.4), dynamic_slice_sizes={1} | dynamic-slice | bytes 12
  124.9 0.0 collective-permute-done.2
  124.9 0.6 concatenate.4
  125.6 0.0 all-to-all-done.1.terms
  125.6 1.2 shard_map.88
  (8 shorter events, 0.1 us)
Async XLA Ops:
  3.7 9.7 %copy-start.2 = (bf16[384,128]{1,0:T(8,128)(2,1)S(1)}, bf16[384,128]{1,0:T(8,128)(2,1)}, u32[]{:S(2)}) copy-start(bf16[384,128]{1,0:T(8,128)(2,1)} %get-tuple-element.14) | copy-start | bytes 294916
  3.8 54.4 %all-to-all-start = ((bf16[32,144,128]{2,1,0:T(8,128)(2,1)}), bf16[32,144,128]{2,1,0:T(8,128)(2,1)S(1)}, u32[]{:S(2)}, u32[]{:S(2)}) async-start(bf16[32,144,128]{2,1,0:T(8,128)(2,1)} %get-tuple-element.13), calls=%async_computation | async-start | bytes 2359296 | tf_op jit(solution)/shard_map/all_to_all | solution.py:305
  13.4 45.0 %copy-start = (bf16[128,3072]{1,0:T(8,128)(2,1)S(1)}, bf16[128,3072]{1,0:T(8,128)(2,1)}, u32[]{:S(2)}) copy-start(bf16[128,3072]{1,0:T(8,128)(2,1)} %upstream_at.1) | copy-start | bytes 2359300
  51.1 13.5 %collective-permute-start = (bf16[1536,128]{1,0:T(8,128)(2,1)}, bf16[1536,128]{1,0:T(8,128)(2,1)S(1)}, u32[]{:S(2)}, u32[]{:S(2)}) collective-permute-start(bf16[1536,128]{1,0:T(8,128)(2,1)} %get-tuple-element.26), channel_id=1, source_target_pairs={{0,1},{1,2},{2,3},{3,4},{4,5},{5,6},{6,7},{7,8},{8,9},{9,10},{10,1... | collective-permute-start | bytes 1179656 | tf_op jit(solution)/shard_map/ppermute | solution.py:278
  54.7 9.9 %collective-permute-start.1 = (bf16[1536,128]{1,0:T(8,128)(2,1)}, bf16[1536,128]{1,0:T(8,128)(2,1)S(1)}, u32[]{:S(2)}, u32[]{:S(2)}) collective-permute-start(bf16[1536,128]{1,0:T(8,128)(2,1)} %get-tuple-element.25), channel_id=1, source_target_pairs={{0,15},{1,0},{2,1},{3,2},{4,3},{5,4},{6,5},{7,6},{8,7},{9,8},{10,9... | collective-permute-start | bytes 1179656 | tf_op jit(solution)/shard_map/ppermute | solution.py:278
  74.5 7.8 %copy-start.1 = (bf16[6384,128]{1,0:T(8,128)(2,1)S(1)}, bf16[6384,128]{1,0:T(8,128)(2,1)}, u32[]{:S(2)}) copy-start(bf16[6384,128]{1,0:T(8,128)(2,1)} %get-tuple-element.20) | copy-start | bytes 4902916
  74.5 51.1 %all-to-all-start.1 = ((bf16[32,128,128]{2,1,0:T(8,128)(2,1)}), bf16[32,128,128]{2,1,0:T(8,128)(2,1)S(1)}, u32[]{:S(2)}, u32[]{:S(2)}) async-start(bf16[32,128,128]{2,1,0:T(8,128)(2,1)} %get-tuple-element.19), calls=%async_computation.1 | async-start | bytes 2097152 | tf_op jit(solution)/shard_map/all_to_all | solution.py:372
  120.3 4.6 %collective-permute-start.2 = (bf16[15,128]{1,0:T(8,128)(2,1)S(1)}, bf16[15,128]{1,0:T(8,128)(2,1)S(1)}, u32[]{:S(2)}, u32[]{:S(2)}) collective-permute-start(bf16[15,128]{1,0:T(8,128)(2,1)S(1)} %slice.26), channel_id=1, source_target_pairs={{0,1},{1,2},{2,3},{3,4},{4,5},{5,6},{6,7},{7,8},{8,9},{9,10},{10,1... | collective-permute-start | bytes 11528

commit v11 on v8

--- a/solution.py
+++ b/solution.py
@@ -212,16 +212,8 @@
         hidden[:, pl.ds(at, 128)] = dot(unit, value.astype(BF), NT).astype(BF)
         return carry
 
-    lax.fori_loop(0, 24, some_columns, 0, unroll=4)
+    lax.fori_loop(0, 24, some_columns, 0, unroll=8)
     sent = [pltpu.make_async_copy(hidden, hidden_at, out_sems.at[16])]
-    sent[-1].start()
-
-    def weight(d, j):
-        product = dot(whole[ids[d, j]], grad[ids[d, 4 + j]], NT).astype(BF)
-        terms[d, j * 32 : (j + 1) * 32] = jnp.concatenate([product[:32], product[32:]], axis=1)
-
-    slots(weight, 16)
-    sent.append(pltpu.make_async_copy(terms, terms_at, out_sems.at[17]))
     sent[-1].start()
 
     def backward(d, j):
@@ -233,6 +225,14 @@
         here, size = (part.at[o], 400) if o < 15 else (part.at[o, :384], 384)
         sent.append(pltpu.make_async_copy(here, part_at.at[400 * o : 400 * o + size], out_sems.at[o]))
         sent[-1].start()
+
+    def weight(d, j):
+        product = dot(whole[ids[d, j]], grad[ids[d, 4 + j]], NT).astype(BF)
+        terms[d, j * 32 : (j + 1) * 32] = jnp.concatenate([product[:32], product[32:]], axis=1)
+
+    slots(weight, 16)
+    sent.append(pltpu.make_async_copy(terms, terms_at, out_sems.at[17]))
+    sent[-1].start()
     for copy in sent:
         copy.wait()
 

time: 128 us -> 127 us (level)
  no operation moved by 1% of the time
where the time goes in v11:
time: 127 us
  blocking collectives  74.9 us (59%)
  starting transfers between devices  27.3 us (21%)
  Pallas kernels  19.3 us (15%)
  local copies, waits for them, and re-layouts  2.92 us (2%)
  between operations  2.12 us (2%)
    unnamed x1, blocking collectives  38 us
    all_gather x1, blocking collectives, on_device(): same = lax.all_gather(turned, 'half', axis=0, tiled=True)  36.9 us
    pallas_call x1, Pallas kernels, on_device(): call(main_kernel, (shape(128, 3072), shape(6384, 128), shape(n_row, 128,...  9.82 us
    all_to_all x1, starting transfers between devices, on_device(): parcels = lax.all_to_all(parcels, 'row', 0, 0, tiled=True)  9.62 us
    all_to_all x1, starting transfers between devices, on_device(): terms = lax.all_to_all(terms, 'row', 0, 0, tiled=True)  7.85 us
    ppermute x2, starting transfers between devices, shift(): return lax.ppermute(a, COL, [(i, (i + by) % n_col) for i in range(n_col)])  7.04 us
    pallas_call x1, Pallas kernels, on_device(): call(early_kernel, (jax.ShapeDtypeStruct((48, BLK, 128), F32), shape(48,...  5.83 us
    unnamed x1, starting transfers between devices  2.79 us
  transfers between devices with their start and end apart: 5, of which 1 were waited for; matrix products, arithmetic and copies ran while one was open for 32% of the time, Pallas kernels for 5%

profile of v11, /device:TPU:6, one launch (start us, length us, event | category | flops | bytes accessed | tf_op | source)
XLA Modules:
  0.0 127.0 jit_solution(3121228120731166533)
XLA Ops:
  1.3 2.4 %shard_map.85 = (bf16[32,144,128]{2,1,0:T(8,128)(2,1)}, bf16[384,128]{1,0:T(8,128)(2,1)}) custom-call(s32[1]{0:T(128)} %bitcast.first, s32[1,4]{1,0:T(1,128)} %rows_at.1, s32[1,4]{1,0:T(1,128)} %columns_at.1, s32[1]{0:T(128)S(6)} %copy.9.count_at.count, bf16[1,4,4096]{2,1,0:T(4,128)(2,1)} %blocks_at.1, bf16[128,384]{1,0:T(8,128)(2,1)} %tokens_at.1), custom_call_target="tpu_custom_call" | custom-call | flops 10000000 | bytes 2097152 | tf_op jit(solution)/shard_map/pallas_call | solution.py:279
  3.7 0.0 copy-start.2
  3.8 9.6 %all-to-all-start = ((bf16[32,144,128]{2,1,0:T(8,128)(2,1)}), bf16[32,144,128]{2,1,0:T(8,128)(2,1)S(1)}, u32[]{:S(2)}, u32[]{:S(2)}) async-start(bf16[32,144,128]{2,1,0:T(8,128)(2,1)} %get-tuple-element.13), calls=%async_computation | async-start | bytes 2359296 | tf_op jit(solution)/shard_map/all_to_all | solution.py:298
  13.4 0.0 copy-start
  13.4 36.9 %all_gather.3 = bf16[3072,128]{1,0:T(8,128)(2,1)S(1)} all-gather(bf16[384,128]{1,0:T(8,128)(2,1)S(1)} %copy-done.2), channel_id=1, replica_groups=mesh['row'=32,'half'=8,'side'=2] {'half'}, dimensions={0}, use_global_device_ids=true | all-gather | bytes 884736 | tf_op jit(solution)/shard_map/all_gather | solution.py:304
  50.3 0.9 fusion.8
  51.2 3.5 %collective-permute-start = (bf16[1536,128]{1,0:T(8,128)(2,1)}, bf16[1536,128]{1,0:T(8,128)(2,1)S(1)}, u32[]{:S(2)}, u32[]{:S(2)}) collective-permute-start(bf16[1536,128]{1,0:T(8,128)(2,1)} %get-tuple-element.24), channel_id=1, source_target_pairs={{0,1},{1,2},{2,3},{3,4},{4,5},{5,6},{6,7},{7,8},{8,9},{9,10},{10,1... | collective-permute-start | bytes 1179656 | tf_op jit(solution)/shard_map/ppermute | solution.py:277
  54.7 3.6 %collective-permute-start.1 = (bf16[1536,128]{1,0:T(8,128)(2,1)}, bf16[1536,128]{1,0:T(8,128)(2,1)S(1)}, u32[]{:S(2)}, u32[]{:S(2)}) collective-permute-start(bf16[1536,128]{1,0:T(8,128)(2,1)} %get-tuple-element.23), channel_id=1, source_target_pairs={{0,15},{1,0},{2,1},{3,2},{4,3},{5,4},{6,5},{7,6},{8,7},{9,8},{10,9... | collective-permute-start | bytes 1179656 | tf_op jit(solution)/shard_map/ppermute | solution.py:277
  58.3 0.0 all-to-all-done.weights_at
  58.3 0.1 fusion.4
  58.4 0.1 pad_add_fusion.ids
  58.5 0.0 copy-done
  58.5 5.8 %shard_map.86 = (f32[48,64,128]{2,1,0:T(8,128)S(1)}, bf16[48,64,128]{2,1,0:T(8,128)(2,1)S(1)}, s32[160]{0:T(256)S(1)}) custom-call(s32[32,12]{1,0:T(8,128)S(1)} %pad_add_fusion.ids, bf16[32,144,128]{2,1,0:T(8,128)(2,1)S(1)} %all-to-all-done.weights_at, bf16[48,64,128]{2,1,0:T(8,128)(2,1)S(1)} %bitcast.8, bf16[128,3072]{1,0:T(8,128)(2,1)S(1)} %copy-done), custom_call_target="tpu_custom_call" | custom-call | flops 500000000 | bytes 2097152 | tf_op jit(solution)/shard_map/pallas_call | solution.py:309
  64.3 0.0 collective-permute-done
  64.3 0.3 collective-permute-done.1
  64.6 9.8 %shard_map.87 = (bf16[128,3072]{1,0:T(8,128)(2,1)}, bf16[6384,128]{1,0:T(8,128)(2,1)}, bf16[32,128,128]{2,1,0:T(8,128)(2,1)}) custom-call(s32[32,12]{1,0:T(8,128)S(1)} %pad_add_fusion.ids, s32[160]{0:T(256)S(1)} %get-tuple-element.15.entries, bf16[32,144,128]{2,1,0:T(8,128)(2,1)S(1)} %all-to-all-done.weights_at, bf16[48,64,128]{2,1,0:T(8,128)(2,1)S(1)} %bitcast.9, ...), custom_call_target="tpu_custom_call" | custom-call | flops 1000000000 | bytes 2097152 | tf_op jit(solution)/shard_map/pallas_call | solution.py:334
  74.4 7.8 %all-to-all-start.1 = ((bf16[32,128,128]{2,1,0:T(8,128)(2,1)}), bf16[32,128,128]{2,1,0:T(8,128)(2,1)S(1)}, u32[]{:S(2)}, u32[]{:S(2)}) async-start(bf16[32,128,128]{2,1,0:T(8,128)(2,1)} %get-tuple-element.19), calls=%async_computation.1 | async-start | bytes 2097152 | tf_op jit(solution)/shard_map/all_to_all | solution.py:359
  82.3 38.0 %fusion = bf16[400,128]{1,0:T(8,128)(2,1)S(1)} fusion(bf16[6384,128]{1,0:T(8,128)(2,1)S(1)} %copy-done.1), kind=kCustom, calls=%all-reduce-scatter | all-reduce-scatter fusion | flops 819201 | bytes 1738752
  120.3 2.8 %collective-permute-start.2 = (bf16[15,128]{1,0:T(8,128)(2,1)S(1)}, bf16[15,128]{1,0:T(8,128)(2,1)S(1)}, u32[]{:S(2)}, u32[]{:S(2)}) collective-permute-start(bf16[15,128]{1,0:T(8,128)(2,1)S(1)} %slice.27), channel_id=1, source_target_pairs={{0,1},{1,2},{2,3},{3,4},{4,5},{5,6},{6,7},{7,8},{8,9},{9,10},{10,1... | collective-permute-start | bytes 11528
  123.1 1.3 dynamic-slice.4
  125.0 0.0 collective-permute-done.2
  125.0 0.6 concatenate.4
  125.7 0.0 all-to-all-done.1.terms
  125.8 1.2 shard_map.88
  (7 shorter events, 0.1 us)
Async XLA Ops:
  3.7 9.7 %copy-start.2 = (bf16[384,128]{1,0:T(8,128)(2,1)S(1)}, bf16[384,128]{1,0:T(8,128)(2,1)}, u32[]{:S(2)}) copy-start(bf16[384,128]{1,0:T(8,128)(2,1)} %get-tuple-element.14) | copy-start | bytes 294916
  3.8 54.5 %all-to-all-start = ((bf16[32,144,128]{2,1,0:T(8,128)(2,1)}), bf16[32,144,128]{2,1,0:T(8,128)(2,1)S(1)}, u32[]{:S(2)}, u32[]{:S(2)}) async-start(bf16[32,144,128]{2,1,0:T(8,128)(2,1)} %get-tuple-element.13), calls=%async_computation | async-start | bytes 2359296 | tf_op jit(solution)/shard_map/all_to_all | solution.py:298
  13.4 45.1 %copy-start = (bf16[128,3072]{1,0:T(8,128)(2,1)S(1)}, bf16[128,3072]{1,0:T(8,128)(2,1)}, u32[]{:S(2)}) copy-start(bf16[128,3072]{1,0:T(8,128)(2,1)} %upstream_at.1) | copy-start | bytes 2359300
  51.2 13.1 %collective-permute-start = (bf16[1536,128]{1,0:T(8,128)(2,1)}, bf16[1536,128]{1,0:T(8,128)(2,1)S(1)}, u32[]{:S(2)}, u32[]{:S(2)}) collective-permute-start(bf16[1536,128]{1,0:T(8,128)(2,1)} %get-tuple-element.24), channel_id=1, source_target_pairs={{0,1},{1,2},{2,3},{3,4},{4,5},{5,6},{6,7},{7,8},{8,9},{9,10},{10,1... | collective-permute-start | bytes 1179656 | tf_op jit(solution)/shard_map/ppermute | solution.py:277
  54.7 9.9 %collective-permute-start.1 = (bf16[1536,128]{1,0:T(8,128)(2,1)}, bf16[1536,128]{1,0:T(8,128)(2,1)S(1)}, u32[]{:S(2)}, u32[]{:S(2)}) collective-permute-start(bf16[1536,128]{1,0:T(8,128)(2,1)} %get-tuple-element.23), channel_id=1, source_target_pairs={{0,15},{1,0},{2,1},{3,2},{4,3},{5,4},{6,5},{7,6},{8,7},{9,8},{10,9... | collective-permute-start | bytes 1179656 | tf_op jit(solution)/shard_map/ppermute | solution.py:277
  74.4 7.9 %copy-start.1 = (bf16[6384,128]{1,0:T(8,128)(2,1)S(1)}, bf16[6384,128]{1,0:T(8,128)(2,1)}, u32[]{:S(2)}) copy-start(bf16[6384,128]{1,0:T(8,128)(2,1)} %get-tuple-element.20) | copy-start | bytes 4902916
  74.4 51.3 %all-to-all-start.1 = ((bf16[32,128,128]{2,1,0:T(8,128)(2,1)}), bf16[32,128,128]{2,1,0:T(8,128)(2,1)S(1)}, u32[]{:S(2)}, u32[]{:S(2)}) async-start(bf16[32,128,128]{2,1,0:T(8,128)(2,1)} %get-tuple-element.19), calls=%async_computation.1 | async-start | bytes 2097152 | tf_op jit(solution)/shard_map/all_to_all | solution.py:359
  120.3 4.7 %collective-permute-start.2 = (bf16[15,128]{1,0:T(8,128)(2,1)S(1)}, bf16[15,128]{1,0:T(8,128)(2,1)S(1)}, u32[]{:S(2)}, u32[]{:S(2)}) collective-permute-start(bf16[15,128]{1,0:T(8,128)(2,1)S(1)} %slice.27), channel_id=1, source_target_pairs={{0,1},{1,2},{2,3},{3,4},{4,5},{5,6},{6,7},{7,8},{8,9},{9,10},{10,1... | collective-permute-start | bytes 11528

commit v12 on v11

--- a/solution.py
+++ b/solution.py
@@ -230,7 +230,7 @@
         product = dot(whole[ids[d, j]], grad[ids[d, 4 + j]], NT).astype(BF)
         terms[d, j * 32 : (j + 1) * 32] = jnp.concatenate([product[:32], product[32:]], axis=1)
 
-    slots(weight, 16)
+    slots(weight, 32)
     sent.append(pltpu.make_async_copy(terms, terms_at, out_sems.at[17]))
     sent[-1].start()
     for copy in sent:
@@ -241,7 +241,7 @@
     def some(d, kept):
         return kept + terms[d].astype(F32)
 
-    kept = lax.fori_loop(1, terms.shape[0], some, terms[0].astype(F32))
+    kept = lax.fori_loop(1, terms.shape[0], some, terms[0].astype(F32), unroll=31)
     slot = first[0] + lax.broadcasted_iota(jnp.int32, (128, 128), 0) // 32
     total[...] = jnp.where(slot < count[0], kept, 0.0)
     for i in range(32):

time: 127 us -> 127 us (level)
  transfers between devices with their start and end apart: 5 -> 5, of which waited for: 1 -> 0; matrix products, arithmetic and copies ran while one was open for 32% -> 33% of each run, Pallas kernels for 5% -> 5%
where the time goes in v12:
time: 127 us; the launch traced here: 126 us
  blocking collectives  74.9 us (59%)
  starting transfers between devices  26.6 us (21%)
  Pallas kernels  19.2 us (15%)
  local copies, waits for them, and re-layouts  2.92 us (2%)
  between operations  2.13 us (2%)
    unnamed x1, blocking collectives  38.1 us
    all_gather x1, blocking collectives, on_device(): same = lax.all_gather(turned, 'half', axis=0, tiled=True)  36.9 us
    all_to_all x1, starting transfers between devices, on_device(): parcels = lax.all_to_all(parcels, 'row', 0, 0, tiled=True)  9.62 us
    pallas_call x1, Pallas kernels, on_device(): call(main_kernel, (shape(128, 3072), shape(6384, 128), shape(n_row, 128,...  9.12 us
    all_to_all x1, starting transfers between devices, on_device(): terms = lax.all_to_all(terms, 'row', 0, 0, tiled=True)  7.33 us
    ppermute x2, starting transfers between devices, shift(): return lax.ppermute(a, COL, [(i, (i + by) % n_col) for i in range(n_col)])  7.04 us
    pallas_call x1, Pallas kernels, on_device(): call(early_kernel, (jax.ShapeDtypeStruct((48, BLK, 128), F32), shape(48,...  6.65 us
    unnamed x1, starting transfers between devices  2.57 us
  transfers between devices with their start and end apart: 5, of which 0 were waited for; matrix products, arithmetic and copies ran while one was open for 33% of the time, Pallas kernels for 5%

profile of v12, /device:TPU:6, one launch (start us, length us, event | category | flops | bytes accessed | tf_op | source)
XLA Modules:
  0.0 126.0 jit_solution(10253595012350569332)
XLA Ops:
  1.3 2.4 %shard_map.85 = (bf16[32,144,128]{2,1,0:T(8,128)(2,1)}, bf16[384,128]{1,0:T(8,128)(2,1)}) custom-call(s32[1]{0:T(128)} %bitcast.first, s32[1,4]{1,0:T(1,128)} %rows_at.1, s32[1,4]{1,0:T(1,128)} %columns_at.1, s32[1]{0:T(128)S(6)} %copy.9.count_at.count, bf16[1,4,4096]{2,1,0:T(4,128)(2,1)} %blocks_at.1, bf16[128,384]{1,0:T(8,128)(2,1)} %tokens_at.1), custom_call_target="tpu_custom_call" | custom-call | flops 10000000 | bytes 2097152 | tf_op jit(solution)/shard_map/pallas_call | solution.py:279
  3.7 0.0 copy-start.2
  3.8 9.6 %all-to-all-start = ((bf16[32,144,128]{2,1,0:T(8,128)(2,1)}), bf16[32,144,128]{2,1,0:T(8,128)(2,1)S(1)}, u32[]{:S(2)}, u32[]{:S(2)}) async-start(bf16[32,144,128]{2,1,0:T(8,128)(2,1)} %get-tuple-element.13), calls=%async_computation | async-start | bytes 2359296 | tf_op jit(solution)/shard_map/all_to_all | solution.py:298
  13.4 0.0 copy-start
  13.4 36.9 %all_gather.3 = bf16[3072,128]{1,0:T(8,128)(2,1)S(1)} all-gather(bf16[384,128]{1,0:T(8,128)(2,1)S(1)} %copy-done.2), channel_id=1, replica_groups=mesh['row'=32,'half'=8,'side'=2] {'half'}, dimensions={0}, use_global_device_ids=true | all-gather | bytes 884736 | tf_op jit(solution)/shard_map/all_gather | solution.py:304
  50.3 0.9 fusion.8
  51.2 3.5 %collective-permute-start = (bf16[1536,128]{1,0:T(8,128)(2,1)}, bf16[1536,128]{1,0:T(8,128)(2,1)S(1)}, u32[]{:S(2)}, u32[]{:S(2)}) collective-permute-start(bf16[1536,128]{1,0:T(8,128)(2,1)} %get-tuple-element.24), channel_id=1, source_target_pairs={{0,1},{1,2},{2,3},{3,4},{4,5},{5,6},{6,7},{7,8},{8,9},{9,10},{10,1... | collective-permute-start | bytes 1179656 | tf_op jit(solution)/shard_map/ppermute | solution.py:277
  54.7 3.6 %collective-permute-start.1 = (bf16[1536,128]{1,0:T(8,128)(2,1)}, bf16[1536,128]{1,0:T(8,128)(2,1)S(1)}, u32[]{:S(2)}, u32[]{:S(2)}) collective-permute-start(bf16[1536,128]{1,0:T(8,128)(2,1)} %get-tuple-element.23), channel_id=1, source_target_pairs={{0,15},{1,0},{2,1},{3,2},{4,3},{5,4},{6,5},{7,6},{8,7},{9,8},{10,9... | collective-permute-start | bytes 1179656 | tf_op jit(solution)/shard_map/ppermute | solution.py:277
  58.3 0.0 all-to-all-done.weights_at
  58.3 0.1 fusion.4
  58.4 0.1 pad_add_fusion.ids
  58.5 6.6 %shard_map.86 = (f32[48,64,128]{2,1,0:T(8,128)S(1)}, bf16[48,64,128]{2,1,0:T(8,128)(2,1)S(1)}, s32[160]{0:T(256)S(1)}) custom-call(s32[32,12]{1,0:T(8,128)S(1)} %pad_add_fusion.ids, bf16[32,144,128]{2,1,0:T(8,128)(2,1)S(1)} %all-to-all-done.weights_at, bf16[48,64,128]{2,1,0:T(8,128)(2,1)S(1)} %bitcast.8, bf16[128,3072]{1,0:T(8,128)(2,1)S(1)} %copy-done), custom_call_target="tpu_custom_call" | custom-call | flops 500000000 | bytes 2097152 | tf_op jit(solution)/shard_map/pallas_call | solution.py:309
  65.1 0.0 collective-permute-done
  65.1 0.0 collective-permute-done.1
  65.2 9.1 %shard_map.87 = (bf16[128,3072]{1,0:T(8,128)(2,1)}, bf16[6384,128]{1,0:T(8,128)(2,1)}, bf16[32,128,128]{2,1,0:T(8,128)(2,1)}) custom-call(s32[32,12]{1,0:T(8,128)S(1)} %pad_add_fusion.ids, s32[160]{0:T(256)S(1)} %get-tuple-element.15.entries, bf16[32,144,128]{2,1,0:T(8,128)(2,1)S(1)} %all-to-all-done.weights_at, bf16[48,64,128]{2,1,0:T(8,128)(2,1)S(1)} %bitcast.9, ...), custom_call_target="tpu_custom_call" | custom-call | flops 1000000000 | bytes 2097152 | tf_op jit(solution)/shard_map/pallas_call | solution.py:334
  74.3 7.3 %all-to-all-start.1 = ((bf16[32,128,128]{2,1,0:T(8,128)(2,1)}), bf16[32,128,128]{2,1,0:T(8,128)(2,1)S(1)}, u32[]{:S(2)}, u32[]{:S(2)}) async-start(bf16[32,128,128]{2,1,0:T(8,128)(2,1)} %get-tuple-element.19), calls=%async_computation.1 | async-start | bytes 2097152 | tf_op jit(solution)/shard_map/all_to_all | solution.py:359
  81.6 0.0 copy-done.1
  81.6 38.1 %fusion = bf16[400,128]{1,0:T(8,128)(2,1)S(1)} fusion(bf16[6384,128]{1,0:T(8,128)(2,1)S(1)} %copy-done.1), kind=kCustom, calls=%all-reduce-scatter | all-reduce-scatter fusion | flops 819201 | bytes 1738752
  119.7 2.6 %collective-permute-start.2 = (bf16[15,128]{1,0:T(8,128)(2,1)S(1)}, bf16[15,128]{1,0:T(8,128)(2,1)S(1)}, u32[]{:S(2)}, u32[]{:S(2)}) collective-permute-start(bf16[15,128]{1,0:T(8,128)(2,1)S(1)} %slice.27), channel_id=1, source_target_pairs={{0,1},{1,2},{2,3},{3,4},{4,5},{5,6},{6,7},{7,8},{8,9},{9,10},{10,1... | collective-permute-start | bytes 11528
  122.3 1.3 %dynamic-slice.4 = u32[1]{0:T(128)} dynamic-slice(u32[512]{0:T(512)} %constant.66, u32[]{:S(6)} %partition-id.4), dynamic_slice_sizes={1} | dynamic-slice | bytes 12
  124.2 0.0 collective-permute-done.2
  124.2 0.6 concatenate.4
  125.0 0.0 all-to-all-done.1.terms
  125.0 1.0 shard_map.88
  (7 shorter events, 0.1 us)
Async XLA Ops:
  3.7 9.7 %copy-start.2 = (bf16[384,128]{1,0:T(8,128)(2,1)S(1)}, bf16[384,128]{1,0:T(8,128)(2,1)}, u32[]{:S(2)}) copy-start(bf16[384,128]{1,0:T(8,128)(2,1)} %get-tuple-element.14) | copy-start | bytes 294916
  3.8 54.5 %all-to-all-start = ((bf16[32,144,128]{2,1,0:T(8,128)(2,1)}), bf16[32,144,128]{2,1,0:T(8,128)(2,1)S(1)}, u32[]{:S(2)}, u32[]{:S(2)}) async-start(bf16[32,144,128]{2,1,0:T(8,128)(2,1)} %get-tuple-element.13), calls=%async_computation | async-start | bytes 2359296 | tf_op jit(solution)/shard_map/all_to_all | solution.py:298
  13.4 45.1 %copy-start = (bf16[128,3072]{1,0:T(8,128)(2,1)S(1)}, bf16[128,3072]{1,0:T(8,128)(2,1)}, u32[]{:S(2)}) copy-start(bf16[128,3072]{1,0:T(8,128)(2,1)} %upstream_at.1) | copy-start | bytes 2359300
  51.2 13.9 %collective-permute-start = (bf16[1536,128]{1,0:T(8,128)(2,1)}, bf16[1536,128]{1,0:T(8,128)(2,1)S(1)}, u32[]{:S(2)}, u32[]{:S(2)}) collective-permute-start(bf16[1536,128]{1,0:T(8,128)(2,1)} %get-tuple-element.24), channel_id=1, source_target_pairs={{0,1},{1,2},{2,3},{3,4},{4,5},{5,6},{6,7},{7,8},{8,9},{9,10},{10,1... | collective-permute-start | bytes 1179656 | tf_op jit(solution)/shard_map/ppermute | solution.py:277
  54.7 10.4 %collective-permute-start.1 = (bf16[1536,128]{1,0:T(8,128)(2,1)}, bf16[1536,128]{1,0:T(8,128)(2,1)S(1)}, u32[]{:S(2)}, u32[]{:S(2)}) collective-permute-start(bf16[1536,128]{1,0:T(8,128)(2,1)} %get-tuple-element.23), channel_id=1, source_target_pairs={{0,15},{1,0},{2,1},{3,2},{4,3},{5,4},{6,5},{7,6},{8,7},{9,8},{10,9... | collective-permute-start | bytes 1179656 | tf_op jit(solution)/shard_map/ppermute | solution.py:277
  74.3 7.4 %copy-start.1 = (bf16[6384,128]{1,0:T(8,128)(2,1)S(1)}, bf16[6384,128]{1,0:T(8,128)(2,1)}, u32[]{:S(2)}) copy-start(bf16[6384,128]{1,0:T(8,128)(2,1)} %get-tuple-element.20) | copy-start | bytes 4902916
  74.3 50.7 %all-to-all-start.1 = ((bf16[32,128,128]{2,1,0:T(8,128)(2,1)}), bf16[32,128,128]{2,1,0:T(8,128)(2,1)S(1)}, u32[]{:S(2)}, u32[]{:S(2)}) async-start(bf16[32,128,128]{2,1,0:T(8,128)(2,1)} %get-tuple-element.19), calls=%async_computation.1 | async-start | bytes 2097152 | tf_op jit(solution)/shard_map/all_to_all | solution.py:359
  119.7 4.5 %collective-permute-start.2 = (bf16[15,128]{1,0:T(8,128)(2,1)S(1)}, bf16[15,128]{1,0:T(8,128)(2,1)S(1)}, u32[]{:S(2)}, u32[]{:S(2)}) collective-permute-start(bf16[15,128]{1,0:T(8,128)(2,1)S(1)} %slice.27), channel_id=1, source_target_pairs={{0,1},{1,2},{2,3},{3,4},{4,5},{5,6},{6,7},{7,8},{8,9},{9,10},{10,1... | collective-permute-start | bytes 11528
